TPU v7x, 32 devices: a whole 2x2x4 slice. The times are simulated.
32 devices in a mesh: seq: 8 (over y, x, core), head: 4 (over z).
Axes of the slice: x: 2, y: 2, z: 4, core: 2. Of those that a mesh axis runs over, the one named last changes fastest.
Arguments:
- inputs: bfloat16 [4, 2048, 1536], P(None, 'seq'), may hold values from -6 to 6
- cotangent: bfloat16 [4, 2048, 1536], P(None, 'seq'), may hold values from -6 to 6
- tail_keys: bfloat16 [4, 1024, 1536], P(None, None, 'head'), may hold values from -6 to 6
- tail_values: bfloat16 [4, 1024, 1536], P(None, None, 'head'), may hold values from -6 to 6
- tail_forget: float32 [4, 1024, 24], P(None, None, 'head'), may hold values from -0.3 to -0.002
- gain_one: bfloat16 [1536], P('seq'), may hold values from 0.5 to 1.5
- gain_two: bfloat16 [1536], P('seq'), may hold values from 0.5 to 1.5
- w_query: bfloat16 [1536, 1536], P('seq', 'head'), may hold values from -0.15625 to 0.15625
- w_key: bfloat16 [1536, 1536], P('seq', 'head'), may hold values from -0.15625 to 0.15625
- w_value: bfloat16 [1536, 1536], P('seq', 'head'), may hold values from -0.15625 to 0.15625
- w_forget: bfloat16 [1536, 24], P('seq', 'head'), may hold values from -0.15625 to 0.15625
- forget_bias: float32 [24], replicated, may hold values from 1 to 8
- query_gain: bfloat16 [64], replicated, may hold values from 0.5 to 1.5
- key_gain: bfloat16 [64], replicated, may hold values from 0.5 to 1.5
- w_outgate: bfloat16 [1536, 1536], P('seq', 'head'), may hold values from -0.15625 to 0.15625
- w_out: bfloat16 [1536, 1536], P('head', 'seq'), may hold values from -0.625 to 0.625
- w_gate: bfloat16 [1536, 4096], P('seq', 'head'), may hold values from -0.15625 to 0.15625
- w_up: bfloat16 [1536, 4096], P('seq', 'head'), may hold values from -0.15625 to 0.15625
- w_down: bfloat16 [4096, 1536], P('head', 'seq'), may hold values from -0.09375 to 0.09375
Outputs:
- layer_out: bfloat16 [4, 2048, 1536], P(None, 'seq')
- input_grad: float32 [4, 2048, 1536], P(None, 'seq')
- grad_gain_one: float32 [1536], P('seq')
- grad_gain_two: float32 [1536], P('seq')
- grad_query: float32 [1536, 1536], P('seq', 'head')
- grad_key: float32 [1536, 1536], P('seq', 'head')
- grad_value: float32 [1536, 1536], P('seq', 'head')
- grad_forget: float32 [1536, 24], P('seq', 'head')
- grad_forget_bias: float32 [24], replicated
- grad_query_gain: float32 [64], replicated
- grad_key_gain: float32 [64], replicated
- grad_outgate: float32 [1536, 1536], P('seq', 'head')
- grad_out: float32 [1536, 1536], P('head', 'seq')
- grad_gate: float32 [1536, 4096], P('seq', 'head')
- grad_up: float32 [1536, 4096], P('seq', 'head')
- grad_down: float32 [4096, 1536], P('head', 'seq')
All inputs are finite; a program needn't handle non-finite values.
Results may differ from a plain program's by a relative error of at most 0.025.
Values may be sent and summed in bfloat16 or wider, within the bound.
No kernel may reach another device: no remote copies, remote signals or barrier semaphores. Data moves between devices by JAX's collectives and lax.ppermute only.
A program may use at most 320 MiB of HBM per device.

v0:
```python
import jax
import jax.numpy as jnp
from jax import lax
from jax.sharding import PartitionSpec as P

HEAD_SIZE = 64


epsilon = 1e-06


def carried_in(x, axis, combine, identity, reverse):
    length, position = (lax.axis_size(axis), lax.axis_index(axis))
    everything = lax.all_gather(x, axis)
    start = jnp.broadcast_to(jnp.asarray(identity, x.dtype), x.shape)

    def hop(k, before):
        at = length - 1 - k if reverse else k
        reached = at > position if reverse else at < position
        new = combine(before, everything[at])
        return jnp.where(reached, new, before)

    return lax.fori_loop(0, length, hop, start)


def rms_factor(values):
    return lax.rsqrt(jnp.mean(values * values, axis=-1, keepdims=True) + epsilon)


def norm_backward(source, factor, gain_row, upstream):
    scaled = upstream * gain_row
    inner_mean = jnp.mean(scaled * source, axis=-1, keepdims=True)
    return (factor * scaled - source * factor**3 * inner_mean, upstream * source * factor)


def add_pair(earlier, later_term):
    return earlier + later_term


def add_rows(target, update, first_row):
    current = lax.dynamic_slice_in_dim(target, first_row, update.shape[0], 0)
    return lax.dynamic_update_slice_in_dim(target, current + update, first_row, 0)


def shards(
    inputs,
    cotangent,
    tail_keys,
    tail_values,
    tail_forget,
    gain_one,
    gain_two,
    w_query,
    w_key,
    w_value,
    w_forget,
    forget_bias,
    query_gain,
    key_gain,
    w_outgate,
    w_out,
    w_gate,
    w_up,
    w_down,
):
    micro_count = inputs.shape[0]
    tokens = inputs.shape[1]
    head_cols = w_query.shape[1]
    heads_here = w_forget.shape[1]
    seq_count = lax.axis_size("seq")
    seq_rank = lax.axis_index("seq")
    head_rank = lax.axis_index("head")
    length = tokens * seq_count
    score_scale = HEAD_SIZE ** (-0.5)
    bias_here = lax.dynamic_slice_in_dim(forget_bias, head_rank * heads_here, heads_here, 0)
    gain_query = query_gain.astype(jnp.float32)
    gain_key = key_gain.astype(jnp.float32)
    query_place = seq_rank * tokens + jnp.arange(tokens, dtype=jnp.int32)
    last_place = seq_rank * tokens + tokens - 1

    def fetch_weights():
        return (
            lax.all_gather(gain_one, "seq", axis=0, tiled=True),
            lax.all_gather(gain_two, "seq", axis=0, tiled=True),
            lax.all_gather(w_query, "seq", axis=0, tiled=True),
            lax.all_gather(w_key, "seq", axis=0, tiled=True),
            lax.all_gather(w_value, "seq", axis=0, tiled=True),
            lax.all_gather(w_forget, "seq", axis=0, tiled=True),
            lax.all_gather(w_outgate, "seq", axis=0, tiled=True),
            lax.all_gather(w_gate, "seq", axis=0, tiled=True),
            lax.all_gather(w_up, "seq", axis=0, tiled=True),
            lax.all_gather(w_out, "seq", axis=1, tiled=True),
            lax.all_gather(w_down, "seq", axis=1, tiled=True),
        )

    def head_total(partial_sum):
        return lax.psum(partial_sum.astype(jnp.bfloat16), "head").astype(jnp.float32)

    def head_grad(partial_sum):
        return lax.psum(partial_sum.astype(jnp.bfloat16), "head").astype(jnp.float32)

    def split_heads(row_block):
        return row_block.reshape(row_block.shape[0], heads_here, HEAD_SIZE)

    def block_rows_of():
        return tokens

    def block_scores(query_heads, query_decay, key_block, key_decay, key_first):
        scores = (
            jnp.einsum(
                "qhd,khd->qhk",
                query_heads,
                split_heads(key_block),
                preferred_element_type=jnp.float32,
            )
            * score_scale
        )
        scores = scores + query_decay[:, :, None] - key_decay.T[None, :, :]
        key_place = key_first + jnp.arange(key_block.shape[0], dtype=jnp.int32)
        visible = key_place[None, :] <= query_place[:, None]
        return jnp.where(visible[:, None, :], scores, -jnp.inf)

    def absorb(fold_state, scores, value_block):
        run_max, run_total, run_acc = fold_state
        new_max = jnp.maximum(run_max, jnp.max(scores, axis=-1))
        rescale = jnp.exp(run_max - new_max)
        exp_scores = jnp.exp(scores - new_max[:, :, None])
        run_total = run_total * rescale + jnp.sum(exp_scores, axis=-1)
        run_acc = run_acc * rescale[:, :, None] + jnp.einsum(
            "qhk,khd->qhd",
            exp_scores.astype(jnp.bfloat16),
            split_heads(value_block),
            preferred_element_type=jnp.float32,
        )
        return (new_max, run_total, run_acc)

    shard_sums = jax.tree.map(
        lambda array_in: jnp.zeros(array_in.shape, jnp.float32),
        (
            gain_one,
            gain_two,
            w_query,
            w_key,
            w_value,
            w_forget,
            w_outgate,
            w_gate,
            w_up,
            w_out,
            w_down,
        ),
    )
    bias_acc = jnp.zeros((heads_here,), jnp.float32)
    query_gain_acc = jnp.zeros((HEAD_SIZE,), jnp.float32)
    key_gain_acc = jnp.zeros((HEAD_SIZE,), jnp.float32)
    outputs = []
    input_grads = []
    for micro_index in range(micro_count):
        weights_now = fetch_weights()
        (
            full_gain_one,
            full_gain_two,
            full_query,
            full_key,
            full_value,
            full_forget,
            full_outgate,
            full_gate,
            full_up,
            full_out,
            full_down,
        ) = weights_now
        layer_in = inputs[micro_index].astype(jnp.float32)
        factor_one = rms_factor(layer_in)
        gain_one_row = full_gain_one.astype(jnp.float32)
        normed_one = (layer_in * factor_one * gain_one_row).astype(jnp.bfloat16)
        query_raw = jnp.dot(normed_one, full_query, preferred_element_type=jnp.float32)
        key_raw = jnp.dot(normed_one, full_key, preferred_element_type=jnp.float32)
        value_rows = jnp.dot(normed_one, full_value, preferred_element_type=jnp.float32).astype(
            jnp.bfloat16
        )
        forget_logit = (
            jnp.dot(normed_one, full_forget, preferred_element_type=jnp.float32) + bias_here
        )
        gate_logit = jnp.dot(normed_one, full_outgate, preferred_element_type=jnp.float32)
        local_cumsum = jnp.cumsum(jax.nn.log_sigmoid(forget_logit), axis=0)
        offset = carried_in(
            local_cumsum[-1], "seq", add_pair, jnp.zeros_like(local_cumsum[-1]), False
        )
        sent_decay = local_cumsum + offset[None, :]
        decay_whole = lax.all_gather(sent_decay, "seq", axis=0, tiled=True)
        decay_own = lax.dynamic_slice_in_dim(decay_whole, seq_rank * tokens, tokens, 0)
        query_shaped = split_heads(query_raw)
        query_factor = rms_factor(query_shaped)
        query_heads = (query_shaped * query_factor * gain_query).astype(jnp.bfloat16)
        key_shaped = split_heads(key_raw)
        key_factor = rms_factor(key_shaped)
        key_rows = (
            (key_shaped * key_factor * gain_key).astype(jnp.bfloat16).reshape(tokens, head_cols)
        )
        tail_key_rows = tail_keys[micro_index]
        tail_value_rows = tail_values[micro_index]
        tail_decay = jnp.cumsum(tail_forget[micro_index], axis=0) - jnp.sum(
            tail_forget[micro_index], axis=0, keepdims=True
        )
        tail_first = -tail_key_rows.shape[0]
        start_state = (
            jnp.full((tokens, heads_here), -jnp.inf, jnp.float32),
            jnp.zeros((tokens, heads_here), jnp.float32),
            jnp.zeros((tokens, heads_here, HEAD_SIZE), jnp.float32),
        )
        start_state = absorb(
            start_state,
            block_scores(query_heads, decay_own, tail_key_rows, tail_decay, tail_first),
            tail_value_rows,
        )
        fold_fold_state = start_state
        key_piece = lax.all_gather(key_rows, "seq", axis=0, tiled=True)
        value_piece = lax.all_gather(value_rows, "seq", axis=0, tiled=True)
        block_rows = block_rows_of()

        def visit_block(carry_state, block_index):
            offset_rows = block_index * block_rows
            key_first = offset_rows

            def live_block(inner_state):
                key_block = lax.dynamic_slice_in_dim(key_piece, offset_rows, block_rows, 0)
                value_block = lax.dynamic_slice_in_dim(value_piece, offset_rows, block_rows, 0)
                key_decay = lax.dynamic_slice_in_dim(decay_whole, key_first, block_rows, 0)
                scores = block_scores(query_heads, decay_own, key_block, key_decay, key_first)
                return absorb(inner_state, scores, value_block)

            return (
                lax.cond(
                    key_first <= last_place,
                    live_block,
                    lambda inner_state: inner_state,
                    carry_state,
                ),
                None,
            )

        fold_fold_state, _ = lax.scan(
            visit_block,
            fold_fold_state,
            jnp.arange(key_piece.shape[0] // block_rows, dtype=jnp.int32),
        )
        run_max, run_total, run_acc = fold_fold_state
        log_total = run_max + jnp.log(run_total)
        attended = run_acc / run_total[:, :, None]
        attended_rows = attended.reshape(tokens, head_cols)
        gate_value = jax.nn.sigmoid(gate_logit)
        gated_rows = (attended_rows * gate_value).astype(jnp.bfloat16)
        hidden = layer_in + head_total(
            jnp.dot(gated_rows, full_out, preferred_element_type=jnp.float32)
        )
        factor_two = rms_factor(hidden)
        gain_two_row = full_gain_two.astype(jnp.float32)
        normed_two = (hidden * factor_two * gain_two_row).astype(jnp.bfloat16)
        gate_raw = jnp.dot(normed_two, full_gate, preferred_element_type=jnp.float32)
        up_raw = jnp.dot(normed_two, full_up, preferred_element_type=jnp.float32)
        silu_gate = jax.nn.silu(gate_raw)
        activated = (silu_gate * up_raw).astype(jnp.bfloat16)
        result = hidden + head_total(
            jnp.dot(activated, full_down, preferred_element_type=jnp.float32)
        )
        outputs.append(result.astype(jnp.bfloat16))
        weights_now = fetch_weights()
        (
            full_gain_one,
            full_gain_two,
            full_query,
            full_key,
            full_value,
            full_forget,
            full_outgate,
            full_gate,
            full_up,
            full_out,
            full_down,
        ) = weights_now
        upstream = cotangent[micro_index]
        grad_down = jnp.einsum("tf,td->fd", activated, upstream, preferred_element_type=jnp.float32)
        act_grad = jnp.einsum("td,fd->tf", upstream, full_down, preferred_element_type=jnp.float32)
        sig_gate = jax.nn.sigmoid(gate_raw)
        gate_grad = (act_grad * up_raw * sig_gate * (1.0 + gate_raw * (1.0 - sig_gate))).astype(
            jnp.bfloat16
        )
        up_grad = (act_grad * silu_gate).astype(jnp.bfloat16)
        grad_gate = jnp.einsum(
            "td,tf->df", normed_two, gate_grad, preferred_element_type=jnp.float32
        )
        grad_up = jnp.einsum("td,tf->df", normed_two, up_grad, preferred_element_type=jnp.float32)
        normed_two_grad = head_grad(
            jnp.einsum("tf,df->td", gate_grad, full_gate, preferred_element_type=jnp.float32)
            + jnp.einsum("tf,df->td", up_grad, full_up, preferred_element_type=jnp.float32)
        )
        hidden_back, gain_two_terms = norm_backward(
            hidden, factor_two, gain_two_row, normed_two_grad
        )
        hidden_grad = upstream.astype(jnp.float32) + hidden_back
        branch_grad = hidden_grad.astype(jnp.bfloat16)
        grad_out = jnp.einsum(
            "tc,td->cd", gated_rows, branch_grad, preferred_element_type=jnp.float32
        )
        gated_grad = jnp.einsum(
            "td,cd->tc", branch_grad, full_out, preferred_element_type=jnp.float32
        )
        att_grad = (gated_grad * gate_value).astype(jnp.bfloat16)
        outgate_grad = (gated_grad * attended_rows * gate_value * (1.0 - gate_value)).astype(
            jnp.bfloat16
        )
        grad_heads = split_heads(att_grad)
        row_delta = jnp.sum(grad_heads.astype(jnp.float32) * attended, axis=-1)

        def backward_block(key_block, value_block, key_decay, key_first):
            scores = block_scores(query_heads, decay_own, key_block, key_decay, key_first)
            exp_scores = jnp.exp(scores - log_total[:, :, None])
            prob_grad = jnp.einsum(
                "qhd,khd->qhk",
                grad_heads,
                split_heads(value_block),
                preferred_element_type=jnp.float32,
            )
            score_grad = (exp_scores * (prob_grad - row_delta[:, :, None])).astype(jnp.bfloat16)
            query_part = (
                jnp.einsum(
                    "qhk,khd->qhd",
                    score_grad,
                    split_heads(key_block),
                    preferred_element_type=jnp.float32,
                )
                * score_scale
            )
            row_part = jnp.sum(score_grad.astype(jnp.float32), axis=-1)
            return (exp_scores, score_grad, query_part, row_part)

        def fold_backward(grad_state, piece_pair):
            key_piece, value_piece = piece_pair
            block_rows = block_rows_of()

            def visit_block(carry_state, block_index):
                offset_rows = block_index * block_rows
                key_first = offset_rows

                def live_block(inner_state):
                    query_acc, row_acc, key_acc, value_acc, decay_acc = inner_state
                    key_block = lax.dynamic_slice_in_dim(key_piece, offset_rows, block_rows, 0)
                    value_block = lax.dynamic_slice_in_dim(value_piece, offset_rows, block_rows, 0)
                    key_decay = lax.dynamic_slice_in_dim(decay_whole, key_first, block_rows, 0)
                    exp_scores, score_grad, query_part, row_part = backward_block(
                        key_block, value_block, key_decay, key_first
                    )
                    key_part = (
                        jnp.einsum(
                            "qhk,qhd->khd",
                            score_grad,
                            query_heads,
                            preferred_element_type=jnp.float32,
                        )
                        * score_scale
                    )
                    value_part = jnp.einsum(
                        "qhk,qhd->khd",
                        exp_scores.astype(jnp.bfloat16),
                        grad_heads,
                        preferred_element_type=jnp.float32,
                    )
                    decay_part = -jnp.sum(score_grad.astype(jnp.float32), axis=0).T
                    return (
                        query_acc + query_part,
                        row_acc + row_part,
                        add_rows(key_acc, key_part.reshape(block_rows, head_cols), key_first),
                        add_rows(value_acc, value_part.reshape(block_rows, head_cols), key_first),
                        add_rows(decay_acc, decay_part, key_first),
                    )

                return (
                    lax.cond(
                        key_first <= last_place,
                        live_block,
                        lambda inner_state: inner_state,
                        carry_state,
                    ),
                    None,
                )

            grad_state, _ = lax.scan(
                visit_block,
                grad_state,
                jnp.arange(key_piece.shape[0] // block_rows, dtype=jnp.int32),
            )
            return grad_state

        tail_parts = backward_block(tail_key_rows, tail_value_rows, tail_decay, tail_first)
        grad_start = (
            tail_parts[2],
            tail_parts[3],
            jnp.zeros((length, head_cols), jnp.float32),
            jnp.zeros((length, head_cols), jnp.float32),
            jnp.zeros((length, heads_here), jnp.float32),
        )
        query_grad_heads, row_grad, key_full, value_full, decay_full = fold_backward(
            grad_start,
            (
                lax.all_gather(key_rows, "seq", axis=0, tiled=True),
                lax.all_gather(value_rows, "seq", axis=0, tiled=True),
            ),
        )
        key_own, value_own, decay_key_own = (
            lax.psum_scatter(key_full, "seq", scatter_dimension=0, tiled=True),
            lax.psum_scatter(value_full, "seq", scatter_dimension=0, tiled=True),
            lax.psum_scatter(decay_full, "seq", scatter_dimension=0, tiled=True),
        )
        decay_grad = row_grad + decay_key_own
        suffix = jnp.cumsum(decay_grad[::-1], axis=0)[::-1]
        later_sum = carried_in(suffix[0], "seq", add_pair, jnp.zeros_like(suffix[0]), True)
        forget_grad = ((suffix + later_sum[None, :]) * jax.nn.sigmoid(-forget_logit)).astype(
            jnp.bfloat16
        )
        query_back, query_gain_terms = norm_backward(
            query_shaped, query_factor, gain_query, query_grad_heads
        )
        query_raw_grad = query_back.reshape(tokens, head_cols).astype(jnp.bfloat16)
        key_back, key_gain_terms = norm_backward(
            key_shaped, key_factor, gain_key, split_heads(key_own)
        )
        key_raw_grad = key_back.reshape(tokens, head_cols).astype(jnp.bfloat16)
        value_raw_grad = value_own.astype(jnp.bfloat16)
        grad_query = jnp.einsum(
            "td,tc->dc", normed_one, query_raw_grad, preferred_element_type=jnp.float32
        )
        grad_key = jnp.einsum(
            "td,tc->dc", normed_one, key_raw_grad, preferred_element_type=jnp.float32
        )
        grad_value = jnp.einsum(
            "td,tc->dc", normed_one, value_raw_grad, preferred_element_type=jnp.float32
        )
        grad_forget = jnp.einsum(
            "td,th->dh", normed_one, forget_grad, preferred_element_type=jnp.float32
        )
        grad_outgate = jnp.einsum(
            "td,tc->dc", normed_one, outgate_grad, preferred_element_type=jnp.float32
        )
        normed_one_grad = head_grad(
            jnp.einsum("tc,dc->td", query_raw_grad, full_query, preferred_element_type=jnp.float32)
            + jnp.einsum("tc,dc->td", key_raw_grad, full_key, preferred_element_type=jnp.float32)
            + jnp.einsum(
                "tc,dc->td", value_raw_grad, full_value, preferred_element_type=jnp.float32
            )
            + jnp.einsum("th,dh->td", forget_grad, full_forget, preferred_element_type=jnp.float32)
            + jnp.einsum(
                "tc,dc->td", outgate_grad, full_outgate, preferred_element_type=jnp.float32
            )
        )
        input_back, gain_one_terms = norm_backward(
            layer_in, factor_one, gain_one_row, normed_one_grad
        )
        input_grads.append(hidden_grad + input_back)
        bias_acc = bias_acc + jnp.sum(forget_grad.astype(jnp.float32), axis=0)
        query_gain_acc = query_gain_acc + jnp.sum(query_gain_terms, axis=(0, 1))
        key_gain_acc = key_gain_acc + jnp.sum(key_gain_terms, axis=(0, 1))
        partial_grads = (
            jnp.sum(gain_one_terms, axis=0),
            jnp.sum(gain_two_terms, axis=0),
            grad_query,
            grad_key,
            grad_value,
            grad_forget,
            grad_outgate,
            grad_gate,
            grad_up,
            grad_out,
            grad_down,
        )
        shard_sums = jax.tree.map(
            jnp.add,
            shard_sums,
            (
                lax.psum_scatter(
                    partial_grads[0].astype(jnp.bfloat16), "seq", scatter_dimension=0, tiled=True
                ).astype(jnp.float32),
                lax.psum_scatter(
                    partial_grads[1].astype(jnp.bfloat16), "seq", scatter_dimension=0, tiled=True
                ).astype(jnp.float32),
                lax.psum_scatter(
                    partial_grads[2].astype(jnp.bfloat16), "seq", scatter_dimension=0, tiled=True
                ).astype(jnp.float32),
                lax.psum_scatter(
                    partial_grads[3].astype(jnp.bfloat16), "seq", scatter_dimension=0, tiled=True
                ).astype(jnp.float32),
                lax.psum_scatter(
                    partial_grads[4].astype(jnp.bfloat16), "seq", scatter_dimension=0, tiled=True
                ).astype(jnp.float32),
                lax.psum_scatter(
                    partial_grads[5].astype(jnp.bfloat16), "seq", scatter_dimension=0, tiled=True
                ).astype(jnp.float32),
                lax.psum_scatter(
                    partial_grads[6].astype(jnp.bfloat16), "seq", scatter_dimension=0, tiled=True
                ).astype(jnp.float32),
                lax.psum_scatter(
                    partial_grads[7].astype(jnp.bfloat16), "seq", scatter_dimension=0, tiled=True
                ).astype(jnp.float32),
                lax.psum_scatter(
                    partial_grads[8].astype(jnp.bfloat16), "seq", scatter_dimension=0, tiled=True
                ).astype(jnp.float32),
                lax.psum_scatter(
                    partial_grads[9].astype(jnp.bfloat16), "seq", scatter_dimension=1, tiled=True
                ).astype(jnp.float32),
                lax.psum_scatter(
                    partial_grads[10].astype(jnp.bfloat16), "seq", scatter_dimension=1, tiled=True
                ).astype(jnp.float32),
            ),
        )
    bias_full = lax.dynamic_update_slice_in_dim(
        jnp.zeros(forget_bias.shape, jnp.float32), bias_acc, head_rank * heads_here, 0
    )
    bias_total, query_gain_total, key_gain_total = lax.psum(
        (bias_full, query_gain_acc, key_gain_acc), ("seq", "head")
    )
    return (
        jnp.stack(outputs),
        jnp.stack(input_grads),
        shard_sums[0],
        shard_sums[1],
        shard_sums[2],
        shard_sums[3],
        shard_sums[4],
        shard_sums[5],
        bias_total,
        query_gain_total,
        key_gain_total,
        shard_sums[6],
        shard_sums[9],
        shard_sums[7],
        shard_sums[8],
        shard_sums[10],
    )


def solution(mesh):
    placed = (
        P(None, "seq", None),
        P(None, "seq", None),
        P(None, None, "head"),
        P(None, None, "head"),
        P(None, None, "head"),
        P("seq"),
        P("seq"),
        P("seq", "head"),
        P("seq", "head"),
        P("seq", "head"),
        P("seq", "head"),
        P(),
        P(),
        P(),
        P("seq", "head"),
        P("head", "seq"),
        P("seq", "head"),
        P("seq", "head"),
        P("head", "seq"),
    )
    return jax.shard_map(
        shards,
        mesh=mesh,
        in_specs=placed,
        out_specs=(
            P(None, "seq", None),
            P(None, "seq", None),
            P("seq"),
            P("seq"),
            P("seq", "head"),
            P("seq", "head"),
            P("seq", "head"),
            P("seq", "head"),
            P(),
            P(),
            P(),
            P("seq", "head"),
            P("head", "seq"),
            P("seq", "head"),
            P("seq", "head"),
            P("head", "seq"),
        ),
        check_vma=False,
    )
```

profile of v0, /device:TPU:0, one launch (start us, length us, event | category | flops | bytes accessed | tf_op | source)
XLA Modules:
  0.0 4051.4 jit_solution(16072981662626414205)
XLA Ops:
  208.1 49.9 %all-reduce.21.cloned.1.call-done = bf16[256,1536]{1,0:T(8,128)(2,1)} async-done(((bf16[256,1536]{1,0:T(8,128)(2,1)}), bf16[256,1536]{1,0:T(8,128)(2,1)}) %all-reduce.21.cloned.1.call-update) | async-done | bytes 786448 | tf_op jit(solution)/shard_map/psum | solution.py:97
  567.2 207.4 %all-reduce.27.cloned.1.call-done = (bf16[256,1536]{1,0:T(8,128)(2,1)}, bf16[256,1536]{1,0:T(8,128)(2,1)}, bf16[256,1536]{1,0:T(8,128)(2,1)}, bf16[256,1536]{1,0:T(8,128)(2,1)}) async-done(((bf16[256,1536]{1,0:T(8,128)(2,1)}, bf16[256,1536]{1,0:T(8,128)(2,1)}, bf16[256,1536]{1,0:T(8,128)(2,1)}, bf16[256,1536]{1,0:T(8,128)(2,1)}), (bf16[256,1536]{1,0:T(8,128)(2,1)}, bf16[256,1536]{1,0:T(8,128)(2,1)}, ...) | async-done | bytes 3145744 | tf_op jit(solution)/shard_map/psum | solution.py:97
  809.9 91.7 %all-reduce.25.cloned.1.call-done = (bf16[256,1536]{1,0:T(8,128)(2,1)}, bf16[256,1536]{1,0:T(8,128)(2,1)}, bf16[256,1536]{1,0:T(8,128)(2,1)}) async-done(((bf16[256,1536]{1,0:T(8,128)(2,1)}, bf16[256,1536]{1,0:T(8,128)(2,1)}, bf16[256,1536]{1,0:T(8,128)(2,1)}), (bf16[256,1536]{1,0:T(8,128)(2,1)}, bf16[256,1536]{1,0:T(8,128)(2,1)}, bf16[256,1536]{1,0:T(8,128)(2,1)})) %all-reduce.25.cloned.1.call-update) | async-done | bytes 2359312 | tf_op jit(solution)/shard_map/psum | solution.py:100
  1183.0 223.0 %reduce-scatter.73.cloned.1.call-done = f32[256,6]{0,1:T(8,128)} async-done(((f32[2048,6]{0,1:T(8,128)}), f32[256,6]{0,1:T(8,128)}) %reduce-scatter.73.cloned.1.call-update) | async-done | bytes 6160 | tf_op jit(solution)/shard_map/reduce_scatter | solution.py:413
  1409.4 413.1 %all-gather.8 = f32[8,1,6]{2,1,0:T(1,128)S(1)} all-gather(f32[1,1,6]{2,1,0:T(1,128)S(1)} %bitcast.1261), channel_id=1, replica_groups=mesh['seq'=8,'head'=4] {'seq'}, dimensions={0}, use_global_device_ids=true | all-gather | bytes 216 | tf_op jit(solution)/shard_map/all_gather | solution.py:14
  1980.6 46.0 %reduce-scatter.75.cloned.1.call-done = f32[256,384]{0,1:T(8,128)} async-done(((f32[2048,384]{0,1:T(8,128)}), f32[256,384]{0,1:T(8,128)}) %reduce-scatter.75.cloned.1.call-update) | async-done | bytes 393232 | tf_op jit(solution)/shard_map/reduce_scatter | solution.py:411
  2184.2 42.2 %reduce-scatter.59.cloned.1.call-done = f32[256,384]{0,1:T(8,128)} async-done(((f32[2048,384]{0,1:T(8,128)}), f32[256,384]{0,1:T(8,128)}) %reduce-scatter.59.cloned.1.call-update) | async-done | bytes 393232 | tf_op jit(solution)/shard_map/reduce_scatter | solution.py:412
  2575.4 40.3 reduce-scatter.109.cloned.1.call-done
  2858.2 47.6 %reduce-scatter.125.cloned.1.call-done = bf16[192,1024]{1,0:T(8,128)(2,1)} async-done(((bf16[1536,1024]{1,0:T(8,128)(2,1)}), bf16[192,1024]{1,0:T(8,128)(2,1)}) %reduce-scatter.125.cloned.1.call-update) | async-done | bytes 393232 | tf_op jit(solution)/shard_map/reduce_scatter | solution.py:501
  2905.7 49.9 %reduce-scatter.127.cloned.1.call-done = bf16[192,1024]{1,0:T(8,128)(2,1)} async-done(((bf16[1536,1024]{1,0:T(8,128)(2,1)}), bf16[192,1024]{1,0:T(8,128)(2,1)}) %reduce-scatter.127.cloned.1.call-update) | async-done | bytes 393232 | tf_op jit(solution)/shard_map/reduce_scatter | solution.py:501
  2955.6 49.6 %reduce-scatter.123.cloned.1.call-done = bf16[192,1024]{1,0:T(8,128)(2,1)} async-done(((bf16[1536,1024]{1,0:T(8,128)(2,1)}), bf16[192,1024]{1,0:T(8,128)(2,1)}) %reduce-scatter.123.cloned.1.call-update) | async-done | bytes 393232 | tf_op jit(solution)/shard_map/reduce_scatter | solution.py:501
  3005.3 49.9 %reduce-scatter.121.cloned.1.call-done = bf16[192,1024]{1,0:T(8,128)(2,1)} async-done(((bf16[1536,1024]{1,0:T(8,128)(2,1)}), bf16[192,1024]{1,0:T(8,128)(2,1)}) %reduce-scatter.121.cloned.1.call-update) | async-done | bytes 393232 | tf_op jit(solution)/shard_map/reduce_scatter | solution.py:501
  3057.7 47.1 %reduce-scatter.133.cloned.1.call-done = bf16[192,1024]{1,0:T(8,128)(2,1)} async-done(((bf16[1536,1024]{1,0:T(8,128)(2,1)}), bf16[192,1024]{1,0:T(8,128)(2,1)}) %reduce-scatter.133.cloned.1.call-update) | async-done | bytes 393232 | tf_op jit(solution)/shard_map/reduce_scatter | solution.py:504
  3104.8 49.9 %reduce-scatter.135.cloned.1.call-done = bf16[192,1024]{1,0:T(8,128)(2,1)} async-done(((bf16[1536,1024]{1,0:T(8,128)(2,1)}), bf16[192,1024]{1,0:T(8,128)(2,1)}) %reduce-scatter.135.cloned.1.call-update) | async-done | bytes 393232 | tf_op jit(solution)/shard_map/reduce_scatter | solution.py:504
  3154.6 49.6 %reduce-scatter.131.cloned.1.call-done = bf16[192,1024]{1,0:T(8,128)(2,1)} async-done(((bf16[1536,1024]{1,0:T(8,128)(2,1)}), bf16[192,1024]{1,0:T(8,128)(2,1)}) %reduce-scatter.131.cloned.1.call-update) | async-done | bytes 393232 | tf_op jit(solution)/shard_map/reduce_scatter | solution.py:504
  3204.3 50.0 %reduce-scatter.129.cloned.1.call-done = bf16[192,1024]{1,0:T(8,128)(2,1)} async-done(((bf16[1536,1024]{1,0:T(8,128)(2,1)}), bf16[192,1024]{1,0:T(8,128)(2,1)}) %reduce-scatter.129.cloned.1.call-update) | async-done | bytes 393232 | tf_op jit(solution)/shard_map/reduce_scatter | solution.py:504
  3256.8 47.1 %reduce-scatter.141.cloned.1.call-done = bf16[1024,192]{0,1:T(8,128)(2,1)} async-done(((bf16[1024,1536]{0,1:T(8,128)(2,1)}), bf16[1024,192]{0,1:T(8,128)(2,1)}) %reduce-scatter.141.cloned.1.call-update) | async-done | bytes 393232 | tf_op jit(solution)/shard_map/reduce_scatter | solution.py:510
  3304.0 50.0 %reduce-scatter.143.cloned.1.call-done = bf16[1024,192]{0,1:T(8,128)(2,1)} async-done(((bf16[1024,1536]{0,1:T(8,128)(2,1)}), bf16[1024,192]{0,1:T(8,128)(2,1)}) %reduce-scatter.143.cloned.1.call-update) | async-done | bytes 393232 | tf_op jit(solution)/shard_map/reduce_scatter | solution.py:510
  3354.0 49.5 %reduce-scatter.139.cloned.1.call-done = bf16[1024,192]{0,1:T(8,128)(2,1)} async-done(((bf16[1024,1536]{0,1:T(8,128)(2,1)}), bf16[1024,192]{0,1:T(8,128)(2,1)}) %reduce-scatter.139.cloned.1.call-update) | async-done | bytes 393232 | tf_op jit(solution)/shard_map/reduce_scatter | solution.py:510
  3403.5 49.9 %reduce-scatter.137.cloned.1.call-done = bf16[1024,192]{0,1:T(8,128)(2,1)} async-done(((bf16[1024,1536]{0,1:T(8,128)(2,1)}), bf16[1024,192]{0,1:T(8,128)(2,1)}) %reduce-scatter.137.cloned.1.call-update) | async-done | bytes 393232 | tf_op jit(solution)/shard_map/reduce_scatter | solution.py:510
  3574.0 40.2 reduce-scatter.89.cloned.1.call-done
  3654.2 40.4 reduce-scatter.101.cloned.1.call-done
  3734.4 40.2 reduce-scatter.97.cloned.1.call-done
  3776.6 226.9 %all-reduce.23.cloned.1.call-done = (bf16[256,1536]{1,0:T(8,128)(2,1)}, bf16[256,1536]{1,0:T(8,128)(2,1)}, bf16[256,1536]{1,0:T(8,128)(2,1)}, bf16[256,1536]{1,0...) async-done(((bf16[256,1536]{1,0:T(8,128)(2,1)}, bf16[256,1536]{1,0:T(8,128)(2,1)}, ...) | async-done | bytes 6291472 | tf_op jit(solution)/shard_map/psum | solution.py:97
  (1559 shorter events, 2311.1 us)
Async XLA Ops:
  1151.0 1025.4 %reduce-scatter.65.cloned.1.call-start = ((), (), s32[]{:S(2)}) async-start(), calls=%async_computation.69 | async-start | bytes 3538944 | tf_op jit(solution)/shard_map/reduce_scatter | solution.py:412
  1151.6 1074.8 %reduce-scatter.59.cloned.1.call-start = ((), (), s32[]{:S(2)}) async-start(), calls=%async_computation.66 | async-start | bytes 3538944 | tf_op jit(solution)/shard_map/reduce_scatter | solution.py:412
  1159.7 1104.3 %reduce-scatter.151.cloned.1.call-start = ((), (), s32[]{:S(2)}) async-start(), calls=%async_computation.112 | async-start | bytes 442368
  1893.6 1012.2 %reduce-scatter.125.cloned.1.call-start = ((), (), s32[]{:S(2)}) async-start(), calls=%async_computation.99 | async-start | bytes 3538944 | tf_op jit(solution)/shard_map/reduce_scatter | solution.py:501
  1897.6 1058.0 %reduce-scatter.127.cloned.1.call-start = ((), (), s32[]{:S(2)}) async-start(), calls=%async_computation.100 | async-start | bytes 3538944 | tf_op jit(solution)/shard_map/reduce_scatter | solution.py:501
  1901.8 1103.5 %reduce-scatter.123.cloned.1.call-start = ((), (), s32[]{:S(2)}) async-start(), calls=%async_computation.98 | async-start | bytes 3538944 | tf_op jit(solution)/shard_map/reduce_scatter | solution.py:501
  1906.0 1149.2 %reduce-scatter.121.cloned.1.call-start = ((), (), s32[]{:S(2)}) async-start(), calls=%async_computation.97 | async-start | bytes 3538944 | tf_op jit(solution)/shard_map/reduce_scatter | solution.py:501
  1910.0 1194.8 %reduce-scatter.133.cloned.1.call-start = ((), (), s32[]{:S(2)}) async-start(), calls=%async_computation.103 | async-start | bytes 3538944 | tf_op jit(solution)/shard_map/reduce_scatter | solution.py:504
  1914.1 1240.5 %reduce-scatter.135.cloned.1.call-start = ((), (), s32[]{:S(2)}) async-start(), calls=%async_computation.104 | async-start | bytes 3538944 | tf_op jit(solution)/shard_map/reduce_scatter | solution.py:504
  1918.1 1286.2 %reduce-scatter.131.cloned.1.call-start = ((), (), s32[]{:S(2)}) async-start(), calls=%async_computation.102 | async-start | bytes 3538944 | tf_op jit(solution)/shard_map/reduce_scatter | solution.py:504
  1922.3 1332.0 %reduce-scatter.129.cloned.1.call-start = ((), (), s32[]{:S(2)}) async-start(), calls=%async_computation.101 | async-start | bytes 3538944 | tf_op jit(solution)/shard_map/reduce_scatter | solution.py:504
  1926.3 1377.6 %reduce-scatter.141.cloned.1.call-start = ((), (), s32[]{:S(2)}) async-start(), calls=%async_computation.107 | async-start | bytes 3538944 | tf_op jit(solution)/shard_map/reduce_scatter | solution.py:510
  1930.4 1423.5 %reduce-scatter.143.cloned.1.call-start = ((), (), s32[]{:S(2)}) async-start(), calls=%async_computation.108 | async-start | bytes 3538944 | tf_op jit(solution)/shard_map/reduce_scatter | solution.py:510
  1934.5 1469.0 %reduce-scatter.139.cloned.1.call-start = ((), (), s32[]{:S(2)}) async-start(), calls=%async_computation.106 | async-start | bytes 3538944 | tf_op jit(solution)/shard_map/reduce_scatter | solution.py:510
  1938.7 1514.7 %reduce-scatter.137.cloned.1.call-start = ((), (), s32[]{:S(2)}) async-start(), calls=%async_computation.105 | async-start | bytes 3538944 | tf_op jit(solution)/shard_map/reduce_scatter | solution.py:510
  1942.8 1552.6 %reduce-scatter.95.cloned.1.call-start = ((), (), s32[]{:S(2)}) async-start(), calls=%async_computation.84 | async-start | bytes 1327104 | tf_op jit(solution)/shard_map/reduce_scatter | solution.py:489
  2032.8 1501.2 %reduce-scatter.93.cloned.1.call-start = ((), (), s32[]{:S(2)}) async-start(), calls=%async_computation.83 | async-start | bytes 1327104 | tf_op jit(solution)/shard_map/reduce_scatter | solution.py:489
  2034.7 1539.3 %reduce-scatter.91.cloned.1.call-start = ((), (), s32[]{:S(2)}) async-start(), calls=%async_computation.82 | async-start | bytes 1327104 | tf_op jit(solution)/shard_map/reduce_scatter | solution.py:489
  2036.5 1577.7 %reduce-scatter.89.cloned.1.call-start = ((), (), s32[]{:S(2)}) async-start(), calls=%async_computation.81 | async-start | bytes 1327104 | tf_op jit(solution)/shard_map/reduce_scatter | solution.py:489
  2039.3 1614.8 %reduce-scatter.103.cloned.1.call-start = ((), (), s32[]{:S(2)}) async-start(), calls=%async_computation.88 | async-start | bytes 1327104 | tf_op jit(solution)/shard_map/reduce_scatter | solution.py:492
  2079.6 1615.0 %reduce-scatter.101.cloned.1.call-start = ((), (), s32[]{:S(2)}) async-start(), calls=%async_computation.87 | async-start | bytes 1327104 | tf_op jit(solution)/shard_map/reduce_scatter | solution.py:492
  2129.7 1604.7 %reduce-scatter.99.cloned.1.call-start = ((), (), s32[]{:S(2)}) async-start(), calls=%async_computation.86 | async-start | bytes 1327104 | tf_op jit(solution)/shard_map/reduce_scatter | solution.py:492
  2179.1 1595.5 %reduce-scatter.97.cloned.1.call-start = ((), (), s32[]{:S(2)}) async-start(), calls=%async_computation.85 | async-start | bytes 1327104 | tf_op jit(solution)/shard_map/reduce_scatter | solution.py:492
  2234.5 1769.0 %all-reduce.23.cloned.1.call-start = ((), (), s32[]{:S(2)}) async-start(), calls=%async_computation.113 | async-start | bytes 12582912 | tf_op jit(solution)/shard_map/psum | solution.py:97
  (324 other events, 29667.0 us)
Sparse Core Ops, SparseCore 0:
  200.1 57.8 all-reduce.20
  567.1 207.4 all-reduce.26
  806.4 95.2 all-reduce.24
  986.4 193.1 reduce-scatter.78
  1182.9 223.0 reduce-scatter.72
  1409.0 207.6 reduce-scatter.60
  1620.0 207.0 reduce-scatter.66
  1830.3 46.2 reduce-scatter.68
  1880.3 46.2 reduce-scatter.62
  1929.9 46.2 reduce-scatter.56
  1980.3 46.2 reduce-scatter.74
  2030.5 46.2 reduce-scatter.76
  2080.6 46.2 reduce-scatter.70
  2130.1 46.2 reduce-scatter.64
  2180.2 46.2 reduce-scatter.58
  2909.4 46.2 reduce-scatter.126
  2959.0 46.2 reduce-scatter.122
  3008.9 46.2 reduce-scatter.120
  3108.4 46.2 reduce-scatter.134
  3158.0 46.2 reduce-scatter.130
  3208.0 46.2 reduce-scatter.128
  3257.7 46.2 reduce-scatter.140
  3357.2 46.2 reduce-scatter.138
  3778.2 225.2 all-reduce.22
  (44 shorter events, 1479.4 us)
where the time goes:
time: 4080 us; the launch traced here: 4050 us
  waiting for transfers between devices  2630 us (64%)
  blocking collectives  598 us (15%)
  matrix products  320 us (8%)
  local copies, waits for them, and re-layouts  272 us (7%)
  other arithmetic  162 us (4%)
  loops' own time  45.7 us (1%)
    psum x3, waiting for transfers between devices, head_total(): lax.psum(partial_sum.astype(jnp.bfloat16), 'head').astype(jnp.float32)  484 us
    all_gather x8, blocking collectives, carried_in(): everything = lax.all_gather(x, axis)  471 us
    reduce_scatter x4, waiting for transfers between devices, shards(): lax.psum_scatter(decay_full, 'seq', scatter_dimension=0, tiled=True)  243 us
    reduce_scatter x4, waiting for transfers between devices, shards(): lax.psum_scatter(partial_grads[7].astype(jnp.bfloat16), 'seq', scatter_di...  197 us
    reduce_scatter x4, waiting for transfers between devices, shards(): lax.psum_scatter(partial_grads[8].astype(jnp.bfloat16), 'seq', scatter_di...  197 us
    reduce_scatter x4, waiting for transfers between devices, shards(): lax.psum_scatter(partial_grads[10].astype(jnp.bfloat16), 'seq', scatter_d...  197 us
    reduce_scatter x4, waiting for transfers between devices, shards(): lax.psum_scatter(partial_grads[2].astype(jnp.bfloat16), 'seq', scatter_di...  159 us
    reduce_scatter x4, waiting for transfers between devices, shards(): lax.psum_scatter(partial_grads[6].astype(jnp.bfloat16), 'seq', scatter_di...  159 us
  transfers between devices with their start and end apart: 68, of which 54 were waited for; matrix products, arithmetic and copies ran while one was open for 14% of the time, Pallas kernels for 0%

commit v1 on v0

v1 whole, which is shorter than its diff:
```python
import functools

import jax
import jax.numpy as jnp
from jax import lax
from jax.experimental import pallas as pl
from jax.experimental.pallas import tpu as pltpu
from jax.sharding import PartitionSpec as P

HEAD_SIZE = 64
LANES = 128
EPSILON = 1e-06
F32 = jnp.float32
BF16 = jnp.bfloat16
NN = (((1,), (0,)), ((), ()))
NT = (((1,), (1,)), ((), ()))
HIDE = -1e30
SCALE = HEAD_SIZE**-0.5
MIB = 1024 * 1024


def dot(left, right, dims=NN):
    return lax.dot_general(left, right, dims, preferred_element_type=F32)


def params(mib=48):
    return pltpu.CompilerParams(vmem_limit_bytes=mib * MIB)


def lanes_of(rows):
    return lax.broadcasted_iota(jnp.int32, (rows, LANES), 1)


def swap_halves(block):
    return pltpu.roll(block, HEAD_SIZE, 1)


def in_three(value):
    high = value.astype(BF16).astype(F32)
    rest = value - high
    middle = rest.astype(BF16).astype(F32)
    return high, middle, rest - middle


def at_lanes(lane, first, parts, base):
    for place, part in enumerate(parts):
        base = jnp.where(lane == first + place, part, base)
    return base


def triangle(rows, lower):
    down = lax.broadcasted_iota(jnp.int32, (rows, rows), 0)
    across = lax.broadcasted_iota(jnp.int32, (rows, rows), 1)
    return jnp.where(down >= across if lower else down <= across, 1.0, 0.0).astype(BF16)


def running_sum(tri, column, lane):
    spread = at_lanes(lane, 0, in_three(column), jnp.zeros(lane.shape, F32))
    sums = dot(tri, spread.astype(BF16))
    return sums[:, 0:1] + sums[:, 1:2] + sums[:, 2:3]


def forget_column(tail_block):
    return tail_block[:, 64:65] + tail_block[:, 65:66] + tail_block[:, 66:67]


def per_head(low, values):
    first = jnp.sum(jnp.where(low, values, 0.0), axis=-1, keepdims=True)
    second = jnp.sum(jnp.where(low, 0.0, values), axis=-1, keepdims=True)
    return jnp.where(low, first, second) * (1.0 / HEAD_SIZE)


def rms_factor(values):
    return lax.rsqrt(jnp.mean(values * values, axis=-1, keepdims=True) + EPSILON)


def merge_pair(low, first, second):
    return jnp.where(low, first, swap_halves(second))


def merge_swapped(low, first, second):
    return jnp.where(low, swap_halves(first), second)


def unpack_rows(low_half, first, second):
    top = jnp.where(low_half, first, swap_halves(second))
    bottom = jnp.where(low_half, swap_halves(first), second)
    return jnp.concatenate([top, bottom], axis=0)


def pack_rows(low_half, block):
    half = block.shape[0] // 2
    top, bottom = block[:half], block[half:]
    first = jnp.where(low_half, top, swap_halves(bottom))
    second = jnp.where(low_half, swap_halves(top), bottom)
    return first, second


def project_kernel(
    heads, x_ref, w_ref, bias_ref, gain_ref, gq_ref, gk_ref, a_ref, raw_ref, gl_ref, pay_ref
):
    x = x_ref[...].astype(F32)
    rows = x.shape[0]
    cols = gl_ref.shape[1]
    a = (x * rms_factor(x) * gain_ref[...]).astype(BF16)
    a_ref[...] = a
    proj = dot(a, w_ref[...])
    raw_ref[...] = proj[:, : 2 * cols]
    gl_ref[...] = proj[:, 3 * cols : 4 * cols]
    logit = proj[:, 4 * cols :] + bias_ref[...]
    lane = lanes_of(rows)
    low = lane < HEAD_SIZE
    for group in range(cols // LANES):
        at = group * LANES
        query = proj[:, at : at + LANES]
        key = proj[:, cols + at : cols + at + LANES]
        value = proj[:, 2 * cols + at : 2 * cols + at + LANES]
        query = query * lax.rsqrt(per_head(low, query * query) + EPSILON) * gq_ref[...]
        key = key * lax.rsqrt(per_head(low, key * key) + EPSILON) * gk_ref[...]
        for half in range(2):
            head = 2 * group + half
            if head >= heads:
                continue
            zl = at_lanes(lane, 64, in_three(logit[:, head : head + 1]), jnp.zeros(lane.shape, F32))
            if half == 0:
                both = merge_pair(low, query, key)
                rest = jnp.where(low, value, zl)
            else:
                both = merge_swapped(low, query, key)
                rest = jnp.where(low, swap_halves(value), zl)
            pay_ref[head, :, :LANES] = both.astype(BF16)
            pay_ref[head, :, LANES:] = rest.astype(BF16)


def project(heads, cols, x, weights, bias_row, gain_row, gq_row, gk_row, micros):
    total, width = x.shape
    rows = total // micros
    wide = weights.shape[1]
    whole = lambda m: (0, 0)
    part = lambda m: (m, 0)
    return pl.pallas_call(
        functools.partial(project_kernel, heads),
        grid=(micros,),
        in_specs=[
            pl.BlockSpec((rows, width), part),
            pl.BlockSpec((width, wide), whole),
            pl.BlockSpec((1, LANES), whole),
            pl.BlockSpec((1, width), whole),
            pl.BlockSpec((1, LANES), whole),
            pl.BlockSpec((1, LANES), whole),
        ],
        out_specs=[
            pl.BlockSpec((rows, width), part),
            pl.BlockSpec((rows, 2 * cols), part),
            pl.BlockSpec((rows, cols), part),
            pl.BlockSpec((heads, rows, 2 * LANES), lambda m: (m, 0, 0)),
        ],
        out_shape=[
            jax.ShapeDtypeStruct((total, width), BF16),
            jax.ShapeDtypeStruct((total, 2 * cols), F32),
            jax.ShapeDtypeStruct((total, cols), F32),
            jax.ShapeDtypeStruct((micros * heads, rows, 2 * LANES), BF16),
        ],
        compiler_params=params(),
        cost_estimate=pl.CostEstimate(
            flops=2 * total * width * wide,
            bytes_accessed=2 * width * wide + 10 * total * width,
            transcendentals=0,
        ),
        name="project",
    )(x, weights, bias_row, gain_row, gq_row, gk_row)


def attend_kernel(size, pay_ref, tk_ref, tv_ref, ap_ref, af_ref, q_ref, k_ref, v_ref):
    blocks, _, rows, _ = pay_ref.shape
    length = blocks * rows
    lane = lanes_of(rows)
    low = lane < HEAD_SIZE
    tri = triangle(rows, True)
    zero = jnp.zeros(lane.shape, F32)

    def build(b, carry):
        at = pl.ds(pl.multiple_of(b * rows, rows), rows)
        both = pay_ref[b, 0, :, :LANES].astype(F32)
        rest = pay_ref[b, 0, :, LANES:].astype(F32)
        logit = forget_column(rest)
        log_forget = jnp.minimum(logit, 0.0) - jnp.log1p(jnp.exp(-jnp.abs(logit)))
        decay = running_sum(tri, log_forget, lane) + carry
        high, middle, least = in_three(decay)
        query_side = at_lanes(lane, 64, (high, middle, least, 1.0, 1.0, 1.0), zero)
        key_side = at_lanes(lane, 64, (1.0, 1.0, 1.0, -high, -middle, -least), zero)
        value_side = at_lanes(lane, 64, (1.0, 1.0, 1.0), zero)
        q_ref[0, at, :] = jnp.where(low, both * SCALE, query_side).astype(BF16)
        k_ref[0, at, :] = jnp.where(low, swap_halves(both), key_side).astype(BF16)
        v_ref[0, at, :] = jnp.where(low, rest, value_side).astype(BF16)
        return decay[rows - 1 :, :]

    lax.fori_loop(0, blocks, build, jnp.zeros((1, 1), F32))

    tail_length = tk_ref.shape[1]
    visible = lax.broadcasted_iota(jnp.int32, (size, size), 0) >= lax.broadcasted_iota(
        jnp.int32, (size, size), 1
    )
    half_low = lanes_of(rows // 2) < HEAD_SIZE
    lane_here = lanes_of(size)

    def one_block(qi, carry):
        at = pl.ds(pl.multiple_of(qi * size, size), size)
        query = q_ref[0, at, :]

        def absorb(key, value, total, masked=False):
            scores = dot(query, key, NT)
            if masked:
                scores = jnp.where(visible, scores, HIDE)
            return total + dot(jnp.exp(scores).astype(BF16), value)

        total = jnp.zeros((size, LANES), F32)
        for t in range(tail_length // size):
            here = pl.ds(t * size, size)
            total = absorb(tk_ref[0, here, :], tv_ref[0, here, :], total)

        def earlier(ki, total):
            here = pl.ds(pl.multiple_of(ki * size, size), size)
            return absorb(k_ref[0, here, :], v_ref[0, here, :], total)

        total = lax.fori_loop(0, qi, earlier, total)
        total = absorb(k_ref[0, at, :], v_ref[0, at, :], total, True)
        weight = total[:, 64:65]
        mixture = total / weight
        af_ref[0, at, :] = mixture
        for piece in range(size // rows):
            block = mixture[piece * rows : (piece + 1) * rows]
            packed = jnp.where(
                half_low, block[: rows // 2], swap_halves(block[rows // 2 :])
            )
            ap_ref[qi * (size // rows) + piece, 0] = packed.astype(BF16)
        old = query.astype(F32)
        shifted = forget_column(old) - jnp.log(weight)
        q_ref[0, at, :] = at_lanes(lane_here, 64, in_three(shifted), old).astype(BF16)
        return carry

    lax.fori_loop(0, length // size, one_block, 0)


def attend(pay, tail_key, tail_value):
    blocks, pairs, rows, _ = pay.shape
    length = blocks * rows
    tail_length = tail_key.shape[1]
    size = min(512, length)
    pair = lambda j: (j, 0, 0)
    across = lambda j: (0, j, 0, 0)
    entries = length * (tail_length + length // 2) * pairs
    return pl.pallas_call(
        functools.partial(attend_kernel, size),
        grid=(pairs,),
        in_specs=[
            pl.BlockSpec((blocks, 1, rows, 2 * LANES), across),
            pl.BlockSpec((1, tail_length, LANES), pair),
            pl.BlockSpec((1, tail_length, LANES), pair),
        ],
        out_specs=[
            pl.BlockSpec((blocks, 1, rows // 2, LANES), across),
            pl.BlockSpec((1, length, LANES), pair),
            pl.BlockSpec((1, length, LANES), pair),
            pl.BlockSpec((1, length, LANES), pair),
            pl.BlockSpec((1, length, LANES), pair),
        ],
        out_shape=[
            jax.ShapeDtypeStruct((blocks, pairs, rows // 2, LANES), BF16),
            jax.ShapeDtypeStruct((pairs, length, LANES), F32),
            jax.ShapeDtypeStruct((pairs, length, LANES), BF16),
            jax.ShapeDtypeStruct((pairs, length, LANES), BF16),
            jax.ShapeDtypeStruct((pairs, length, LANES), BF16),
        ],
        compiler_params=params(),
        cost_estimate=pl.CostEstimate(
            flops=16 * LANES * entries, bytes_accessed=8 * pairs * length * LANES, transcendentals=entries
        ),
        name="attend",
    )(pay, tail_key, tail_value)


def attend_back_kernel(
    size,
    q_ref,
    k_ref,
    v_ref,
    tk_ref,
    tv_ref,
    af_ref,
    dap_ref,
    rest_ref,
    g_ref,
    da_ref,
    dqt_ref,
    sums_ref,
):
    blocks, _, rows, _ = rest_ref.shape
    length = blocks * rows
    lane = lanes_of(rows)
    low = lane < HEAD_SIZE
    zero = jnp.zeros(lane.shape, F32)

    def build(b, carry):
        at = pl.ds(pl.multiple_of(b * rows, rows), rows)
        packed = dap_ref[b, 0].astype(F32)
        grad = jnp.concatenate([packed, swap_halves(packed)], axis=0)
        grad = jnp.where(low, grad, 0.0)
        delta = jnp.sum(grad * af_ref[0, at, :], axis=-1, keepdims=True)
        da_ref[at, :] = at_lanes(lane, 64, in_three(-delta), grad).astype(BF16)
        return carry

    lax.fori_loop(0, blocks, build, 0)

    across = lax.broadcasted_iota(jnp.int32, (size, size), 1)
    down = lax.broadcasted_iota(jnp.int32, (size, size), 0)
    visible = across >= down
    count = length // size

    def block_at(i):
        return pl.ds(pl.multiple_of(i * size, size), size)

    def pieces(key, value, at, masked=False):
        scores = dot(key, q_ref[0, at, :], NT)
        if masked:
            scores = jnp.where(visible, scores, HIDE)
        prob = jnp.exp(scores)
        score_grad = prob * dot(value, da_ref[at, :], NT)
        return prob.astype(BF16), score_grad.astype(BF16)

    tail_length = tk_ref.shape[1]
    tail_count = tail_length // size

    def tail_block(qi, carry):
        at = block_at(qi)
        total = jnp.zeros((LANES, size), F32)
        for t in range(tail_count):
            key = tk_ref[0, pl.ds(t * size, size), :]
            _, score_grad = pieces(key, tv_ref[0, pl.ds(t * size, size), :], at)
            total = total + dot(key.T, score_grad)
        dqt_ref[:, at] = total
        return carry

    lax.fori_loop(0, count, tail_block, 0)
    lane_here = lanes_of(size)
    low_here = lane_here < HEAD_SIZE

    def key_block(ki, carry):
        own = block_at(ki)
        key = k_ref[0, own, :]
        value = v_ref[0, own, :]
        key_turned = key.T

        def one(at, sums, masked=False):
            key_sum, value_sum = sums
            prob, score_grad = pieces(key, value, at, masked)
            dqt_ref[:, at] += dot(key_turned, score_grad)
            return (
                key_sum + dot(score_grad, q_ref[0, at, :]),
                value_sum + dot(prob, da_ref[at, :]),
            )

        start = (jnp.zeros((size, LANES), F32), jnp.zeros((size, LANES), F32))
        sums = one(own, start, True)
        key_sum, value_sum = lax.fori_loop(
            ki + 1, count, lambda qi, sums: one(block_at(qi), sums), sums
        )
        sums_ref[own, :] = key_sum
        for piece in range(size // rows):
            here = slice(piece * rows, (piece + 1) * rows)
            g_ref[ki * (size // rows) + piece, 0, :, LANES:] = value_sum[here].astype(BF16)
        return carry

    lax.fori_loop(0, count, key_block, 0)

    tri = triangle(rows, False)

    def finish(i, carry):
        b = blocks - 1 - i
        at = pl.ds(pl.multiple_of(b * rows, rows), rows)
        query = dqt_ref[:, at].T
        key = sums_ref[at, :]
        decay_grad = query[:, 64:65] - key[:, 67:68]
        suffix = running_sum(tri, decay_grad, lane) + carry
        logit = forget_column(rest_ref[b, 0].astype(F32))
        forget_grad = suffix / (1.0 + jnp.exp(logit))
        both = jnp.where(low, query * SCALE, swap_halves(key))
        rest = jnp.where(low, g_ref[b, 0, :, LANES:].astype(F32), jnp.where(lane == 64, forget_grad, 0.0))
        g_ref[b, 0, :, :LANES] = both.astype(BF16)
        g_ref[b, 0, :, LANES:] = rest.astype(BF16)
        return suffix[0:1, :]

    lax.fori_loop(0, blocks, finish, jnp.zeros((1, 1), F32))


def attend_back(saved, tail_key, tail_value, mixture, packed_grad, pay):
    blocks, pairs, rows, _ = pay.shape
    length = blocks * rows
    tail_length = tail_key.shape[1]
    size = min(512, length)
    pair = lambda j: (j, 0, 0)
    across = lambda j: (0, j, 0, 0)
    entries = length * (tail_length + length // 2) * pairs
    return pl.pallas_call(
        functools.partial(attend_back_kernel, size),
        grid=(pairs,),
        in_specs=[
            pl.BlockSpec((1, length, LANES), pair),
            pl.BlockSpec((1, length, LANES), pair),
            pl.BlockSpec((1, length, LANES), pair),
            pl.BlockSpec((1, tail_length, LANES), pair),
            pl.BlockSpec((1, tail_length, LANES), pair),
            pl.BlockSpec((1, length, LANES), pair),
            pl.BlockSpec((blocks, 1, rows // 2, LANES), across),
            pl.BlockSpec((blocks, 1, rows, LANES), lambda j: (0, j, 0, 1)),
        ],
        out_specs=pl.BlockSpec((blocks, 1, rows, 2 * LANES), across),
        out_shape=jax.ShapeDtypeStruct((blocks, pairs, rows, 2 * LANES), BF16),
        scratch_shapes=[
            pltpu.VMEM((length, LANES), BF16),
            pltpu.VMEM((LANES, length), F32),
            pltpu.VMEM((length, LANES), F32),
        ],
        compiler_params=params(),
        cost_estimate=pl.CostEstimate(
            flops=40 * LANES * entries, bytes_accessed=10 * pairs * length * LANES, transcendentals=entries
        ),
        name="attend_back",
    )(*saved, tail_key, tail_value, mixture, packed_grad, pay)


def group_of(heads, ref, group, low_half):
    first = ref[2 * group].astype(F32)
    second = ref[2 * group + 1].astype(F32) if 2 * group + 1 < heads else jnp.zeros_like(first)
    return unpack_rows(low_half, first, second)


def gate_kernel(heads, ap_ref, gl_ref, o_ref):
    rows, cols = o_ref.shape
    half_low = lanes_of(rows // 2) < HEAD_SIZE
    for group in range(cols // LANES):
        at = slice(group * LANES, (group + 1) * LANES)
        mixture = group_of(heads, ap_ref, group, half_low)
        o_ref[:, at] = (mixture * jax.nn.sigmoid(gl_ref[:, at])).astype(BF16)


def gate(heads, packed, gl, micros):
    total, cols = gl.shape
    rows = total // micros
    return pl.pallas_call(
        functools.partial(gate_kernel, heads),
        grid=(micros,),
        in_specs=[
            pl.BlockSpec((heads, rows // 2, LANES), lambda m: (m, 0, 0)),
            pl.BlockSpec((rows, cols), lambda m: (m, 0)),
        ],
        out_specs=pl.BlockSpec((rows, cols), lambda m: (m, 0)),
        out_shape=jax.ShapeDtypeStruct((total, cols), BF16),
        compiler_params=params(),
        cost_estimate=pl.CostEstimate(
            flops=4 * total * cols, bytes_accessed=8 * total * cols, transcendentals=total * cols
        ),
        name="gate",
    )(packed, gl)


def feed_kernel(
    chunk,
    ff,
    x_ref,
    dy_ref,
    o_ref,
    w_ref,
    gain_ref,
    hid_ref,
    c_ref,
    u_ref,
    dgr_ref,
    dur_ref,
    out_ref,
    dc_ref,
    dg_ref,
    out_acc,
    dc_acc,
):
    parts, _, cols = o_ref.shape
    hidden = x_ref[...].astype(F32)
    for z in range(parts):
        hidden = hidden + dot(o_ref[z], w_ref[:, z * cols : (z + 1) * cols], NT)
    hid_ref[...] = hidden
    factor = rms_factor(hidden)
    c_ref[...] = (hidden * factor * gain_ref[...]).astype(BF16)
    out_acc[...] = jnp.zeros_like(out_acc)
    dc_acc[...] = jnp.zeros_like(dc_acc)

    def step(i, carry):
        at = pl.multiple_of(i * chunk, chunk)
        here = pl.ds(at, chunk)
        w_gate = w_ref[:, pl.ds(pl.multiple_of(parts * cols + at, LANES), chunk)]
        w_up = w_ref[:, pl.ds(pl.multiple_of(parts * cols + ff + at, LANES), chunk)]
        w_down = w_ref[:, pl.ds(pl.multiple_of(parts * cols + 2 * ff + at, LANES), chunk)]
        c = c_ref[...]
        gr = dot(c, w_gate)
        ur = dot(c, w_up)
        sig = jax.nn.sigmoid(gr)
        silu = gr * sig
        u = (silu * ur).astype(BF16)
        u_ref[:, here] = u
        out_acc[...] += dot(u, w_down, NT)
        du = dot(dy_ref[...], w_down)
        dgr = (du * ur * sig * (1.0 + gr * (1.0 - sig))).astype(BF16)
        dur = (du * silu).astype(BF16)
        dgr_ref[:, here] = dgr
        dur_ref[:, here] = dur
        dc_acc[...] += dot(dgr, w_gate, NT) + dot(dur, w_up, NT)
        return carry

    lax.fori_loop(0, ff // chunk, step, 0)
    out_ref[...] = out_acc[...].astype(BF16)
    dc = dc_acc[...]
    dc_ref[...] = dc.astype(BF16)

    @pl.when(pl.program_id(0) == 0)
    def _():
        dg_ref[...] = jnp.zeros_like(dg_ref)

    dg_ref[...] += jnp.sum(dc * hid_ref[...] * factor, axis=0, keepdims=True)


def feed(x, dy, o_all, weights, gain_row, ff, micros):
    total, width = x.shape
    rows = total // micros
    parts, _, cols = o_all.shape
    chunk = min(512, ff)
    whole = lambda m: (0, 0)
    part = lambda m: (m, 0)
    return pl.pallas_call(
        functools.partial(feed_kernel, chunk, ff),
        grid=(micros,),
        in_specs=[
            pl.BlockSpec((rows, width), part),
            pl.BlockSpec((rows, width), part),
            pl.BlockSpec((parts, rows, cols), lambda m: (0, m, 0)),
            pl.BlockSpec(weights.shape, whole, pipeline_mode=pl.Buffered(1)),
            pl.BlockSpec((1, width), whole),
        ],
        out_specs=[
            pl.BlockSpec((rows, width), part),
            pl.BlockSpec((rows, width), part),
            pl.BlockSpec((rows, ff), part),
            pl.BlockSpec((rows, ff), part),
            pl.BlockSpec((rows, ff), part),
            pl.BlockSpec((rows, width), part),
            pl.BlockSpec((rows, width), part),
            pl.BlockSpec((1, width), whole),
        ],
        out_shape=[
            jax.ShapeDtypeStruct((total, width), F32),
            jax.ShapeDtypeStruct((total, width), BF16),
            jax.ShapeDtypeStruct((total, ff), BF16),
            jax.ShapeDtypeStruct((total, ff), BF16),
            jax.ShapeDtypeStruct((total, ff), BF16),
            jax.ShapeDtypeStruct((total, width), BF16),
            jax.ShapeDtypeStruct((total, width), BF16),
            jax.ShapeDtypeStruct((1, width), F32),
        ],
        scratch_shapes=[pltpu.VMEM((rows, width), F32), pltpu.VMEM((rows, width), F32)],
        compiler_params=params(56),
        cost_estimate=pl.CostEstimate(
            flops=2 * total * width * (parts * cols + 6 * ff),
            bytes_accessed=2 * weights.size + 20 * total * width,
            transcendentals=total * ff,
        ),
        name="feed",
    )(x, dy, o_all, weights, gain_row)


def norm_back(source, factor, gain_row, upstream):
    scaled = upstream * gain_row
    inner = jnp.mean(scaled * source, axis=-1, keepdims=True)
    return factor * scaled - source * (factor * factor * factor) * inner


def hidden_back_kernel(
    heads, dc_ref, hid_ref, dy_ref, gain_ref, w_ref, gl_ref, ap_ref, dh_ref, dhb_ref, dgl_ref, dap_ref
):
    rows, cols = gl_ref.shape
    hidden = hid_ref[...]
    back = norm_back(hidden, rms_factor(hidden), gain_ref[...], dc_ref[...].astype(F32))
    dh = dy_ref[...].astype(F32) + back
    dh_ref[...] = dh
    dhb = dh.astype(BF16)
    dhb_ref[...] = dhb
    gated_grad = dot(dhb, w_ref[...])
    half_low = lanes_of(rows // 2) < HEAD_SIZE
    for group in range(cols // LANES):
        at = slice(group * LANES, (group + 1) * LANES)
        mixture = group_of(heads, ap_ref, group, half_low)
        gate_value = jax.nn.sigmoid(gl_ref[:, at])
        grad = gated_grad[:, at]
        dgl_ref[:, at] = (grad * mixture * gate_value * (1.0 - gate_value)).astype(BF16)
        first, second = pack_rows(half_low, grad * gate_value)
        dap_ref[2 * group] = first.astype(BF16)
        if 2 * group + 1 < heads:
            dap_ref[2 * group + 1] = second.astype(BF16)


def hidden_back(heads, dc, hidden, dy, gain_row, w_own, gl, packed, micros):
    total, width = dc.shape
    rows = total // micros
    cols = gl.shape[1]
    whole = lambda m: (0, 0)
    part = lambda m: (m, 0)
    cube = lambda m: (m, 0, 0)
    return pl.pallas_call(
        functools.partial(hidden_back_kernel, heads),
        grid=(micros,),
        in_specs=[
            pl.BlockSpec((rows, width), part),
            pl.BlockSpec((rows, width), part),
            pl.BlockSpec((rows, width), part),
            pl.BlockSpec((1, width), whole),
            pl.BlockSpec((width, cols), whole),
            pl.BlockSpec((rows, cols), part),
            pl.BlockSpec((heads, rows // 2, LANES), cube),
        ],
        out_specs=[
            pl.BlockSpec((rows, width), part),
            pl.BlockSpec((rows, width), part),
            pl.BlockSpec((rows, cols), part),
            pl.BlockSpec((heads, rows // 2, LANES), cube),
        ],
        out_shape=[
            jax.ShapeDtypeStruct((total, width), F32),
            jax.ShapeDtypeStruct((total, width), BF16),
            jax.ShapeDtypeStruct((total, cols), BF16),
            jax.ShapeDtypeStruct((micros * heads, rows // 2, LANES), BF16),
        ],
        compiler_params=params(),
        cost_estimate=pl.CostEstimate(
            flops=2 * total * width * cols, bytes_accessed=14 * total * width, transcendentals=total * cols
        ),
        name="hidden_back",
    )(dc, hidden, dy, gain_row, w_own, gl, packed)


def project_back_kernel(
    heads,
    g_ref,
    raw_ref,
    x_ref,
    dgl_ref,
    w_ref,
    gq_ref,
    gk_ref,
    grads_ref,
    da_ref,
    dg_ref,
    dgq_ref,
    dgk_ref,
    db_ref,
):
    rows, cols = dgl_ref.shape
    lane = lanes_of(rows)
    low = lane < HEAD_SIZE
    zero = jnp.zeros(lane.shape, F32)

    @pl.when(pl.program_id(0) == 0)
    def _():
        for ref in (dg_ref, dgq_ref, dgk_ref, db_ref):
            ref[...] = jnp.zeros_like(ref)

    def head_back(raw, upstream, gain_row, sum_ref):
        factor = lax.rsqrt(per_head(low, raw * raw) + EPSILON)
        scaled = upstream * gain_row
        inner = per_head(low, scaled * raw)
        sum_ref[...] += jnp.sum(upstream * raw * factor, axis=0, keepdims=True)
        return factor * scaled - raw * (factor * factor * factor) * inner

    forget = zero
    for group in range(cols // LANES):
        at = group * LANES
        here = slice(at, at + LANES)
        pair = (2 * group, 2 * group + 1)
        both = [g_ref[h, :, :LANES].astype(F32) if h < heads else zero for h in pair]
        rest = [g_ref[h, :, LANES:].astype(F32) if h < heads else zero for h in pair]
        query = head_back(raw_ref[:, here], merge_pair(low, *both), gq_ref[...], dgq_ref)
        key = head_back(
            raw_ref[:, cols + at : cols + at + LANES],
            merge_swapped(low, *both),
            gk_ref[...],
            dgk_ref,
        )
        grads_ref[:, here] = query.astype(BF16)
        grads_ref[:, cols + at : cols + at + LANES] = key.astype(BF16)
        value = merge_pair(low, *rest)
        grads_ref[:, 2 * cols + at : 2 * cols + at + LANES] = value.astype(BF16)
        for h, block in zip(pair, rest):
            if h < heads:
                forget = jnp.where(lane == h, block[:, 64:65], forget)
    grads_ref[:, 3 * cols : 4 * cols] = dgl_ref[...]
    grads_ref[:, 4 * cols :] = forget.astype(BF16)
    db_ref[...] += jnp.sum(forget, axis=0, keepdims=True)
    da = dot(grads_ref[...], w_ref[...], NT)
    da_ref[...] = da.astype(BF16)
    x = x_ref[...].astype(F32)
    dg_ref[...] += jnp.sum(da * x * rms_factor(x), axis=0, keepdims=True)


def project_back(heads, returned, raw, x, dgl, weights, gq_row, gk_row, micros):
    total, width = x.shape
    rows = total // micros
    cols = dgl.shape[1]
    wide = weights.shape[1]
    whole = lambda m: (0, 0)
    part = lambda m: (m, 0)
    return pl.pallas_call(
        functools.partial(project_back_kernel, heads),
        grid=(micros,),
        in_specs=[
            pl.BlockSpec((heads, rows, 2 * LANES), lambda m: (m, 0, 0)),
            pl.BlockSpec((rows, 2 * cols), part),
            pl.BlockSpec((rows, width), part),
            pl.BlockSpec((rows, cols), part),
            pl.BlockSpec((width, wide), whole),
            pl.BlockSpec((1, LANES), whole),
            pl.BlockSpec((1, LANES), whole),
        ],
        out_specs=[
            pl.BlockSpec((rows, wide), part),
            pl.BlockSpec((rows, width), part),
            pl.BlockSpec((1, width), whole),
            pl.BlockSpec((1, LANES), whole),
            pl.BlockSpec((1, LANES), whole),
            pl.BlockSpec((1, LANES), whole),
        ],
        out_shape=[
            jax.ShapeDtypeStruct((total, wide), BF16),
            jax.ShapeDtypeStruct((total, width), BF16),
            jax.ShapeDtypeStruct((1, width), F32),
            jax.ShapeDtypeStruct((1, LANES), F32),
            jax.ShapeDtypeStruct((1, LANES), F32),
            jax.ShapeDtypeStruct((1, LANES), F32),
        ],
        compiler_params=params(),
        cost_estimate=pl.CostEstimate(
            flops=2 * total * width * wide,
            bytes_accessed=2 * width * wide + 12 * total * width,
            transcendentals=0,
        ),
        name="project_back",
    )(returned, raw, x, dgl, weights, gq_row, gk_row)


def input_back_kernel(da_ref, x_ref, dh_ref, gain_ref, out_ref):
    x = x_ref[...].astype(F32)
    out_ref[...] = dh_ref[...] + norm_back(
        x, rms_factor(x), gain_ref[...], da_ref[...].astype(F32)
    )


def input_back(da, x, dh, gain_row, micros):
    total, width = x.shape
    rows = total // micros
    part = lambda m: (m, 0)
    block = pl.BlockSpec((rows, width), part)
    return pl.pallas_call(
        input_back_kernel,
        grid=(micros,),
        in_specs=[block, block, block, pl.BlockSpec((1, width), lambda m: (0, 0))],
        out_specs=block,
        out_shape=jax.ShapeDtypeStruct((total, width), F32),
        compiler_params=params(),
        cost_estimate=pl.CostEstimate(
            flops=10 * total * width, bytes_accessed=12 * total * width, transcendentals=0
        ),
        name="input_back",
    )(da, x, dh, gain_row)


def pad_to(array, size, axis):
    missing = size - array.shape[axis]
    if missing == 0:
        return array
    widths = [(0, missing if i == axis else 0) for i in range(array.ndim)]
    return jnp.pad(array, widths)


def turned_product(left, right):
    return lax.dot_general(
        left, right, (((0,), (0,)), ((), ())), preferred_element_type=F32
    ).astype(BF16)


def shards(
    inputs,
    cotangent,
    tail_keys,
    tail_values,
    tail_forget,
    gain_one,
    gain_two,
    w_query,
    w_key,
    w_value,
    w_forget,
    forget_bias,
    query_gain,
    key_gain,
    w_outgate,
    w_out,
    w_gate,
    w_up,
    w_down,
):
    micros, rows, width = inputs.shape
    total = micros * rows
    own_cols = w_query.shape[1]
    heads = w_forget.shape[1]
    ff = w_gate.shape[1]
    seq_count = lax.axis_size("seq")
    head_count = lax.axis_size("head")
    seq_rank = lax.axis_index("seq")
    head_rank = lax.axis_index("head")
    cols = -(-own_cols // LANES) * LANES
    pair_total = micros * heads
    pairs = -(-pair_total // seq_count)
    padded_pairs = pairs * seq_count
    tail_length = tail_keys.shape[1]

    x = inputs.reshape(total, width)
    dy = cotangent.reshape(total, width)

    small = jnp.concatenate([w_forget, gain_one[:, None], gain_two[:, None]], axis=1)
    first_shard = jnp.concatenate(
        [pad_to(w, cols, 1) for w in (w_query, w_key, w_value, w_outgate)]
        + [pad_to(small, LANES, 1)],
        axis=1,
    )
    first = lax.all_gather(first_shard, "seq", axis=0, tiled=True)
    out_all = lax.all_gather(pad_to(w_out.T, cols, 1), "head", axis=1, tiled=True)
    second_shard = jnp.concatenate([out_all, w_gate, w_up, w_down.T], axis=1)
    second = lax.all_gather(second_shard, "seq", axis=0, tiled=True)
    out_own = lax.dynamic_slice_in_dim(second, head_rank * cols, cols, 1)
    gain_one_row = first[:, 4 * cols + heads].astype(F32)[None, :]
    gain_two_row = first[:, 4 * cols + heads + 1].astype(F32)[None, :]
    bias_here = lax.dynamic_slice_in_dim(forget_bias, head_rank * heads, heads, 0)
    bias_row = pad_to(bias_here[None, :], LANES, 1)
    gq_row = jnp.tile(query_gain.astype(F32), 2)[None, :]
    gk_row = jnp.tile(key_gain.astype(F32), 2)[None, :]

    tail_key_parts, tail_value_parts = [], []
    for j in range(pairs):
        p = jnp.minimum(seq_rank * pairs + j, pair_total - 1)
        m, h = p // heads, p % heads
        tail_of = lambda array, wide: lax.dynamic_slice(
            array, (m, 0, h * wide), (1, tail_length, wide)
        )[0]
        forget = tail_of(tail_forget, 1)
        decay = jnp.cumsum(forget, axis=0) - jnp.sum(forget, axis=0, keepdims=True)
        high = lax.reduce_precision(decay, 8, 7)
        middle = lax.reduce_precision(decay - high, 8, 7)
        least = decay - high - middle
        ones = jnp.ones((tail_length, 3), BF16)
        parts = jnp.concatenate([-high, -middle, -least], axis=1).astype(BF16)
        tail_key_parts.append(
            pad_to(jnp.concatenate([tail_of(tail_keys, HEAD_SIZE), ones, parts], axis=1), LANES, 1)
        )
        tail_value_parts.append(
            pad_to(jnp.concatenate([tail_of(tail_values, HEAD_SIZE), ones], axis=1), LANES, 1)
        )
    tail_key = jnp.stack(tail_key_parts)
    tail_value = jnp.stack(tail_value_parts)

    def to_owners(array):
        array = pad_to(array, padded_pairs, 0)
        array = array.reshape((seq_count, pairs) + array.shape[1:])
        return lax.all_to_all(array, "seq", 0, 0, tiled=True)

    def from_owners(array):
        array = lax.all_to_all(array, "seq", 0, 0, tiled=True)
        return array.reshape((padded_pairs,) + array.shape[2:])[:pair_total]

    a, raw, gl, pay = project(
        heads, cols, x, first, bias_row, gain_one_row, gq_row, gk_row, micros
    )
    pay = to_owners(pay)
    packed, mixture, *saved = attend(pay, tail_key, tail_value)
    packed = from_owners(packed)
    o = gate(heads, packed, gl, micros)
    o_all = lax.all_gather(o, "head", axis=0)
    hidden, c, u, dgr, dur, out_part, dc_part, dgain_two = feed(
        x, dy, o_all, second, gain_two_row, ff, micros
    )
    dc = lax.psum(dc_part, "head")
    out_sum = lax.psum(out_part, "head")
    layer_out = (hidden + out_sum.astype(F32)).astype(BF16)
    dh, dhb, dgl, dap = hidden_back(heads, dc, hidden, dy, gain_two_row, out_own, gl, packed, micros)
    dap = to_owners(dap)
    returned = attend_back(saved, tail_key, tail_value, mixture, dap, pay)
    returned = from_owners(returned)
    grads, da_part, dgain_one, dgq, dgk, dbias = project_back(
        heads, returned, raw, x, dgl, first, gq_row, gk_row, micros
    )
    da = lax.psum(da_part, "head")
    input_grad = input_back(da, x, dh, gain_one_row, micros)

    def scattered(grad):
        return lax.psum_scatter(grad, "seq", scatter_dimension=0, tiled=True).astype(F32)

    grad_gate = scattered(turned_product(c, dgr))
    grad_up = scattered(turned_product(c, dur))
    grad_down = scattered(turned_product(dy, u)).T
    grad_out = scattered(turned_product(dhb, o))[:, :own_cols].T
    grad_first = scattered(turned_product(a, grads))

    bias_full = lax.dynamic_update_slice_in_dim(
        jnp.zeros(forget_bias.shape, F32), dbias[0, :heads], head_rank * heads, 0
    )
    fold = lambda row: row[0, :HEAD_SIZE] + row[0, HEAD_SIZE:]
    gains, bias_total, gq_total, gk_total = lax.psum(
        (jnp.concatenate([dgain_one, dgain_two], axis=0), bias_full, fold(dgq), fold(dgk)),
        ("seq", "head"),
    )
    own_rows = gain_one.shape[0]
    gains = lax.dynamic_slice_in_dim(gains, seq_rank * own_rows, own_rows, 1)
    shape = inputs.shape
    return (
        layer_out.reshape(shape),
        input_grad.reshape(shape),
        gains[0],
        gains[1],
        grad_first[:, :own_cols],
        grad_first[:, cols : cols + own_cols],
        grad_first[:, 2 * cols : 2 * cols + own_cols],
        grad_first[:, 4 * cols : 4 * cols + heads],
        bias_total,
        gq_total,
        gk_total,
        grad_first[:, 3 * cols : 3 * cols + own_cols],
        grad_out,
        grad_gate,
        grad_up,
        grad_down,
    )


def solution(mesh):
    by_rows = P("seq", "head")
    by_cols = P("head", "seq")
    placed = (
        P(None, "seq", None),
        P(None, "seq", None),
        P(None, None, "head"),
        P(None, None, "head"),
        P(None, None, "head"),
        P("seq"),
        P("seq"),
        by_rows,
        by_rows,
        by_rows,
        by_rows,
        P(),
        P(),
        P(),
        by_rows,
        by_cols,
        by_rows,
        by_rows,
        by_cols,
    )
    return jax.shard_map(
        shards,
        mesh=mesh,
        in_specs=placed,
        out_specs=(
            P(None, "seq", None),
            P(None, "seq", None),
            P("seq"),
            P("seq"),
            by_rows,
            by_rows,
            by_rows,
            by_rows,
            P(),
            P(),
            P(),
            by_rows,
            by_cols,
            by_rows,
            by_rows,
            by_cols,
        ),
        check_vma=False,
    )
```

time: 4080 us -> 991 us (0.24)
  waiting for transfers between devices: 2630 us -> 558 us
  blocking collectives: 598 us -> 83.2 us
  matrix products: 320 us -> 37.8 us
  local copies, waits for them, and re-layouts: 272 us -> 46.6 us
  Pallas kernels: 0 us -> 204 us
  other arithmetic: 162 us -> 24.3 us
  loops' own time: 45.7 us -> 0 us
    reduce_scatter x44 -> x4, waiting for transfers between devices: 1820 us -> 55.5 us  [scattered(): lax.psum_scatter(grad, 'seq', scatter_dimension=0, tiled=True).astype(F32)]
    all_gather x13 -> x1, blocking collectives: 519 us -> 21.6 us  [shards(): lax.all_gather(pad_to(w_out.T, cols, 1), 'head', axis=1, tiled=True)]
    psum x4 -> x2, waiting for transfers between devices: 576 us -> 277 us  [the longest x1 178 us: shards(): out_sum = lax.psum(out_part, 'head')]
    dot_general x152 -> x5, matrix products: 320 us -> 37.8 us  [turned_product(): lax.dot_general(left, right, (((0,), (0,)), ((), ())), preferred_element_...]
    pallas_call x0 -> x8, Pallas kernels: none -> 204 us  [the longest x1 62.7 us: attend_back(): pl.pallas_call(functools.partial(attend_back_kernel, size), grid=(pairs,)...]
    unnamed x72 -> x11, waiting for transfers between devices: 134 us -> 0.18 us
    dynamic_slice x81 -> x1, local copies, waits for them, and re-layouts: 98.8 us -> 1.39 us  [shards(): out_own = lax.dynamic_slice_in_dim(second, head_rank * cols, cols, 1)]
    all_to_all x0 -> x3, waiting for transfers between devices: none -> 65 us  [the longest x1 40.9 us: from_owners(): array = lax.all_to_all(array, 'seq', 0, 0, tiled=True)]
  transfers between devices with their start and end apart: 68 -> 13, of which waited for: 54 -> 10; matrix products, arithmetic and copies ran while one was open for 14% -> 9% of each run, Pallas kernels for 0% -> 10%
where the time goes in v1:
time: 991 us; the launch traced here: 983 us
  waiting for transfers between devices  558 us (56%)
  Pallas kernels  204 us (21%)
  blocking collectives  83.2 us (8%)
  local copies, waits for them, and re-layouts  46.6 us (5%)
  matrix products  37.8 us (4%)
  other arithmetic  24.3 us (2%)
  between operations  15.1 us (2%)
  starting transfers between devices  13.6 us (1%)
    psum x1, waiting for transfers between devices, shards(): out_sum = lax.psum(out_part, 'head')  178 us
    psum x1, waiting for transfers between devices, shards(): dc = lax.psum(dc_part, 'head')  99.5 us
    all_gather x1, waiting for transfers between devices, shards(): second = lax.all_gather(second_shard, 'seq', axis=0, tiled=True)  78.9 us
    pallas_call x1, Pallas kernels, attend_back(): pl.pallas_call(functools.partial(attend_back_kernel, size), grid=(pairs,)...  62.7 us
    reduce_scatter x4, waiting for transfers between devices, scattered(): lax.psum_scatter(grad, 'seq', scatter_dimension=0, tiled=True).astype(F32)  55.5 us
    pallas_call x1, Pallas kernels, attend(): pl.pallas_call(functools.partial(attend_kernel, size), grid=(pairs,), in_...  47.6 us
    psum x1, blocking collectives, shards(): lax.psum((jnp.concatenate([dgain_one, dgain_two], axis=0), bias_full, fol...  46.4 us
    all_gather x1, waiting for transfers between devices, shards(): o_all = lax.all_gather(o, 'head', axis=0)  42.4 us
  transfers between devices with their start and end apart: 13, of which 10 were waited for; matrix products, arithmetic and copies ran while one was open for 9% of the time, Pallas kernels for 10%

profile of v1, /device:TPU:0, one launch (start us, length us, event | category | flops | bytes accessed | tf_op | source)
XLA Modules:
  0.0 982.7 jit_solution(5089161700610380017)
XLA Ops:
  18.4 39.1 %all-gather.5.cloned.1.call-done.w_ref = bf16[1536,1664]{1,0:T(8,128)(2,1)} async-done(((bf16[192,1664]{1,0:T(8,128)(2,1)}), bf16[1536,1664]{1,0:T(8,128)(2,1)}) %all-gather.5.cloned.1.call-update) | async-done | bytes 5111824 | tf_op jit(solution)/shard_map/all_gather | solution.py:840
  59.2 12.9 %project.1 = (bf16[1024,1536]{1,0:T(8,128)(2,1)S(1)}, f32[1024,768]{1,0:T(8,128)}, f32[1024,384]{1,0:T(8,128)S(1)}, bf16[24,256,256]{2,1,0:T(8,128)(2,1)}) custom-call(bf16[1024,1536]{1,0:T(8,128)(2,1)} %bitcast.89, bf16[1536,1664]{1,0:T(8,128)(2,1)} %all-gather.5.cloned.1.call-done.w_ref, f32[1,128]{1,0:T(1,128)S(1)} %pad.32.bias_ref, ...), custom_call_target="tpu_custom_call" | custom-call | flops 5234491392 | bytes 20840448 | tf_op jit(solution)/shard_map/project/pallas_call | solution.py:141
  98.2 17.8 %all-to-all-done.pay_ref.rest_ref = bf16[8,3,256,256]{3,2,1,0:T(8,128)(2,1)} async-done(((bf16[8,3,256,256]{3,2,1,0:T(8,128)(2,1)}), bf16[8,3,256,256]{3,2,1,0:T(8,128)(2,1)}, u32[]{:S(2)}, u32[]{:S(2)}) %all-to-all-start) | async-done | bytes 3145760 | tf_op jit(solution)/shard_map/all_to_all | solution.py:878
  116.0 47.6 %attend.1 = (bf16[8,3,128,128]{3,2,1,0:T(8,128)(2,1)S(1)}, f32[3,2048,128]{2,1,0:T(8,128)}, bf16[3,2048,128]{2,1,0:T(8,128)(2,1)S(1)}, bf16[3,2048,128]{2,1,0:T(8,128)(2,1)S(1)}, bf16[3,2048,128]{2,1,0:T(8,128)(2,1)}) custom-call(bf16[8,3,256,256]{3,2,1,0:T(8,128)(2,1)} %all-to-all-done.pay_ref.rest_ref, bf16[3,1024,128]{2,1,0:T(8,128)(2,1)S(1)} %pad_maximum_fusion.1.tk_ref, ...), custom_call_target="tpu_custom_call" | custom-call | flops 25769803776 | bytes 6291456 | tf_op jit(solution)/shard_map/attend/pallas_call | solution.py:253
  164.8 15.2 %all_to_all.20 = bf16[8,3,128,128]{3,2,1,0:T(8,128)(2,1)S(1)} all-to-all(bf16[8,3,128,128]{3,2,1,0:T(8,128)(2,1)S(1)} %get-tuple-element.44), channel_id=1, replica_groups=mesh['seq'=8,'head'=4] {'seq'}, dimensions={0} | all-to-all | bytes 1572864 | tf_op jit(solution)/shard_map/all_to_all | solution.py:881
  181.9 21.6 %all_gather.18 = bf16[192,1536]{1,0:T(8,128)(2,1)S(1)} all-gather(bf16[192,384]{1,0:T(8,128)(2,1)} %bitcast.94), channel_id=1, replica_groups=mesh['seq'=8,'head'=4] {'head'}, dimensions={1}, use_global_device_ids=true | all-gather | bytes 737280 | tf_op jit(solution)/shard_map/all_gather | solution.py:841
  205.8 42.4 %all-gather.9.cloned.1.call-done = bf16[4096,384]{1,0:T(8,128)(2,1)} async-done(((bf16[1024,384]{1,0:T(8,128)(2,1)}), bf16[4096,384]{1,0:T(8,128)(2,1)}) %all-gather.9.cloned.1.call-update) | async-done | bytes 3145744 | tf_op jit(solution)/shard_map/all_gather | solution.py:891
  248.2 78.9 %all-gather.7.cloned.1.call-done.w_ref = bf16[1536,4608]{1,0:T(8,128)(2,1)} async-done(((bf16[192,4608]{1,0:T(8,128)(2,1)}), bf16[1536,4608]{1,0:T(8,128)(2,1)}) %all-gather.7.cloned.1.call-update) | async-done | bytes 14155792 | tf_op jit(solution)/shard_map/all_gather | solution.py:843
  327.1 42.1 %feed.1 = (f32[1024,1536]{1,0:T(8,128)}, bf16[1024,1536]{1,0:T(8,128)(2,1)}, bf16[1024,1024]{1,0:T(8,128)(2,1)}, bf16[1024,1024]{1,0:T(8,128)(2,1)}, bf16[1024,1...) custom-call(bf16[1024,1536]{1,0:T(8,128)(2,1)} %bitcast.90, ...), custom_call_target="tpu_custom_call" | custom-call | flops 24159191040 | bytes 45613056 | tf_op jit(solution)/shard_map/feed/pallas_call | solution.py:537
  369.3 7.6 fusion
  381.9 7.7 convolution_convert_fusion.2
  391.0 99.5 %all-reduce.16.cloned.1.call-done.dc_ref = bf16[1024,1536]{1,0:T(8,128)(2,1)} async-done(((bf16[1024,1536]{1,0:T(8,128)(2,1)}), bf16[1024,1536]{1,0:T(8,128)(2,1)}) %all-reduce.16.cloned.1.call-update) | async-done | bytes 3145744 | tf_op jit(solution)/shard_map/psum | solution.py:895
  490.5 10.0 %hidden_back.1 = (f32[1024,1536]{1,0:T(8,128)}, bf16[1024,1536]{1,0:T(8,128)(2,1)}, bf16[1024,384]{1,0:T(8,128)(2,1)S(1)}, bf16[24,128,128]{2,1,0:T(8,128)(2,1)S(1)}) custom-call(bf16[1024,1536]{1,0:T(8,128)(2,1)} %all-reduce.16.cloned.1.call-done.dc_ref, f32[1024,1536]{1,0:T(8,128)} %get-tuple-element.46.hid_ref, bf16[1024,1536]{1,0:T(8,128)(2,1)} %bitcast.87, ...), custom_call_target="tpu_custom_call" | custom-call | flops 1207959552 | bytes 22020096 | tf_op jit(solution)/shard_map/hidden_back/pallas_call | solution.py:615
  506.0 7.7 convolution_convert_fusion.3
  522.9 62.7 %attend_back.1 = bf16[8,3,256,256]{3,2,1,0:T(8,128)(2,1)} custom-call(bf16[3,2048,128]{2,1,0:T(8,128)(2,1)S(1)} %copy-done.20, bf16[3,2048,128]{2,1,0:T(8,128)(2,1)S(1)} %copy-done.22, bf16[3,2048,128]{2,1,0:T(8,128)(2,1)} %get-tuple-element.50.v_ref, bf16[3,1024,128]{2,1,0:T(8,128)(2,1)S(1)} %copy-done.4, bf16[3,1024,128]{2,1,0:T(8,128)(2,1)S(1)} %copy-done.6, ...), custom_call_target="tpu_custom_call" | custom-call | flops 64424509440 | bytes 7864320 | tf_op jit(solution)/shard_map/attend_back/pallas_call | solution.py:404
  595.5 40.9 %all-to-all-done.3 = bf16[8,3,256,256]{3,2,1,0:T(8,128)(2,1)} async-done(((bf16[8,3,256,256]{3,2,1,0:T(8,128)(2,1)}), bf16[8,3,256,256]{3,2,1,0:T(8,128)(2,1)}, u32[]{:S(2)}, u32[]{:S(2)}) %all-to-all-start.3) | async-done | bytes 3145760 | tf_op jit(solution)/shard_map/all_to_all | solution.py:881
  636.4 18.7 %project_back.1 = (bf16[1024,1664]{1,0:T(8,128)(2,1)}, bf16[1024,1536]{1,0:T(8,128)(2,1)}, f32[1,1536]{1,0:T(1,128)S(1)}, f32[1,128]{1,0:T(1,128)S(1)}, f32[1,128]{1,0:T(1,128)S(1)}, /*index=5*/f32[1,128]{1,0:T(1,128)S(1)}) custom-call(bf16[24,256,256]{2,1,0:T(8,128)(2,1)} %bitcast.34.g_ref, f32[1024,768]{1,0:T(8,128)} %get-tuple-element.54.raw_ref, ...), custom_call_target="tpu_custom_call" | custom-call | flops 5234491392 | bytes 23986176 | tf_op jit(solution)/shard_map/project_back/pallas_call | solution.py:717
  657.0 9.7 convolution_convert_fusion
  673.2 13.7 %reduce-scatter.10.cloned.1.call-done = bf16[192,384]{1,0:T(8,128)(2,1)} async-done(((bf16[1536,384]{1,0:T(8,128)(2,1)}), bf16[192,384]{1,0:T(8,128)(2,1)}) %reduce-scatter.10.cloned.1.call-update) | async-done | bytes 147472 | tf_op jit(solution)/shard_map/reduce_scatter | solution.py:909
  688.8 46.4 %all-reduce.11 = (f32[2,1536]{1,0:T(2,128)S(1)}, f32[24]{0:T(128)}, f32[64]{0:T(128)}, f32[64]{0:T(128)}) all-reduce(f32[2,1536]{1,0:T(2,128)S(1)} %pad_maximum_fusion.3, f32[24]{0:T(128)S(1)} %bitcast_dynamic-update-slice_fusion, f32[64]{0:T(128)S(1)} %add_bitcast_fusion.1, ...), channel_id=1, replica_groups=mesh['seq'=8,'head'=4] {'seq','head'}, use_global_device_ids=true, to_apply=%region_12.13 | all-reduce | flops 3224 | bytes 25792 | tf_op jit(solution)/shard_map/psum | solution.py:921
  735.8 177.8 %all-reduce.18.cloned.1.call-done = (bf16[1024,1536]{1,0:T(8,128)(2,1)}, bf16[1024,1536]{1,0:T(8,128)(2,1)}) async-done(((bf16[1024,1536]{1,0:T(8,128)(2,1)}, bf16[1024,1536]{1,0:T(8,128)(2,1)}), (bf16[1024,1536]{1,0:T(8,128)(2,1)}, bf16[1024,1536]{1,0:T(8,128)(2,1)})) %all-reduce.18.cloned.1.call-update) | async-done | bytes 6291472 | tf_op jit(solution)/shard_map/psum | solution.py:896
  915.5 8.0 input_back.1
  923.5 6.5 add_convert_fusion
  930.0 41.8 %reduce-scatter.8.cloned.1.call-done = bf16[192,1664]{1,0:T(8,128)(2,1)} async-done(((bf16[1536,1664]{1,0:T(8,128)(2,1)}), bf16[192,1664]{1,0:T(8,128)(2,1)}) %reduce-scatter.8.cloned.1.call-update) | async-done | bytes 638992 | tf_op jit(solution)/shard_map/reduce_scatter | solution.py:909
  (168 shorter events, 91.3 us)
Async XLA Ops:
  7.2 50.3 %all-gather.5.cloned.1.call-start = ((), (), s32[]{:S(2)}) async-start(), calls=%async_computation.9 | async-start | bytes 5750784 | tf_op jit(solution)/shard_map/all_gather | solution.py:840
  17.7 54.4 %copy-start.13 = (f32[1,128]{1,0:T(1,128)}, f32[1,128]{1,0:T(1,128)S(1)}, u32[]{:S(2)}) copy-start(f32[1,128]{1,0:T(1,128)S(1)} %broadcast_in_dim_tile.6.gq_ref) | copy-start | bytes 1540
  18.4 53.6 %copy-start.15 = (f32[1,128]{1,0:T(1,128)}, f32[1,128]{1,0:T(1,128)S(1)}, u32[]{:S(2)}) copy-start(f32[1,128]{1,0:T(1,128)S(1)} %broadcast_in_dim_tile.7.gk_ref) | copy-start | bytes 1540
  73.7 42.3 %all-to-all-start = ((bf16[8,3,256,256]{3,2,1,0:T(8,128)(2,1)}), bf16[8,3,256,256]{3,2,1,0:T(8,128)(2,1)}, u32[]{:S(2)}, u32[]{:S(2)}) async-start(bf16[8,3,256,256]{3,2,1,0:T(8,128)(2,1)} %bitcast.84), calls=%async_computation | async-start | bytes 6291456 | tf_op jit(solution)/shard_map/all_to_all | solution.py:878
  78.2 170.1 %all-gather.9.cloned.1.call-start = ((), (), s32[]{:S(2)}) async-start(), calls=%async_computation.16 | async-start | bytes 3932160 | tf_op jit(solution)/shard_map/all_gather | solution.py:891
  98.1 65.5 %copy-start.3 = (bf16[3,1024,128]{2,1,0:T(8,128)(2,1)}, bf16[3,1024,128]{2,1,0:T(8,128)(2,1)S(1)}, u32[]{:S(2)}) copy-start(bf16[3,1024,128]{2,1,0:T(8,128)(2,1)S(1)} %pad_maximum_fusion.1.tk_ref) | copy-start | bytes 2359300
  98.2 65.4 %copy-start.5 = (bf16[3,1024,128]{2,1,0:T(8,128)(2,1)}, bf16[3,1024,128]{2,1,0:T(8,128)(2,1)S(1)}, u32[]{:S(2)}) copy-start(bf16[3,1024,128]{2,1,0:T(8,128)(2,1)S(1)} %pad_maximum_fusion.2.tv_ref) | copy-start | bytes 2359300
  164.8 38.7 %copy-start.31 = (bf16[192,1024]{1,0:T(8,128)(2,1)S(1)}, bf16[192,1024]{1,0:T(8,128)(2,1)}, u32[]{:S(2)}) copy-start(bf16[192,1024]{1,0:T(8,128)(2,1)} %param.35) | copy-start | bytes 1179652
  181.9 145.3 %all-gather.7.cloned.1.call-start = ((), (), s32[]{:S(2)}) async-start(), calls=%async_computation.10 | async-start | bytes 15925248 | tf_op jit(solution)/shard_map/all_gather | solution.py:843
  205.0 285.5 %all-reduce.16.cloned.1.call-start = ((), (), s32[]{:S(2)}) async-start(), calls=%async_computation.11 | async-start | bytes 6291456 | tf_op jit(solution)/shard_map/psum | solution.py:895
  369.3 297.5 %reduce-scatter.16.cloned.1.call-start = ((), (), s32[]{:S(2)}) async-start(), calls=%async_computation.17 | async-start | bytes 3538944
  381.6 287.7 %reduce-scatter.14.cloned.1.call-start = ((), (), s32[]{:S(2)}) async-start(), calls=%async_computation.15 | async-start | bytes 3538944 | tf_op jit(solution)/shard_map/reduce_scatter | solution.py:909
  389.6 101.0 %copy-start.8 = (f32[1,1536]{1,0:T(1,128)S(1)}, f32[1,1536]{1,0:T(1,128)}, u32[]{:S(2)}) copy-start(f32[1,1536]{1,0:T(1,128)} %reshape.432.gain_ref) | copy-start | bytes 18436
  502.3 17.7 %all-to-all-start.2 = ((bf16[8,3,128,128]{3,2,1,0:T(8,128)(2,1)}), bf16[8,3,128,128]{3,2,1,0:T(8,128)(2,1)S(1)}, u32[]{:S(2)}, u32[]{:S(2)}) async-start(bf16[8,3,128,128]{3,2,1,0:T(8,128)(2,1)} %bitcast.82), calls=%async_computation.2 | async-start | bytes 1572864 | tf_op jit(solution)/shard_map/all_to_all | solution.py:878
  506.0 165.3 %reduce-scatter.12.cloned.1.call-start = ((), (), s32[]{:S(2)}) async-start(), calls=%async_computation.14 | async-start | bytes 3538944 | tf_op jit(solution)/shard_map/reduce_scatter | solution.py:909
  585.6 50.8 %all-to-all-start.3 = ((bf16[8,3,256,256]{3,2,1,0:T(8,128)(2,1)}), bf16[8,3,256,256]{3,2,1,0:T(8,128)(2,1)}, u32[]{:S(2)}, u32[]{:S(2)}) async-start(bf16[8,3,256,256]{3,2,1,0:T(8,128)(2,1)} %attend_back.1), calls=%async_computation.3 | async-start | bytes 6291456 | tf_op jit(solution)/shard_map/all_to_all | solution.py:881
  590.1 96.9 %reduce-scatter.10.cloned.1.call-start = ((), (), s32[]{:S(2)}) async-start(), calls=%async_computation.13 | async-start | bytes 1327104 | tf_op jit(solution)/shard_map/reduce_scatter | solution.py:909
  590.4 46.0 %copy-start.12 = (bf16[1024,384]{1,0:T(8,128)(2,1)S(1)}, bf16[1024,384]{1,0:T(8,128)(2,1)}, u32[]{:S(2)}) copy-start(bf16[1024,384]{1,0:T(8,128)(2,1)} %copy-done.11) | copy-start | bytes 2359300
  590.4 46.0 %copy-start.14 = (f32[1,128]{1,0:T(1,128)S(1)}, f32[1,128]{1,0:T(1,128)}, u32[]{:S(2)}) copy-start(f32[1,128]{1,0:T(1,128)} %copy-done.13) | copy-start | bytes 1540
  590.4 46.0 %copy-start.16 = (f32[1,128]{1,0:T(1,128)S(1)}, f32[1,128]{1,0:T(1,128)}, u32[]{:S(2)}) copy-start(f32[1,128]{1,0:T(1,128)} %copy-done.15) | copy-start | bytes 1540
  595.5 318.1 %all-reduce.18.cloned.1.call-start = ((), (), s32[]{:S(2)}) async-start(), calls=%async_computation.18 | async-start | bytes 12582912 | tf_op jit(solution)/shard_map/psum | solution.py:896
  655.2 316.6 %reduce-scatter.8.cloned.1.call-start = ((), (), s32[]{:S(2)}) async-start(), calls=%async_computation.12 | async-start | bytes 5750784 | tf_op jit(solution)/shard_map/reduce_scatter | solution.py:909
  668.0 245.6 %copy-start.10 = (f32[1,1536]{1,0:T(1,128)S(1)}, f32[1,1536]{1,0:T(1,128)}, u32[]{:S(2)}) copy-start(f32[1,1536]{1,0:T(1,128)} %copy-done.9) | copy-start | bytes 18436
  923.5 51.9 %copy-start.1 = (f32[24]{0:T(128)S(1)}, f32[24]{0:T(128)}, u32[]{:S(2)}) copy-start(f32[24]{0:T(128)} %param.30) | copy-start | bytes 292
  (22 other events, 199.1 us)
Sparse Core Ops, SparseCore 0:
  14.2 43.2 all-gather.4
  182.0 66.1 all-gather.8
  250.1 76.9 all-gather.6
  369.4 121.0 all-reduce.15
  493.8 45.2 reduce-scatter.15
  542.7 46.3 reduce-scatter.13
  592.4 54.1 reduce-scatter.11
  650.1 36.7 reduce-scatter.9
  689.4 224.1 all-reduce.17
  917.0 54.7 reduce-scatter.7

commit v2 on v1

v2 whole, which is shorter than its diff:
```python
import functools

import jax
import jax.numpy as jnp
from jax import lax
from jax.experimental import pallas as pl
from jax.experimental.pallas import tpu as pltpu
from jax.sharding import PartitionSpec as P

HEAD_SIZE = 64
LANES = 128
EPSILON = 1e-06
F32 = jnp.float32
BF16 = jnp.bfloat16
NN = (((1,), (0,)), ((), ()))
NT = (((1,), (1,)), ((), ()))
HIDE = -1e30
SCALE = HEAD_SIZE**-0.5
STRIP = 64
MIB = 1024 * 1024


def dot(left, right, dims=NN):
    return lax.dot_general(left, right, dims, preferred_element_type=F32)


def params():
    return pltpu.CompilerParams(vmem_limit_bytes=60 * MIB)


def linked(kernel, inputs, extra, outputs):
    def body(*refs):
        token = refs[inputs + extra + outputs]
        token[...] = jnp.zeros_like(token)
        kernel(
            *refs[:inputs],
            *refs[inputs + extra : inputs + extra + outputs],
            *refs[inputs + extra + outputs + 1 :],
        )

    return body


class Order:
    def __init__(self):
        self.tokens = []

    def call(self, kernel, name, grid, ins, outs, us, scratch=(), before=(), scalars=(), after=()):
        arrays = list(scalars) + [array for array, _ in ins]
        extra = list(before) + list(after) + self.tokens
        count = len(arrays)
        whole = lambda *at: (0, 0)
        out_specs = [spec for _, _, spec in outs] + [pl.BlockSpec((8, LANES), whole)]
        out_shape = [jax.ShapeDtypeStruct(shape, kind) for shape, kind, _ in outs]
        out_shape.append(jax.ShapeDtypeStruct((8, LANES), F32))
        *results, token = pl.pallas_call(
            linked(kernel, count, len(extra), len(outs)),
            grid_spec=pltpu.PrefetchScalarGridSpec(
                num_scalar_prefetch=len(scalars),
                grid=grid,
                in_specs=[spec for _, spec in ins] + [pl.BlockSpec(memory_space=pl.ANY)] * len(extra),
                out_specs=out_specs,
                scratch_shapes=list(scratch),
            ),
            out_shape=out_shape,
            input_output_aliases={count + i: i for i in range(len(before))},
            compiler_params=params(),
            cost_estimate=pl.CostEstimate(flops=int(us * 0.45e9), bytes_accessed=0, transcendentals=0),
            name=name,
        )(*arrays, *extra)
        self.tokens = [token]
        return results


def lanes_of(rows):
    return lax.broadcasted_iota(jnp.int32, (rows, LANES), 1)


def swap_halves(block):
    return pltpu.roll(block, HEAD_SIZE, 1)


def in_three(value):
    high = value.astype(BF16).astype(F32)
    rest = value - high
    middle = rest.astype(BF16).astype(F32)
    return high, middle, rest - middle


def at_lanes(lane, first, parts, base):
    for place, part in enumerate(parts):
        base = jnp.where(lane == first + place, part, base)
    return base


def triangle(rows, lower):
    down = lax.broadcasted_iota(jnp.int32, (rows, rows), 0)
    across = lax.broadcasted_iota(jnp.int32, (rows, rows), 1)
    return jnp.where(down >= across if lower else down <= across, 1.0, 0.0).astype(BF16)


def running_sum(tri, column, lane):
    spread = at_lanes(lane, 0, in_three(column), jnp.zeros(lane.shape, F32))
    sums = dot(tri, spread.astype(BF16))
    return sums[:, 0:1] + sums[:, 1:2] + sums[:, 2:3]


def forget_column(tail_block):
    return tail_block[:, 64:65] + tail_block[:, 65:66] + tail_block[:, 66:67]


def per_head(low, values):
    first = jnp.sum(jnp.where(low, values, 0.0), axis=-1, keepdims=True)
    second = jnp.sum(jnp.where(low, 0.0, values), axis=-1, keepdims=True)
    return jnp.where(low, first, second) * (1.0 / HEAD_SIZE)


def rms_factor(values):
    return lax.rsqrt(jnp.mean(values * values, axis=-1, keepdims=True) + EPSILON)


def merge_pair(low, first, second):
    return jnp.where(low, first, swap_halves(second))


def merge_swapped(low, first, second):
    return jnp.where(low, swap_halves(first), second)


def unpack_rows(low_half, first, second):
    strip = low_half.shape[0]
    rows = []
    for at in range(0, first.shape[0], strip):
        one, two = first[at : at + strip], second[at : at + strip]
        rows.append(jnp.where(low_half, one, swap_halves(two)))
        rows.append(jnp.where(low_half, swap_halves(one), two))
    return jnp.concatenate(rows, axis=0)


def pack_rows(low_half, block):
    strip = low_half.shape[0]
    first, second = [], []
    for at in range(0, block.shape[0], 2 * strip):
        top, bottom = block[at : at + strip], block[at + strip : at + 2 * strip]
        first.append(jnp.where(low_half, top, swap_halves(bottom)))
        second.append(jnp.where(low_half, swap_halves(top), bottom))
    return jnp.concatenate(first, axis=0), jnp.concatenate(second, axis=0)


def project_kernel(
    heads, idle, x_ref, w_ref, bias_ref, gain_ref, gq_ref, gk_ref, a_ref, raw_ref, gl_ref, pay_ref
):
    x = x_ref[...].astype(F32)
    rows = x.shape[0]
    cols = gl_ref.shape[1]
    a = (x * rms_factor(x) * gain_ref[...]).astype(BF16)
    a_ref[...] = a
    proj = dot(a, w_ref[...])
    raw_ref[...] = proj[:, : 2 * cols]
    gl_ref[...] = proj[:, 3 * cols : 4 * cols]
    logit = proj[:, 4 * cols :] + bias_ref[...]
    lane = lanes_of(rows)
    low = lane < HEAD_SIZE
    for group in range(cols // LANES):
        at = group * LANES
        query = proj[:, at : at + LANES]
        key = proj[:, cols + at : cols + at + LANES]
        value = proj[:, 2 * cols + at : 2 * cols + at + LANES]
        query = query * lax.rsqrt(per_head(low, query * query) + EPSILON) * gq_ref[...]
        key = key * lax.rsqrt(per_head(low, key * key) + EPSILON) * gk_ref[...]
        for half in range(2):
            head = 2 * group + half
            if head >= heads:
                continue
            zl = at_lanes(lane, 64, in_three(logit[:, head : head + 1]), jnp.zeros(lane.shape, F32))
            if half == 0:
                both = merge_pair(low, query, key)
                rest = jnp.where(low, value, zl)
            else:
                both = merge_swapped(low, query, key)
                rest = jnp.where(low, swap_halves(value), zl)
            pair = pl.program_id(0) * heads + head
            owner, place = lax.rem(pair, pay_ref.shape[0]), lax.div(pair, pay_ref.shape[0])
            pay_ref[owner, place, :, :LANES] = both.astype(BF16)
            pay_ref[owner, place, :, LANES:] = rest.astype(BF16)

    @pl.when(pl.program_id(0) == 0)
    def _():
        for pair in idle:
            owner, place = pair % pay_ref.shape[0], pair // pay_ref.shape[0]
            pay_ref[owner, place] = jnp.zeros(pay_ref.shape[2:], BF16)


def project(order, heads, cols, owners, x, weights, bias_row, gain_row, gq_row, gk_row, micros, after):
    total, width = x.shape
    rows = total // micros
    wide = weights.shape[1]
    whole = lambda m: (0, 0)
    part = lambda m: (m, 0)
    row = pl.BlockSpec((1, LANES), whole)
    pairs = -(-micros * heads // owners)
    idle = range(micros * heads, pairs * owners)
    sent = (owners, pairs, rows, 2 * LANES)
    return order.call(
        functools.partial(project_kernel, heads, idle),
        "project",
        (micros,),
        [
            (x, pl.BlockSpec((rows, width), part)),
            (weights, pl.BlockSpec((width, wide), whole)),
            (bias_row, row),
            (gain_row, pl.BlockSpec((1, width), whole)),
            (gq_row, row),
            (gk_row, row),
        ],
        [
            ((total, width), BF16, pl.BlockSpec((rows, width), part)),
            ((total, 2 * cols), F32, pl.BlockSpec((rows, 2 * cols), part)),
            ((total, cols), F32, pl.BlockSpec((rows, cols), part)),
            (sent, BF16, pl.BlockSpec(sent, lambda m: (0, 0, 0, 0))),
        ],
        13,
        after=after,
    )


def attend_kernel(size, pay_ref, tk_ref, tv_ref, ap_ref, af_ref, q_ref, k_ref, v_ref):
    blocks, _, rows, _ = pay_ref.shape
    length = blocks * rows
    lane = lanes_of(rows)
    low = lane < HEAD_SIZE
    tri = triangle(rows, True)
    zero = jnp.zeros(lane.shape, F32)

    def build(b, carry):
        at = pl.ds(pl.multiple_of(b * rows, rows), rows)
        both = pay_ref[b, 0, :, :LANES].astype(F32)
        rest = pay_ref[b, 0, :, LANES:].astype(F32)
        logit = forget_column(rest)
        log_forget = jnp.minimum(logit, 0.0) - jnp.log1p(jnp.exp(-jnp.abs(logit)))
        decay = running_sum(tri, log_forget, lane) + carry
        high, middle, least = in_three(decay)
        query_side = at_lanes(lane, 64, (high, middle, least, 1.0, 1.0, 1.0), zero)
        key_side = at_lanes(lane, 64, (1.0, 1.0, 1.0, -high, -middle, -least), zero)
        value_side = at_lanes(lane, 64, (1.0, 1.0, 1.0), zero)
        q_ref[0, at, :] = jnp.where(low, both * SCALE, query_side).astype(BF16)
        k_ref[0, at, :] = jnp.where(low, swap_halves(both), key_side).astype(BF16)
        v_ref[0, at, :] = jnp.where(low, rest, value_side).astype(BF16)
        return decay[rows - 1 :, :]

    lax.fori_loop(0, blocks, build, jnp.zeros((1, 1), F32))

    tail_length = tk_ref.shape[1]
    visible = lax.broadcasted_iota(jnp.int32, (size, size), 0) >= lax.broadcasted_iota(
        jnp.int32, (size, size), 1
    )
    half_low = lanes_of(STRIP) < HEAD_SIZE
    lane_here = lanes_of(size)

    def one_block(qi, carry):
        at = pl.ds(pl.multiple_of(qi * size, size), size)
        query = q_ref[0, at, :]

        def absorb(key, value, total, masked=False):
            scores = dot(query, key, NT)
            if masked:
                scores = jnp.where(visible, scores, HIDE)
            return total + dot(jnp.exp(scores).astype(BF16), value)

        total = jnp.zeros((size, LANES), F32)
        for t in range(tail_length // size):
            here = pl.ds(t * size, size)
            total = absorb(tk_ref[0, here, :], tv_ref[0, here, :], total)

        def earlier(ki, total):
            here = pl.ds(pl.multiple_of(ki * size, size), size)
            return absorb(k_ref[0, here, :], v_ref[0, here, :], total)

        total = lax.fori_loop(0, qi, earlier, total)
        total = absorb(k_ref[0, at, :], v_ref[0, at, :], total, True)
        weight = total[:, 64:65]
        mixture = total / weight
        af_ref[0, at, :] = mixture
        for piece in range(size // rows):
            block = mixture[piece * rows : (piece + 1) * rows]
            packed, _ = pack_rows(half_low, block)
            ap_ref[qi * (size // rows) + piece, 0] = packed.astype(BF16)
        old = query.astype(F32)
        shifted = forget_column(old) - jnp.log(weight)
        q_ref[0, at, :] = at_lanes(lane_here, 64, in_three(shifted), old).astype(BF16)
        return carry

    lax.fori_loop(0, length // size, one_block, 0)


def attend(order, pay, tail_key, tail_value):
    blocks, pairs, rows, _ = pay.shape
    length = blocks * rows
    tail_length = tail_key.shape[1]
    size = min(512, length)
    pair = lambda j: (j, 0, 0)
    across = lambda j: (0, j, 0, 0)
    tail = pl.BlockSpec((1, tail_length, LANES), pair)
    whole = pl.BlockSpec((1, length, LANES), pair)
    return order.call(
        functools.partial(attend_kernel, size),
        "attend",
        (pairs,),
        [
            (pay, pl.BlockSpec((blocks, 1, rows, 2 * LANES), across)),
            (tail_key, tail),
            (tail_value, tail),
        ],
        [
            (
                (blocks, pairs, rows // 2, LANES),
                BF16,
                pl.BlockSpec((blocks, 1, rows // 2, LANES), across),
            ),
            ((pairs, length, LANES), F32, whole),
            ((pairs, length, LANES), BF16, whole),
            ((pairs, length, LANES), BF16, whole),
            ((pairs, length, LANES), BF16, whole),
        ],
        17 * pairs,
    )


def attend_back_kernel(
    size,
    q_ref,
    k_ref,
    v_ref,
    tk_ref,
    tv_ref,
    af_ref,
    dap_ref,
    rest_ref,
    g_ref,
    da_ref,
    dqt_ref,
    sums_ref,
):
    blocks, _, rows, _ = rest_ref.shape
    length = blocks * rows
    lane = lanes_of(rows)
    low = lane < HEAD_SIZE
    zero = jnp.zeros(lane.shape, F32)

    def build(b, carry):
        at = pl.ds(pl.multiple_of(b * rows, rows), rows)
        packed = dap_ref[b, 0].astype(F32)
        strips = []
        for strip in range(0, packed.shape[0], STRIP):
            strips += [packed[strip : strip + STRIP], swap_halves(packed[strip : strip + STRIP])]
        grad = jnp.where(low, jnp.concatenate(strips, axis=0), 0.0)
        delta = jnp.sum(grad * af_ref[0, at, :], axis=-1, keepdims=True)
        da_ref[at, :] = at_lanes(lane, 64, in_three(-delta), grad).astype(BF16)
        return carry

    lax.fori_loop(0, blocks, build, 0)

    across = lax.broadcasted_iota(jnp.int32, (size, size), 1)
    down = lax.broadcasted_iota(jnp.int32, (size, size), 0)
    visible = across >= down
    count = length // size

    def block_at(i):
        return pl.ds(pl.multiple_of(i * size, size), size)

    def pieces(key, value, at, masked=False):
        scores = dot(key, q_ref[0, at, :], NT)
        if masked:
            scores = jnp.where(visible, scores, HIDE)
        prob = jnp.exp(scores)
        score_grad = prob * dot(value, da_ref[at, :], NT)
        return prob.astype(BF16), score_grad.astype(BF16)

    tail_length = tk_ref.shape[1]
    tail_count = tail_length // size

    def tail_block(qi, carry):
        at = block_at(qi)
        total = jnp.zeros((LANES, size), F32)
        for t in range(tail_count):
            key = tk_ref[0, pl.ds(t * size, size), :]
            _, score_grad = pieces(key, tv_ref[0, pl.ds(t * size, size), :], at)
            total = total + dot(key.T, score_grad)
        dqt_ref[:, at] = total
        return carry

    lax.fori_loop(0, count, tail_block, 0)
    lane_here = lanes_of(size)
    low_here = lane_here < HEAD_SIZE

    def key_block(ki, carry):
        own = block_at(ki)
        key = k_ref[0, own, :]
        value = v_ref[0, own, :]
        key_turned = key.T

        def one(at, sums, masked=False):
            key_sum, value_sum = sums
            prob, score_grad = pieces(key, value, at, masked)
            dqt_ref[:, at] += dot(key_turned, score_grad)
            return (
                key_sum + dot(score_grad, q_ref[0, at, :]),
                value_sum + dot(prob, da_ref[at, :]),
            )

        start = (jnp.zeros((size, LANES), F32), jnp.zeros((size, LANES), F32))
        sums = one(own, start, True)
        key_sum, value_sum = lax.fori_loop(
            ki + 1, count, lambda qi, sums: one(block_at(qi), sums), sums
        )
        sums_ref[own, :] = key_sum
        for piece in range(size // rows):
            here = slice(piece * rows, (piece + 1) * rows)
            g_ref[ki * (size // rows) + piece, 0, :, LANES:] = value_sum[here].astype(BF16)
        return carry

    lax.fori_loop(0, count, key_block, 0)

    tri = triangle(rows, False)

    def finish(i, carry):
        b = blocks - 1 - i
        at = pl.ds(pl.multiple_of(b * rows, rows), rows)
        query = dqt_ref[:, at].T
        key = sums_ref[at, :]
        decay_grad = query[:, 64:65] - key[:, 67:68]
        suffix = running_sum(tri, decay_grad, lane) + carry
        logit = forget_column(rest_ref[b, 0].astype(F32))
        forget_grad = suffix / (1.0 + jnp.exp(logit))
        both = jnp.where(low, query * SCALE, swap_halves(key))
        rest = jnp.where(low, g_ref[b, 0, :, LANES:].astype(F32), jnp.where(lane == 64, forget_grad, 0.0))
        g_ref[b, 0, :, :LANES] = both.astype(BF16)
        g_ref[b, 0, :, LANES:] = rest.astype(BF16)
        return suffix[0:1, :]

    lax.fori_loop(0, blocks, finish, jnp.zeros((1, 1), F32))


def attend_back(order, saved, tail_key, tail_value, mixture, packed_grad, pay, place, grad_place):
    blocks, _, rows, _ = pay.shape
    length = blocks * rows
    tail_length = tail_key.shape[1]
    size = min(512, length)
    pair = lambda j: (place, 0, 0)
    tail = pl.BlockSpec((1, tail_length, LANES), pair)
    whole = pl.BlockSpec((1, length, LANES), pair)
    grad = pl.BlockSpec((blocks, 1, rows // 2, LANES), lambda j: (0, grad_place, 0, 0))
    sent = (blocks, 1, rows, 2 * LANES)
    return order.call(
        functools.partial(attend_back_kernel, size),
        "attend_back",
        (1,),
        [(array, whole) for array in saved]
        + [
            (tail_key, tail),
            (tail_value, tail),
            (mixture, whole),
            (packed_grad, grad),
            (pay, pl.BlockSpec((blocks, 1, rows, LANES), lambda j: (0, place, 0, 1))),
        ],
        [(sent, BF16, pl.BlockSpec(sent, lambda j: (0, 0, 0, 0)))],
        22,
        scratch=[
            pltpu.VMEM((length, LANES), BF16),
            pltpu.VMEM((LANES, length), F32),
            pltpu.VMEM((length, LANES), F32),
        ],
    )[0]


def group_of(heads, ref, first_pair, group, low_half):
    owners = ref.shape[0]

    def packed(head):
        if head >= heads:
            return jnp.zeros(ref.shape[2:], F32)
        pair = first_pair + head
        if isinstance(pair, int):
            return ref[pair % owners, pair // owners].astype(F32)
        return ref[lax.rem(pair, owners), lax.div(pair, owners)].astype(F32)

    return unpack_rows(low_half, packed(2 * group), packed(2 * group + 1))


def gate_kernel(heads, first, ap_ref, gl_ref, o_ref, sent_ref):
    rows, cols = o_ref.shape
    half_low = lanes_of(STRIP) < HEAD_SIZE
    pair = (first + pl.program_id(0)) * heads
    for group in range(cols // LANES):
        at = slice(group * LANES, (group + 1) * LANES)
        mixture = group_of(heads, ap_ref, pair, group, half_low)
        gated = (mixture * jax.nn.sigmoid(gl_ref[:, at])).astype(BF16)
        o_ref[:, at] = gated
        for z in range(sent_ref.shape[0]):
            sent_ref[z, :, at] = gated


def gate(order, heads, packed, gl, rows, first, count, copies, before):
    total, cols = gl.shape
    here = pl.BlockSpec((rows, cols), lambda i: (first + i, 0))
    return order.call(
        functools.partial(gate_kernel, heads, first),
        "gate",
        (count,),
        [(packed, pl.BlockSpec(packed.shape, lambda i: (0, 0, 0, 0))), (gl, here)],
        [
            ((total, cols), BF16, here),
            (
                (copies, count * rows, cols),
                BF16,
                pl.BlockSpec((copies, rows, cols), lambda i: (0, i, 0)),
            ),
        ],
        2 * count,
        before=before,
    )


def pack_kernel(*refs):
    out_ref, at = refs[-1], 0
    for ref in refs[:-1]:
        wide = ref.shape[1]
        out_ref[:, at : at + wide] = ref[...]
        at += wide


def pack(order, arrays):
    rows = arrays[0].shape[0]
    wide = sum(array.shape[1] for array in arrays)
    whole = lambda i: (0, 0)
    return order.call(
        pack_kernel,
        "pack",
        (1,),
        [(array, pl.BlockSpec(array.shape, whole)) for array in arrays],
        [((rows, wide), BF16, pl.BlockSpec((rows, wide), whole))],
        2,
    )[0]


def feed_kernel(
    parts,
    own,
    rank_ref,
    x_ref,
    dy_ref,
    wo_ref,
    wg_ref,
    wu_ref,
    wd_ref,
    wg_far_ref,
    wu_far_ref,
    wd_far_ref,
    gain_ref,
    *refs,
):
    o_ref, c_ref, u_ref, dgu_ref, hid_ref, out_ref, dc_ref, out_acc, dc_acc = refs
    step = pl.program_id(0)
    last = pl.num_programs(0) - 1

    def attended():
        return dot(o_ref[0], wo_ref[...], NT)

    @pl.when(step == 0)
    def _():
        hid_ref[...] = x_ref[...].astype(F32) + attended()

    @pl.when((step > 0) & (step < parts))
    def _():
        hid_ref[...] += attended()

    @pl.when(step == parts - 1)
    def _():
        hidden = hid_ref[...]
        c_ref[...] = (hidden * rms_factor(hidden) * gain_ref[...]).astype(BF16)
        out_acc[...] = jnp.zeros_like(out_acc)
        dc_acc[...] = jnp.zeros_like(dc_acc)

    def chunk(w_gate, w_up, w_down):
        c = c_ref[...]
        gr = dot(c, w_gate[...])
        ur = dot(c, w_up[...])
        sig = jax.nn.sigmoid(gr)
        silu = gr * sig
        u = (silu * ur).astype(BF16)
        du = dot(dy_ref[...], w_down[...])
        dgr = (du * ur * sig * (1.0 + gr * (1.0 - sig))).astype(BF16)
        dur = (du * silu).astype(BF16)
        out_acc[...] += dot(u, w_down[...], NT)
        dc_acc[...] += dot(dgr, w_gate[...], NT) + dot(dur, w_up[...], NT)
        return u, dgr, dur

    @pl.when((step >= parts) & (step < parts + own))
    def _():
        u, dgr, dur = chunk(wg_ref, wu_ref, wd_ref)
        wide = u.shape[1]
        u_ref[...] = u
        dgu_ref[:, :wide] = dgr
        dgu_ref[:, wide:] = dur

    @pl.when(step >= parts + own)
    def _():
        chunk(wg_far_ref, wu_far_ref, wd_far_ref)

    @pl.when(step == last)
    def _():
        out_ref[...] = out_acc[...].astype(BF16)
        dc_ref[...] = dc_acc[...].astype(BF16)


def feed(order, rank, x, dy, o_all, near, far, gain_row, ff, chunk, group, before):
    parts, rows, cols = o_all.shape
    total, width = x.shape
    own = ff // chunk
    offset = parts * cols // chunk
    others = (far.shape[1] - parts * cols) // (3 * ff)
    steps = parts + (1 + others) * own
    whole = lambda i, rank: (0, 0)
    here = lambda i, rank: (group, 0)
    early = lambda i: jnp.minimum(i, parts - 1)
    mine = lambda i: jnp.clip(i - parts, 0, own - 1)

    def near_strip(k):
        return pl.BlockSpec((width, chunk), lambda i, rank: (0, k * own + mine(i)))

    def far_strip(k):
        def place(i, rank):
            s = jnp.maximum(i - parts - own, 0)
            return (0, offset + (s // own * 3 + k) * own + s % own)

        return pl.BlockSpec((width, chunk), place)

    wide = pl.BlockSpec((rows, width), whole)
    return order.call(
        functools.partial(feed_kernel, parts, own),
        "feed",
        (steps,),
        [
            (x, pl.BlockSpec((rows, width), here)),
            (dy, pl.BlockSpec((rows, width), here)),
            (far, pl.BlockSpec((width, cols), lambda i, rank: (0, early(i)))),
            (near, near_strip(0)),
            (near, near_strip(1)),
            (near, near_strip(2)),
            (far, far_strip(0)),
            (far, far_strip(1)),
            (far, far_strip(2)),
            (gain_row, pl.BlockSpec((1, width), whole)),
        ]
        + [(o_all, pl.BlockSpec((1, rows, cols), lambda i, rank: (rank[0] ^ early(i), 0, 0)))],
        [
            ((total, width), BF16, pl.BlockSpec((rows, width), here)),
            ((total, ff), BF16, pl.BlockSpec((rows, chunk), lambda i, rank: (group, mine(i)))),
            (
                (total, 2 * ff),
                BF16,
                pl.BlockSpec((rows, 2 * chunk), lambda i, rank: (group, mine(i))),
            ),
            ((rows, width), F32, wide),
            ((rows, width), BF16, wide),
            ((rows, width), BF16, wide),
        ],
        37,
        scratch=[pltpu.VMEM((rows, width), F32), pltpu.VMEM((rows, width), F32)],
        before=before,
        scalars=(rank,),
    )


def norm_back(source, factor, gain_row, upstream):
    scaled = upstream * gain_row
    inner = jnp.mean(scaled * source, axis=-1, keepdims=True)
    return factor * scaled - source * (factor * factor * factor) * inner


def hidden_back_kernel(
    heads,
    pair,
    dc_ref,
    dc_other_ref,
    hid_ref,
    dy_ref,
    gain_ref,
    w_ref,
    gl_ref,
    ap_ref,
    dhb_ref,
    dgl_ref,
    dh_ref,
    dap_ref,
    dg_ref,
):
    rows, cols = gl_ref.shape
    hidden = hid_ref[...]
    factor = rms_factor(hidden)
    dc = dc_ref[...].astype(F32) + dc_other_ref[...].astype(F32)
    dh = dy_ref[...].astype(F32) + norm_back(hidden, factor, gain_ref[...], dc)
    dg_ref[0] = jnp.sum(dc * hidden * factor, axis=0, keepdims=True)
    dh_ref[...] = dh
    dhb = dh.astype(BF16)
    dhb_ref[...] = dhb
    gated_grad = dot(dhb, w_ref[...])
    half_low = lanes_of(STRIP) < HEAD_SIZE
    for group in range(cols // LANES):
        at = slice(group * LANES, (group + 1) * LANES)
        mixture = group_of(heads, ap_ref, pair, group, half_low)
        gate_value = jax.nn.sigmoid(gl_ref[:, at])
        grad = gated_grad[:, at]
        dgl_ref[:, at] = (grad * mixture * gate_value * (1.0 - gate_value)).astype(BF16)
        first, second = pack_rows(half_low, grad * gate_value)
        dap_ref[2 * group] = first.astype(BF16)
        if 2 * group + 1 < heads:
            dap_ref[2 * group + 1] = second.astype(BF16)


def hidden_back(order, heads, dc, dc_other, hidden, dy, gain_row, weights, gl, packed, rows, micro, place, before):
    total, cols = gl.shape
    width = dc.shape[1]
    half = rows // 2
    whole = lambda i: (0, 0)
    here = lambda i: (2 * micro + i, 0)
    part = pl.BlockSpec((half, width), lambda i: (2 * place + i, 0))
    strips = pl.BlockSpec((heads, half // 2, LANES), lambda i: (0, i, 0))
    return order.call(
        functools.partial(hidden_back_kernel, heads, micro * heads),
        "hidden_back",
        (2,),
        [
            (dc, part),
            (dc_other, part),
            (hidden, part),
            (dy, pl.BlockSpec((half, width), here)),
            (gain_row, pl.BlockSpec((1, width), whole)),
            (weights, pl.BlockSpec((width, cols), whole)),
            (gl, pl.BlockSpec((half, cols), here)),
            (packed, pl.BlockSpec(packed.shape[:2] + (half // 2, LANES), lambda i: (0, 0, i, 0))),
        ],
        [
            ((total, width), BF16, pl.BlockSpec((half, width), here)),
            ((total, cols), BF16, pl.BlockSpec((half, cols), here)),
            ((rows, width), F32, pl.BlockSpec((half, width), lambda i: (i, 0))),
            ((heads, half, LANES), BF16, strips),
            ((2, 1, width), F32, pl.BlockSpec((1, 1, width), lambda i: (i, 0, 0))),
        ],
        4,
        before=before,
    )


def project_back_kernel(
    heads,
    upper_ref,
    g_ref,
    raw_ref,
    x_ref,
    dgl_ref,
    w_ref,
    gq_ref,
    gk_ref,
    grads_ref,
    *refs,
):
    *da_refs, sums_ref, all_ref = refs
    rows, cols = dgl_ref.shape
    width = x_ref.shape[1]
    lane = lanes_of(rows)
    low = lane < HEAD_SIZE
    zero = jnp.zeros(lane.shape, F32)
    sums = [jnp.zeros((1, LANES), F32), jnp.zeros((1, LANES), F32)]

    def head_back(raw, upstream, gain_row, which):
        factor = lax.rsqrt(per_head(low, raw * raw) + EPSILON)
        scaled = upstream * gain_row
        inner = per_head(low, scaled * raw)
        sums[which] += jnp.sum(upstream * raw * factor, axis=0, keepdims=True)
        return factor * scaled - raw * (factor * factor * factor) * inner

    forget = zero
    for group in range(cols // LANES):
        at = group * LANES
        here = slice(at, at + LANES)
        pair = (2 * group, 2 * group + 1)
        both = [g_ref[h, :, :LANES].astype(F32) if h < heads else zero for h in pair]
        rest = [g_ref[h, :, LANES:].astype(F32) if h < heads else zero for h in pair]
        query = head_back(raw_ref[:, here], merge_pair(low, *both), gq_ref[...], 0)
        key = head_back(
            raw_ref[:, cols + at : cols + at + LANES],
            merge_swapped(low, *both),
            gk_ref[...],
            1,
        )
        all_ref[:, here] = query.astype(BF16)
        all_ref[:, cols + at : cols + at + LANES] = key.astype(BF16)
        value = merge_pair(low, *rest)
        all_ref[:, 2 * cols + at : 2 * cols + at + LANES] = value.astype(BF16)
        for h, block in zip(pair, rest):
            if h < heads:
                forget = jnp.where(lane == h, block[:, 64:65], forget)
    all_ref[:, 3 * cols : 4 * cols] = dgl_ref[...]
    all_ref[:, 4 * cols :] = forget.astype(BF16)
    grads_ref[:, : 3 * cols] = all_ref[:, : 3 * cols]
    grads_ref[:, 3 * cols :] = all_ref[:, 4 * cols :]
    da = dot(all_ref[...], w_ref[...], NT)
    if len(da_refs) == 1:
        da_refs[0][...] = da.astype(BF16)
    else:
        is_kept = pl.program_id(0) == upper_ref[0]
        for ref, chosen in zip(da_refs, (is_kept, jnp.logical_not(is_kept))):

            @pl.when(chosen)
            def _(ref=ref):
                ref[...] = da.astype(BF16)

    x = x_ref[...].astype(F32)
    sums_ref[0, :, :width] = jnp.sum(da * x * rms_factor(x), axis=0, keepdims=True)
    sums_ref[0, :, width : width + LANES] = sums[0]
    sums_ref[0, :, width + LANES : width + 2 * LANES] = sums[1]
    sums_ref[0, :, width + 2 * LANES :] = jnp.sum(forget, axis=0, keepdims=True)


def project_back(order, heads, upper, returned, raw, x, dgl, weights, gq_row, gk_row, rows, micro, halves, before, after):
    total, cols = dgl.shape
    width, wide = weights.shape
    half = rows // 2
    whole = lambda i, upper: (0, 0)
    here = lambda i, upper: (2 * micro + i, 0)
    row = pl.BlockSpec((1, LANES), whole)
    sums = width + 3 * LANES
    if halves:
        da = [((half, width), BF16, pl.BlockSpec((half, width), whole))] * 2
    else:
        da = [((rows, width), BF16, pl.BlockSpec((half, width), lambda i, upper: (i, 0)))]
    return order.call(
        functools.partial(project_back_kernel, heads),
        "project_back",
        (2,),
        [
            (returned, pl.BlockSpec((heads, half, 2 * LANES), lambda i, upper: (0, i, 0))),
            (raw, pl.BlockSpec((half, 2 * cols), here)),
            (x, pl.BlockSpec((half, width), here)),
            (dgl, pl.BlockSpec((half, cols), here)),
            (weights, pl.BlockSpec((width, wide), whole)),
            (gq_row, row),
            (gk_row, row),
        ],
        [((total, wide - cols), BF16, pl.BlockSpec((half, wide - cols), here))]
        + da
        + [((2, 1, sums), F32, pl.BlockSpec((1, 1, sums), lambda i, upper: (i, 0, 0)))],
        6,
        scratch=[pltpu.VMEM((half, wide), BF16)],
        before=before,
        scalars=(upper,),
        after=after,
    )


def input_back_kernel(rank_ref, x_ref, dh_ref, gain_ref, own_ref, *refs):
    *passed, out_ref = refs
    rank, count = rank_ref[0], len(passed) + 1
    da = own_ref[...].astype(F32)
    for t, ref in enumerate(passed):
        taken = jnp.where(pl.program_id(0) == 0, rank == t + 1, rank == count - 2 - t)
        da = jnp.where(taken, ref[...].astype(F32), da)
    x = x_ref[...].astype(F32)
    out_ref[...] = dh_ref[...] + norm_back(x, rms_factor(x), gain_ref[...], da)


def input_back(order, rank, summed, x, dh, gain_row, micro, before):
    total, width = x.shape
    rows = dh.shape[0]
    half = rows // 2
    here = pl.BlockSpec((half, width), lambda i, rank: (2 * micro + i, 0))
    one = pl.BlockSpec((half, width), lambda i, rank: (i, 0))
    passing = pl.BlockSpec((half, width), lambda i, rank: (0, 0))
    return order.call(
        input_back_kernel,
        "input_back",
        (2,),
        [(x, here), (dh, one), (gain_row, pl.BlockSpec((1, width), lambda i, rank: (0, 0)))]
        + [(block, one if len(summed) == 1 else passing) for block in summed],
        [((total, width), F32, here)],
        4,
        before=before,
        scalars=(rank,),
    )


def layer_out_kernel(hid_ref, part_ref, other_ref, out_ref):
    total = hid_ref[...] + (part_ref[...].astype(F32) + other_ref[...].astype(F32))
    out_ref[...] = total.astype(BF16)


def layer_output(order, hidden, part, other, group, total, before):
    rows, width = hidden.shape
    tiles = 4
    tile = rows // tiles
    one = pl.BlockSpec((tile, width), lambda i: (i, 0))
    return order.call(
        layer_out_kernel,
        "layer_out",
        (tiles,),
        [(hidden, one), (part, one), (other, one)],
        [((total, width), BF16, pl.BlockSpec((tile, width), lambda i: (tiles * group + i, 0)))],
        4,
        before=before,
    )


def pad_to(array, size, axis):
    missing = size - array.shape[axis]
    if missing == 0:
        return array
    widths = [(0, missing if i == axis else 0) for i in range(array.ndim)]
    return jnp.pad(array, widths)


def turned_kernel(*refs):
    out_ref, at = refs[-1], 0
    for left_ref, right_ref in zip(refs[:-1:2], refs[1:-1:2]):
        wide = right_ref.shape[1]
        product = lax.dot_general(
            left_ref[...], right_ref[...], (((0,), (0,)), ((), ())), preferred_element_type=F32
        )
        out_ref[:, at : at + wide] = product.astype(BF16)
        at += wide


def turned_products(order, pairs, us):
    height = pairs[0][0].shape[1]
    tile = 256
    ins, wide = [], 0
    for left, right in pairs:
        ins.append((left, pl.BlockSpec((left.shape[0], tile), lambda i: (0, i))))
        ins.append((right, pl.BlockSpec(right.shape, lambda i: (0, 0))))
        wide += right.shape[1]
    return order.call(
        turned_kernel,
        "turned_products",
        (height // tile,),
        ins,
        [((height, wide), BF16, pl.BlockSpec((tile, wide), lambda i: (i, 0)))],
        us,
    )[0]


def line_steps(count):
    return [((t - 1, t), (count - t, count - 1 - t)) for t in range(1, count)]


def line_sum(kept, sent, axis):
    count = lax.axis_size(axis)
    steps = line_steps(count)
    moving = sent
    for t, hops in enumerate(steps):
        arrived = lax.ppermute(moving, axis, hops)
        moving = arrived + (sent if t + 2 <= count // 2 else kept)
    passed = [moving]
    for hops in steps:
        passed.append(lax.ppermute(passed[-1], axis, hops))
    return passed


def exchanged(array, axis, flip):
    count = lax.axis_size(axis)
    return lax.ppermute(array, axis, [(i, i ^ flip) for i in range(count)])


def to_all(array, axis):
    return lax.all_to_all(array, axis, 0, 0, tiled=True)


def small_sum(row):
    for axis in ("seq", "head"):
        flip = 1
        while flip < lax.axis_size(axis):
            row = row + exchanged(row, axis, flip)
            flip *= 2
    return row


def shards(
    inputs,
    cotangent,
    tail_keys,
    tail_values,
    tail_forget,
    gain_one,
    gain_two,
    w_query,
    w_key,
    w_value,
    w_forget,
    forget_bias,
    query_gain,
    key_gain,
    w_outgate,
    w_out,
    w_gate,
    w_up,
    w_down,
):
    micros, rows, width = inputs.shape
    total = micros * rows
    own_cols = w_query.shape[1]
    heads = w_forget.shape[1]
    ff = w_gate.shape[1]
    seq_count = lax.axis_size("seq")
    head_count = lax.axis_size("head")
    seq_rank = lax.axis_index("seq")
    head_rank = lax.axis_index("head")
    cols = -(-own_cols // LANES) * LANES
    pair_total = micros * heads
    pairs = -(-pair_total // seq_count)
    padded_pairs = pairs * seq_count
    tail_length = tail_keys.shape[1]

    x = inputs.reshape(total, width)
    dy = cotangent.reshape(total, width)

    small = jnp.concatenate([w_forget, gain_one[:, None], gain_two[:, None]], axis=1)
    first_shard = jnp.concatenate(
        [pad_to(w, cols, 1) for w in (w_query, w_key, w_value, w_outgate)]
        + [pad_to(small, LANES, 1)],
        axis=1,
    )
    first = lax.all_gather(first_shard, "seq", axis=0, tiled=True)
    near_shard = jnp.concatenate([w_gate, w_up, w_down.T], axis=1)
    near = lax.all_gather(near_shard, "seq", axis=0, tiled=True)
    split = 3 * ff // 2
    outs, units, early = [pad_to(w_out.T, cols, 1)], [(near_shard[:, :split], near_shard[:, split:])], []
    flip = 1
    while flip < head_count:
        outs.append(exchanged(jnp.concatenate(outs, axis=1), "head", flip))
        early.append(outs[-1])
        if flip > 1:
            units += [tuple(exchanged(part, "head", flip) for part in unit) for unit in units]
            early += [first_part for first_part, _ in units[len(units) // 2 :]]
        flip *= 2
    far_parts = outs + [part for unit in units[1:] for part in unit]
    rank = head_rank.astype(jnp.int32)[None]
    upper = (rank >= head_count // 2).astype(jnp.int32)
    order = Order()
    gain_one_row = first[:, 4 * cols + heads].astype(F32)[None, :]
    gain_two_row = first[:, 4 * cols + heads + 1].astype(F32)[None, :]
    bias_here = lax.dynamic_slice_in_dim(forget_bias, head_rank * heads, heads, 0)
    bias_row = pad_to(bias_here[None, :], LANES, 1)
    gq_row = jnp.tile(query_gain.astype(F32), 2)[None, :]
    gk_row = jnp.tile(key_gain.astype(F32), 2)[None, :]

    tail_key_parts, tail_value_parts = [], []
    for j in range(pairs):
        p = jnp.minimum(j * seq_count + seq_rank, pair_total - 1)
        m, h = p // heads, p % heads
        tail_of = lambda array, wide: lax.dynamic_slice(
            array, (m, 0, h * wide), (1, tail_length, wide)
        )[0]
        forget = tail_of(tail_forget, 1)
        decay = jnp.cumsum(forget, axis=0) - jnp.sum(forget, axis=0, keepdims=True)
        high = lax.reduce_precision(decay, 8, 7)
        middle = lax.reduce_precision(decay - high, 8, 7)
        least = decay - high - middle
        ones = jnp.ones((tail_length, 3), BF16)
        parts = jnp.concatenate([-high, -middle, -least], axis=1).astype(BF16)
        tail_key_parts.append(
            pad_to(jnp.concatenate([tail_of(tail_keys, HEAD_SIZE), ones, parts], axis=1), LANES, 1)
        )
        tail_value_parts.append(
            pad_to(jnp.concatenate([tail_of(tail_values, HEAD_SIZE), ones], axis=1), LANES, 1)
        )
    tail_key, tail_value = jnp.stack(tail_key_parts), jnp.stack(tail_value_parts)

    def pairs_of(stages, first_micro, count):
        low, high = first_micro * heads, (first_micro + count) * heads
        taken = []
        for j, stage in enumerate(stages):
            start, stop = max(low - j * seq_count, 0), min(high - j * seq_count, seq_count)
            if start < stop:
                taken.append(stage[start:stop, 0])
        return jnp.concatenate(taken, axis=0)

    def stage_of(blocks, j):
        low, high = j * seq_count, min((j + 1) * seq_count, pair_total)
        taken = []
        for m in range(low // heads, (high - 1) // heads + 1):
            taken.append(blocks[m][max(low - m * heads, 0) : min(high - m * heads, heads)])
        return pad_to(jnp.concatenate(taken, axis=0), seq_count, 0)[:, None]

    def ready(stages):
        return len(stages) * seq_count // heads if len(stages) < pairs else micros

    a, raw, gl, pay = project(
        order, heads, cols, seq_count, x, first, bias_row, gain_one_row, gq_row, gk_row, micros, early
    )
    pay = to_all(pay, "seq")
    far = lax.all_gather(pack(order, far_parts), "seq", axis=0, tiled=True)
    packed, mixture, *saved = attend(order, pay, tail_key, tail_value)
    packed = to_all(packed, "seq")

    size = 2 if micros % 2 == 0 else 1
    groups = micros // size
    gated, o_alls = (), []
    for g in range(groups):
        *gated, sent = gate(order, heads, packed, gl, rows, g * size, size, head_count, gated)
        o_alls.append(to_all(sent, "head"))
    o = gated[0]

    chunk = min(512, ff)
    hiddens, out_parts, dc_parts, dc_others = [], [], [], []
    dhs, daps, gains_two = [], [], []
    fed, backed, returned_stages = (), (), []

    def back_to_heads(m):
        nonlocal backed
        g = m // size
        *backed, dh, dap, gain = hidden_back(
            order,
            heads,
            dc_parts[g],
            dc_others[g],
            hiddens[g],
            dy,
            gain_two_row,
            far,
            gl,
            packed,
            rows,
            m,
            m % size,
            backed,
        )
        dhs.append(dh)
        daps.append(dap)
        gains_two.append(gain)

    for g in range(groups):
        *fed, hidden, out_part, dc_part = feed(
            order,
            rank,
            x,
            dy,
            o_alls[g],
            near,
            far,
            gain_two_row,
            ff,
            chunk,
            g,
            fed,
        )
        hiddens.append(hidden)
        out_parts.append(out_part)
        dc_parts.append(dc_part)
        dc_others.append(exchanged(dc_part, "head", 1))
        if g > 0:
            for m in range((g - 1) * size, g * size):
                back_to_heads(m)
    c, u, dgu = fed

    def scattered(grad):
        return lax.psum_scatter(grad, "seq", scatter_dimension=0, tiled=True)

    unit_grads = scattered(turned_products(order, [(c, dgu), (dy, u)], 13))

    grads, da_sums, gains_one = (), [], []
    last_group = (groups - 1) * size
    da_group = []

    after = ()

    def back_to_input():
        nonlocal grads, da_group, after
        for m in range(len(gains_one), ready(returned_stages)):
            by_line = m >= last_group
            *out, gain = project_back(
                order,
                heads,
                upper,
                pairs_of(returned_stages, m, 1),
                raw,
                x,
                backed[1],
                first,
                gq_row,
                gk_row,
                rows,
                m,
                by_line,
                grads,
                after,
            )
            grads, da = out[:1], out[1:]
            gains_one.append(gain)
            after = ()
            if by_line:
                da_sums.append(line_sum(*da, "head"))
            else:
                da_group += da
                if len(da_group) == size:
                    total_da = lax.psum(jnp.concatenate(da_group, axis=0), "head")
                    da_sums.extend([total_da[i * rows : (i + 1) * rows]] for i in range(size))
                    da_group = []

    layer_out = ()

    def put_out(g):
        nonlocal layer_out
        other = exchanged(out_parts[g], "head", 1)
        layer_out = layer_output(order, hiddens[g], out_parts[g], other, g, total, layer_out)

    sent_grads = []
    for j in range(pairs):
        needed = (min((j + 1) * seq_count, pair_total) - 1) // heads
        if needed >= len(daps):
            for m in range(len(daps), micros):
                back_to_heads(m)
            mixed_grads = scattered(turned_products(order, [(backed[0], o), (a, backed[1])], 8))
        if j == len(sent_grads):
            here = [k for k in range(j, pairs) if (min((k + 1) * seq_count, pair_total) - 1) // heads < len(daps)]
            stages = jnp.concatenate([stage_of(daps, k) for k in here], axis=1)
            stages = to_all(stages, "seq")
            sent_grads += [(stages, k - j) for k in here]
        returned = attend_back(
            order, saved, tail_key, tail_value, mixture, sent_grads[j][0], pay, j, sent_grads[j][1]
        )
        returned_stages.append(to_all(returned, "seq"))
    put_out(0)
    after = (unit_grads,)
    last_stage = returned_stages.pop()
    back_to_input()
    for g in range(1, groups):
        put_out(g)
    returned_stages.append(last_stage)
    after = (mixed_grads,)
    back_to_input()
    head_grads = turned_products(order, [(a, grads[0])], 9)

    input_grad = ()
    for m in range(micros):
        input_grad = input_back(order, rank, da_sums[m], x, dhs[m], gain_one_row, m, input_grad)

    head_grads = head_grads.reshape(seq_count, -1, head_grads.shape[1])
    head_grads = jnp.sum(to_all(head_grads, "seq").astype(F32), axis=0)
    unit_grads, mixed_grads = unit_grads.astype(F32), mixed_grads.astype(F32)
    strips = [unit_grads[:, i * chunk : (i + 1) * chunk] for i in range(2 * ff // chunk)]
    grad_gate = jnp.concatenate(strips[0::2], axis=1)
    grad_up = jnp.concatenate(strips[1::2], axis=1)
    grad_down = unit_grads[:, 2 * ff :].T
    grad_out = mixed_grads[:, :own_cols].T

    one_sums = jnp.sum(jnp.concatenate(gains_one, axis=0), axis=0)
    two_sums = jnp.sum(jnp.concatenate(gains_two, axis=0), axis=0) * (1.0 / head_count)
    bias_full = lax.dynamic_update_slice(
        jnp.zeros((1, forget_bias.shape[0]), F32),
        one_sums[:, width + 2 * LANES : width + 2 * LANES + heads],
        (0, head_rank * heads),
    )
    sums = small_sum(jnp.concatenate([one_sums[:, : width + 2 * LANES], two_sums, bias_full], axis=1))[0]
    gq_total = sums[width : width + HEAD_SIZE] + sums[width + HEAD_SIZE : width + LANES]
    gk_total = sums[width + LANES : width + LANES + HEAD_SIZE] + sums[width + LANES + HEAD_SIZE : width + 2 * LANES]
    bias_total = sums[2 * width + 2 * LANES :]
    input_grad, layer_out = input_grad[0], layer_out[0]
    own_rows = gain_one.shape[0]
    own = lambda at: lax.dynamic_slice_in_dim(sums[at : at + width], seq_rank * own_rows, own_rows, 0)
    shape = inputs.shape
    return (
        layer_out.reshape(shape),
        input_grad.reshape(shape),
        own(0),
        own(width + 2 * LANES),
        head_grads[:, :own_cols],
        head_grads[:, cols : cols + own_cols],
        head_grads[:, 2 * cols : 2 * cols + own_cols],
        head_grads[:, 3 * cols : 3 * cols + heads],
        bias_total,
        gq_total,
        gk_total,
        mixed_grads[:, cols : cols + own_cols],
        grad_out,
        grad_gate,
        grad_up,
        grad_down,
    )


def solution(mesh):
    by_rows = P("seq", "head")
    by_cols = P("head", "seq")
    placed = (
        P(None, "seq", None),
        P(None, "seq", None),
        P(None, None, "head"),
        P(None, None, "head"),
        P(None, None, "head"),
        P("seq"),
        P("seq"),
        by_rows,
        by_rows,
        by_rows,
        by_rows,
        P(),
        P(),
        P(),
        by_rows,
        by_cols,
        by_rows,
        by_rows,
        by_cols,
    )
    return jax.shard_map(
        shards,
        mesh=mesh,
        in_specs=placed,
        out_specs=(
            P(None, "seq", None),
            P(None, "seq", None),
            P("seq"),
            P("seq"),
            by_rows,
            by_rows,
            by_rows,
            by_rows,
            P(),
            P(),
            P(),
            by_rows,
            by_cols,
            by_rows,
            by_rows,
            by_cols,
        ),
        check_vma=False,
    )
```

time: 991 us -> 777 us (0.78)
  waiting for transfers between devices: 558 us -> 242 us
  Pallas kernels: 204 us -> 324 us
  starting transfers between devices: 13.6 us -> 76.8 us
  blocking collectives: 83.2 us -> 25.5 us
  matrix products: 37.8 us -> 0 us
    psum x2 -> x1, waiting for transfers between devices: 277 us -> 0.02 us  [back_to_input(): total_da = lax.psum(jnp.concatenate(da_group, axis=0), 'head')]
    all_gather x2, waiting for transfers between devices: 121 us -> 0.01 us  [the longest x1 0.01 us: shards(): near = lax.all_gather(near_shard, 'seq', axis=0, tiled=True)]
    pallas_call x8 -> x27, Pallas kernels: 204 us -> 324 us  [call(): pl.pallas_call(linked(kernel, count, len(extra), len(outs)), grid_spec=pl...]
    ppermute x0 -> x25, waiting for transfers between devices: none -> 107 us  [the longest x13 90.7 us: exchanged(): return lax.ppermute(array, axis, [(i, i ^ flip) for i in range(count)])]
    psum x1 -> x0, blocking collectives: 46.4 us -> none  [shards(): lax.psum((jnp.concatenate([dgain_one, dgain_two], axis=0), bias_full, fol...]
    ppermute x0 -> x25, starting transfers between devices: none -> 40.8 us  [the longest x13 21.6 us: exchanged(): return lax.ppermute(array, axis, [(i, i ^ flip) for i in range(count)])]
    dot_general x5 -> x0, matrix products: 37.8 us -> none  [turned_product(): lax.dot_general(left, right, (((0,), (0,)), ((), ())), preferred_element_...]
    reduce_scatter x4 -> x2, waiting for transfers between devices: 55.5 us -> 22 us  [scattered(): return lax.psum_scatter(grad, 'seq', scatter_dimension=0, tiled=True)]
  transfers between devices with their start and end apart: 13 -> 40, of which waited for: 10 -> 17; matrix products, arithmetic and copies ran while one was open for 9% -> 8% of each run, Pallas kernels for 10% -> 37%
where the time goes in v2:
time: 777 us; the launch traced here: 766 us
  Pallas kernels  324 us (42%)
  waiting for transfers between devices  242 us (31%)
  starting transfers between devices  76.8 us (10%)
  local copies, waits for them, and re-layouts  48.9 us (6%)
  other arithmetic  32.6 us (4%)
  blocking collectives  25.5 us (3%)
  between operations  15.7 us (2%)
    pallas_call x27, Pallas kernels, call(): pl.pallas_call(linked(kernel, count, len(extra), len(outs)), grid_spec=pl...  324 us
    all_to_all x9, waiting for transfers between devices, to_all(): return lax.all_to_all(array, axis, 0, 0, tiled=True)  96.5 us
    ppermute x13, waiting for transfers between devices, exchanged(): return lax.ppermute(array, axis, [(i, i ^ flip) for i in range(count)])  90.7 us
    all_to_all x9, starting transfers between devices, to_all(): return lax.all_to_all(array, axis, 0, 0, tiled=True)  35.8 us
    all_to_all x1, blocking collectives, to_all(): return lax.all_to_all(array, axis, 0, 0, tiled=True)  25.5 us
    reduce_scatter x2, waiting for transfers between devices, scattered(): return lax.psum_scatter(grad, 'seq', scatter_dimension=0, tiled=True)  22 us
    ppermute x13, starting transfers between devices, exchanged(): return lax.ppermute(array, axis, [(i, i ^ flip) for i in range(count)])  21.6 us
    all_gather x1, waiting for transfers between devices, shards(): first = lax.all_gather(first_shard, 'seq', axis=0, tiled=True)  16.1 us
  transfers between devices with their start and end apart: 40, of which 17 were waited for; matrix products, arithmetic and copies ran while one was open for 8% of the time, Pallas kernels for 37%

profile of v2, /device:TPU:0, one launch (start us, length us, event | category | flops | bytes accessed | tf_op | source)
XLA Modules:
  0.0 765.6 jit_solution(17964009117260173602)
XLA Ops:
  22.5 14.2 %collective-permute-done.refs_6_.refs_1_ = bf16[192,384]{1,0:T(8,128)(2,1)S(1)} collective-permute-done((bf16[192,384]{1,0:T(8,128)(2,1)S(1)}, bf16[192,384]{1,0:T(8,128)(2,1)S(1)}, u32[]{:S(2)}, u32[]{:S(2)}) %collective-permute-start) | collective-permute-done | bytes 147488 | tf_op jit(solution)/shard_map/ppermute | solution.py:970
  41.5 16.1 %all-gather.4.cloned.1.call-done.refs_1_.refs_5_ = bf16[1536,1664]{1,0:T(8,128)(2,1)} async-done(((bf16[192,1664]{1,0:T(8,128)(2,1)}), bf16[1536,1664]{1,0:T(8,128)(2,1)}) %all-gather.4.cloned.1.call-update) | async-done | bytes 5111824 | tf_op jit(solution)/shard_map/all_gather | solution.py:1031
  59.9 13.1 %collective-permute-done.1.refs_7_.refs_2_ = bf16[192,768]{1,0:T(8,128)(2,1)S(1)} collective-permute-done((bf16[192,768]{1,0:T(8,128)(2,1)S(1)}, bf16[192,768]{1,0:T(8,128)(2,1)S(1)}, u32[]{:S(2)}, u32[]{:S(2)}) %collective-permute-start.1) | collective-permute-done | bytes 294944 | tf_op jit(solution)/shard_map/ppermute | solution.py:970
  73.9 14.0 %project.1 = (bf16[1024,1536]{1,0:T(8,128)(2,1)}, f32[1024,768]{1,0:T(8,128)}, f32[1024,384]{1,0:T(8,128)}, bf16[8,3,256,256]{3,2,1,0:T(8,128)(2,1)}, f32[8,128]{1,0:T(8,128)}) custom-call(bf16[1024,1536]{1,0:T(8,128)(2,1)} %bitcast.85, bf16[1536,1664]{1,0:T(8,128)(2,1)} %all-gather.4.cloned.1.call-done.refs_1_.refs_5_, f32[1,128]{1,0:T(1,128)} %pad.32.refs_2_, ...), custom_call_target="tpu_custom_call" | custom-call | flops 5849999872 | tf_op jit(solution)/shard_map/project/pallas_call | solution.py:56
  127.0 23.9 %all-to-all-done.refs_0_.refs_7_ = bf16[8,3,256,256]{3,2,1,0:T(8,128)(2,1)S(1)} async-done(((bf16[8,3,256,256]{3,2,1,0:T(8,128)(2,1)}), bf16[8,3,256,256]{3,2,1,0:T(8,128)(2,1)S(1)}, u32[]{:S(2)}, u32[]{:S(2)}) %all-to-all-start) | async-done | bytes 3145760 | tf_op jit(solution)/shard_map/all_to_all | solution.py:974
  152.5 48.1 %attend.1 = (bf16[8,3,128,128]{3,2,1,0:T(8,128)(2,1)}, f32[3,2048,128]{2,1,0:T(8,128)}, bf16[3,2048,128]{2,1,0:T(8,128)(2,1)}, bf16[3,2048,128]{2,1,0:T(8,128)(2...) custom-call(bf16[8,3,256,256]{3,2,1,0:T(8,128)(2,1)} %copy-done.7, ...), custom_call_target="tpu_custom_call" | custom-call | flops 22950000640 | tf_op jit(solution)/shard_map/attend/pallas_call | solution.py:56
  200.7 25.5 %all_to_all.50.refs_0_.refs_7_ = bf16[8,3,128,128]{3,2,1,0:T(8,128)(2,1)} all-to-all(bf16[8,3,128,128]{3,2,1,0:T(8,128)(2,1)} %get-tuple-element.118), channel_id=1, replica_groups=mesh['seq'=8,'head'=4] {'seq'}, dimensions={0} | all-to-all | bytes 1572864 | tf_op jit(solution)/shard_map/all_to_all | solution.py:974
  236.4 31.5 %all-to-all-done.3.refs_11_ = bf16[4,512,384]{2,1,0:T(8,128)(2,1)S(1)} async-done(((bf16[4,512,384]{2,1,0:T(8,128)(2,1)}), bf16[4,512,384]{2,1,0:T(8,128)(2,1)S(1)}, u32[]{:S(2)}, u32[]{:S(2)}) %all-to-all-start.3) | async-done | bytes 1572896 | tf_op jit(solution)/shard_map/all_to_all | solution.py:974
  272.2 36.8 %feed.2 = (bf16[1024,1536]{1,0:T(8,128)(2,1)}, bf16[1024,1024]{1,0:T(8,128)(2,1)}, bf16[1024,2048]{1,0:T(8,128)(2,1)}, f32[512,1536]{1,0:T(8,128)}, bf16[512,153...) custom-call(s32[1]{0:T(128)} %bitcast.refs_0_, bf16[1024,1536]{1,0:T(8,128)(2,1)} %bitcast.86, ...), custom_call_target="tpu_custom_call" | custom-call | flops 16650000384 | tf_op jit(solution)/shard_map/feed/pallas_call | solution.py:56
  312.3 37.3 %feed.3 = (bf16[1024,1536]{1,0:T(8,128)(2,1)}, bf16[1024,1024]{1,0:T(8,128)(2,1)}, bf16[1024,2048]{1,0:T(8,128)(2,1)}, f32[512,1536]{1,0:T(8,128)}, bf16[512,153...) custom-call(s32[1]{0:T(128)} %bitcast.refs_0_, ...), custom_call_target="tpu_custom_call", output_to_operand_aliasing={{0}: (12, {}), {1}: (13, {}), {2}: (14, {})} | custom-call | flops 16650000384 | tf_op jit(solution)/shard_map/feed/pallas_call | solution.py:56
  365.4 15.6 %turned_products.3 = (bf16[1536,3072]{1,0:T(8,128)(2,1)}, f32[8,128]{1,0:T(8,128)}) custom-call(bf16[1024,1536]{1,0:T(8,128)(2,1)} %get-tuple-element.148.refs_0_, bf16[1024,2048]{1,0:T(8,128)(2,1)} %get-tuple-element.149.refs_1_, bf16[1024,1536]{1,0:T(8,128)(2,1)} %bitcast.100, bf16[1024,1024]{1,0:T(8,128)(2,1)} %get-tuple-element.150.refs_3_, ...), custom_call_target="tpu_custom_call" | custom-call | flops 5849999872 | tf_op jit(solution)/shard_map/turned_products/pallas_call | solution.py:56
  381.8 23.1 %attend_back.3 = (bf16[8,1,256,256]{3,2,1,0:T(8,128)(2,1)}, f32[8,128]{1,0:T(8,128)}) custom-call(bf16[3,2048,128]{2,1,0:T(8,128)(2,1)} %get-tuple-element.134.refs_0_, bf16[3,2048,128]{2,1,0:T(8,128)(2,1)} %get-tuple-element.135.refs_1_, bf16[3,2048,128]{2,1,0:T(8,128)(2,1)} %get-tuple-element.136.refs_2_, ...), custom_call_target="tpu_custom_call" | custom-call | flops 9900000256 | tf_op jit(solution)/shard_map/attend_back/pallas_call | solution.py:56
  415.6 8.4 %turned_products.4 = (bf16[1536,768]{1,0:T(8,128)(2,1)}, f32[8,128]{1,0:T(8,128)}) custom-call(bf16[1024,1536]{1,0:T(8,128)(2,1)} %get-tuple-element.159.refs_0_, bf16[1024,384]{1,0:T(8,128)(2,1)} %get-tuple-element.160.refs_1_, bf16[1024,1536]{1,0:T(8,128)(2,1)} %get-tuple-element.161.refs_2_.refs_0_, bf16[1024,384]{1,0:T(8,128)(2,1)} %get-tuple-element.162.refs_3_.refs_4_, ...), custom_call_target="tpu_custom_call" | custom-call | flops 3600000000 | tf_op jit(solution)/shard_map/turned_products/pallas_call | solution.py:56
  443.5 23.1 %attend_back.4 = (bf16[8,1,256,256]{3,2,1,0:T(8,128)(2,1)}, f32[8,128]{1,0:T(8,128)}) custom-call(bf16[3,2048,128]{2,1,0:T(8,128)(2,1)} %get-tuple-element.134.refs_0_, bf16[3,2048,128]{2,1,0:T(8,128)(2,1)} %get-tuple-element.135.refs_1_, bf16[3,2048,128]{2,1,0:T(8,128)(2,1)} %get-tuple-element.136.refs_2_, ...), custom_call_target="tpu_custom_call" | custom-call | flops 9900000256 | tf_op jit(solution)/shard_map/attend_back/pallas_call | solution.py:56
  466.6 23.1 %attend_back.5 = (bf16[8,1,256,256]{3,2,1,0:T(8,128)(2,1)}, f32[8,128]{1,0:T(8,128)}) custom-call(bf16[3,2048,128]{2,1,0:T(8,128)(2,1)} %get-tuple-element.134.refs_0_, bf16[3,2048,128]{2,1,0:T(8,128)(2,1)} %get-tuple-element.135.refs_1_, bf16[3,2048,128]{2,1,0:T(8,128)(2,1)} %get-tuple-element.136.refs_2_, ...), custom_call_target="tpu_custom_call" | custom-call | flops 9900000256 | tf_op jit(solution)/shard_map/attend_back/pallas_call | solution.py:56
  495.9 13.3 %all-to-all-done.8 = bf16[8,1,256,256]{3,2,1,0:T(8,128)(2,1)S(1)} async-done(((bf16[8,1,256,256]{3,2,1,0:T(8,128)(2,1)}), bf16[8,1,256,256]{3,2,1,0:T(8,128)(2,1)S(1)}, u32[]{:S(2)}, u32[]{:S(2)}) %all-to-all-start.8) | async-done | bytes 1048608 | tf_op jit(solution)/shard_map/all_to_all | solution.py:974
  519.5 20.1 %all-to-all-done.7 = bf16[8,1,256,256]{3,2,1,0:T(8,128)(2,1)S(1)} async-done(((bf16[8,1,256,256]{3,2,1,0:T(8,128)(2,1)}), bf16[8,1,256,256]{3,2,1,0:T(8,128)(2,1)S(1)}, u32[]{:S(2)}, u32[]{:S(2)}) %all-to-all-start.7) | async-done | bytes 1048608 | tf_op jit(solution)/shard_map/all_to_all | solution.py:974
  546.9 22.0 %reduce-scatter.3.cloned.1.call-done.refs_8_ = bf16[192,3072]{1,0:T(8,128)(2,1)} async-done(((bf16[1536,3072]{1,0:T(8,128)(2,1)}), bf16[192,3072]{1,0:T(8,128)(2,1)}) %reduce-scatter.3.cloned.1.call-update) | async-done | bytes 1179664 | tf_op jit(solution)/shard_map/reduce_scatter | solution.py:1165
  577.0 8.2 %project_back.5 = (bf16[1024,1280]{1,0:T(8,128)(2,1)}, bf16[256,1536]{1,0:T(8,128)(2,1)}, f32[2,1,1920]{2,1,0:T(1,128)}, f32[8,128]{1,0:T(8,128)}) custom-call(s32[1]{0:T(128)S(6)} %convert_element_type.65.refs_0_, bf16[6,256,256]{2,1,0:T(8,128)(2,1)} %pad_maximum_fusion.4.refs_1_, ...), custom_call_target="tpu_custom_call", output_to_operand_aliasing={{0}: (8, {})} | custom-call | flops 2700000000 | tf_op jit(solution)/shard_map/project_back/pallas_call | solution.py:56
  589.8 8.7 %project_back.6 = (bf16[1024,1280]{1,0:T(8,128)(2,1)}, bf16[128,1536]{1,0:T(8,128)(2,1)}, bf16[128,1536]{1,0:T(8,128)(2,1)}, f32[2,1,1920]{2,1,0:T(1,128)}, f32[8,128]{1,0:T(8,128)}) custom-call(s32[1]{0:T(128)S(6)} %convert_element_type.65.refs_0_, bf16[6,256,256]{2,1,0:T(8,128)(2,1)} %pad_maximum_fusion.5.refs_1_, ...), custom_call_target="tpu_custom_call", output_to_operand_aliasing={{0}: (8, {})} | custom-call | flops 2700000000 | tf_op jit(solution)/shard_map/project_back/pallas_call | solution.py:56
  598.6 8.8 %project_back.7 = (bf16[1024,1280]{1,0:T(8,128)(2,1)}, bf16[128,1536]{1,0:T(8,128)(2,1)}, bf16[128,1536]{1,0:T(8,128)(2,1)}, f32[2,1,1920]{2,1,0:T(1,128)}, f32[8,128]{1,0:T(8,128)}) custom-call(s32[1]{0:T(128)S(6)} %convert_element_type.65.refs_0_, bf16[6,256,256]{2,1,0:T(8,128)(2,1)} %slice_bitcast_fusion.1.refs_1_, ...), custom_call_target="tpu_custom_call", output_to_operand_aliasing={{0}: (8, {})} | custom-call | flops 2700000000 | tf_op jit(solution)/shard_map/project_back/pallas_call | solution.py:56
  614.8 9.0 %turned_products.5 = (bf16[1536,1280]{1,0:T(8,128)(2,1)}, f32[8,128]{1,0:T(8,128)}) custom-call(bf16[1024,1536]{1,0:T(8,128)(2,1)} %get-tuple-element.161.refs_2_.refs_0_, bf16[1024,1280]{1,0:T(8,128)(2,1)} %get-tuple-element.193.refs_1_, f32[8,128]{1,0:T(8,128)} %get-tuple-element.194.refs_2_), custom_call_target="tpu_custom_call" | custom-call | flops 4049999872 | tf_op jit(solution)/shard_map/turned_products/pallas_call | solution.py:56
  631.7 42.3 %collective-permute-done.21 = f32[1,3352]{1,0:T(1,128)S(1)} collective-permute-done((f32[1,3352]{1,0:T(1,128)S(1)}, f32[1,3352]{1,0:T(1,128)S(1)}, u32[]{:S(2)}, u32[]{:S(2)}) %collective-permute-start.21) | collective-permute-done | bytes 13440 | tf_op jit(solution)/shard_map/ppermute | solution.py:970
  682.6 17.8 %collective-permute-done.23 = f32[1,3352]{1,0:T(1,128)S(1)} collective-permute-done((f32[1,3352]{1,0:T(1,128)S(1)}, f32[1,3352]{1,0:T(1,128)S(1)}, u32[]{:S(2)}, u32[]{:S(2)}) %collective-permute-start.23) | collective-permute-done | bytes 13440 | tf_op jit(solution)/shard_map/ppermute | solution.py:970
  (306 shorter events, 246.0 us)
Async XLA Ops:
  7.2 50.4 %all-gather.4.cloned.1.call-start = ((), (), s32[]{:S(2)}) async-start(), calls=%async_computation.12 | async-start | bytes 5750784 | tf_op jit(solution)/shard_map/all_gather | solution.py:1031
  14.2 258.1 %all-gather.8.cloned.1.call-start = ((), (), s32[]{:S(2)}) async-start(), calls=%async_computation.14 | async-start | bytes 10616832 | tf_op jit(solution)/shard_map/all_gather | solution.py:1033
  16.6 255.6 %all-gather.6.cloned.1.call-start = ((), (), s32[]{:S(2)}) async-start(), calls=%async_computation.13 | async-start | bytes 15925248 | tf_op jit(solution)/shard_map/all_gather | solution.py:1100
  16.8 56.2 %collective-permute-start.2 = (bf16[192,1536]{1,0:T(8,128)(2,1)S(1)}, bf16[192,1536]{1,0:T(8,128)(2,1)S(1)}, u32[]{:S(2)}, u32[]{:S(2)}) collective-permute-start(bf16[192,1536]{1,0:T(8,128)(2,1)S(1)} %get-tuple-element.311), channel_id=1, source_target_pairs={{0,2},{1,3},{2,0},{3,1},{4,6},{5,7},{6,4},{7,5},{8,10},{9,11},{10,... | collective-permute-start | bytes 1769480 | tf_op jit(solution)/shard_map/ppermute | solution.py:970
  36.7 36.3 %collective-permute-start.1 = (bf16[192,768]{1,0:T(8,128)(2,1)S(1)}, bf16[192,768]{1,0:T(8,128)(2,1)S(1)}, u32[]{:S(2)}, u32[]{:S(2)}) collective-permute-start(bf16[192,768]{1,0:T(8,128)(2,1)S(1)} %pad_maximum_fusion.11), channel_id=1, source_target_pairs={{0,2},{1,3},{2,0},{3,1},{4,6},{5,7},{6,4},{7,5},{8,10},{9,11},{10,... | collective-permute-start | bytes 884744 | tf_op jit(solution)/shard_map/ppermute | solution.py:970
  39.1 48.7 %collective-permute-start.3 = (bf16[192,1536]{1,0:T(8,128)(2,1)S(1)}, bf16[192,1536]{1,0:T(8,128)(2,1)S(1)}, u32[]{:S(2)}, u32[]{:S(2)}) collective-permute-start(bf16[192,1536]{1,0:T(8,128)(2,1)S(1)} %get-tuple-element.310), channel_id=1, source_target_pairs={{0,2},{1,3},{2,0},{3,1},{4,6},{5,7},{6,4},{7,5},{8,10},{9,11},{10,... | collective-permute-start | bytes 1769480 | tf_op jit(solution)/shard_map/ppermute | solution.py:970
  94.8 56.0 %all-to-all-start = ((bf16[8,3,256,256]{3,2,1,0:T(8,128)(2,1)}), bf16[8,3,256,256]{3,2,1,0:T(8,128)(2,1)S(1)}, u32[]{:S(2)}, u32[]{:S(2)}) async-start(bf16[8,3,256,256]{3,2,1,0:T(8,128)(2,1)} %get-tuple-element.116), calls=%async_computation | async-start | bytes 6291456 | tf_op jit(solution)/shard_map/all_to_all | solution.py:974
  228.9 38.9 %all-to-all-start.3 = ((bf16[4,512,384]{2,1,0:T(8,128)(2,1)}), bf16[4,512,384]{2,1,0:T(8,128)(2,1)S(1)}, u32[]{:S(2)}, u32[]{:S(2)}) async-start(bf16[4,512,384]{2,1,0:T(8,128)(2,1)} %get-tuple-element.124), calls=%async_computation.3 | async-start | bytes 3145728 | tf_op jit(solution)/shard_map/all_to_all | solution.py:974
  267.9 43.2 %all-to-all-start.2 = ((bf16[4,512,384]{2,1,0:T(8,128)(2,1)}), bf16[4,512,384]{2,1,0:T(8,128)(2,1)S(1)}, u32[]{:S(2)}, u32[]{:S(2)}) async-start(bf16[4,512,384]{2,1,0:T(8,128)(2,1)} %get-tuple-element.123), calls=%async_computation.2 | async-start | bytes 3145728 | tf_op jit(solution)/shard_map/all_to_all | solution.py:974
  309.0 40.6 %collective-permute-start.6 = (bf16[512,1536]{1,0:T(8,128)(2,1)}, bf16[512,1536]{1,0:T(8,128)(2,1)S(1)}, u32[]{:S(2)}, u32[]{:S(2)}) collective-permute-start(bf16[512,1536]{1,0:T(8,128)(2,1)} %get-tuple-element.138.refs_0_), channel_id=1, source_target_pairs={{0,1},{1,0},{2,3},{3,2},{4,5},{5,4},{6,7},{7,6},{8,9},{9,8},{10,11... | collective-permute-start | bytes 4718600 | tf_op jit(solution)/shard_map/ppermute | solution.py:970
  349.5 55.3 %collective-permute-start.7 = (bf16[512,1536]{1,0:T(8,128)(2,1)}, bf16[512,1536]{1,0:T(8,128)(2,1)S(1)}, u32[]{:S(2)}, u32[]{:S(2)}) collective-permute-start(bf16[512,1536]{1,0:T(8,128)(2,1)} %get-tuple-element.144.refs_0_), channel_id=1, source_target_pairs={{0,1},{1,0},{2,3},{3,2},{4,5},{5,4},{6,7},{7,6},{8,9},{9,8},{10,11... | collective-permute-start | bytes 4718600 | tf_op jit(solution)/shard_map/ppermute | solution.py:970
  365.4 178.1 %reduce-scatter.5.cloned.1.call-start = ((), (), s32[]{:S(2)}) async-start(), calls=%async_computation.16 | async-start | bytes 2654208 | tf_op jit(solution)/shard_map/reduce_scatter | solution.py:1165
  424.0 144.8 %reduce-scatter.3.cloned.1.call-start = ((), (), s32[]{:S(2)}) async-start(), calls=%async_computation.15 | async-start | bytes 10616832 | tf_op jit(solution)/shard_map/reduce_scatter | solution.py:1165
  430.1 82.7 %collective-permute-start.5 = (bf16[512,1536]{1,0:T(8,128)(2,1)}, bf16[512,1536]{1,0:T(8,128)(2,1)}, u32[]{:S(2)}, u32[]{:S(2)}) collective-permute-start(bf16[512,1536]{1,0:T(8,128)(2,1)} %get-tuple-element.133.refs_1_), channel_id=1, source_target_pairs={{0,1},{1,0},{2,3},{3,2},{4,5},{5,4},{6,7},{7,6},{8,9},{9,8},{10,11... | collective-permute-start | bytes 4718600 | tf_op jit(solution)/shard_map/ppermute | solution.py:970
  439.9 49.7 %all-to-all-start.6 = ((bf16[8,1,256,256]{3,2,1,0:T(8,128)(2,1)}), bf16[8,1,256,256]{3,2,1,0:T(8,128)(2,1)S(1)}, u32[]{:S(2)}, u32[]{:S(2)}) async-start(bf16[8,1,256,256]{3,2,1,0:T(8,128)(2,1)} %get-tuple-element.168), calls=%async_computation.6 | async-start | bytes 2097152 | tf_op jit(solution)/shard_map/all_to_all | solution.py:974
  493.8 91.5 %collective-permute-start.4 = (bf16[512,1536]{1,0:T(8,128)(2,1)}, bf16[512,1536]{1,0:T(8,128)(2,1)}, u32[]{:S(2)}, u32[]{:S(2)}) collective-permute-start(bf16[512,1536]{1,0:T(8,128)(2,1)} %get-tuple-element.131.refs_1_), channel_id=1, source_target_pairs={{0,1},{1,0},{2,3},{3,2},{4,5},{5,4},{6,7},{7,6},{8,9},{9,8},{10,11... | collective-permute-start | bytes 4718600 | tf_op jit(solution)/shard_map/ppermute | solution.py:970
  509.2 30.4 %all-to-all-start.7 = ((bf16[8,1,256,256]{3,2,1,0:T(8,128)(2,1)}), bf16[8,1,256,256]{3,2,1,0:T(8,128)(2,1)S(1)}, u32[]{:S(2)}, u32[]{:S(2)}) async-start(bf16[8,1,256,256]{3,2,1,0:T(8,128)(2,1)} %get-tuple-element.169), calls=%async_computation.7 | async-start | bytes 2097152 | tf_op jit(solution)/shard_map/all_to_all | solution.py:974
  512.7 216.0 %all-reduce.13.cloned.1.call-start = ((), (), s32[]{:S(2)}) async-start(), calls=%async_computation.17 | async-start | bytes 3145728 | tf_op jit(solution)/shard_map/psum | solution.py:1204
  613.4 62.2 %collective-permute-start.8 = (bf16[128,1536]{1,0:T(8,128)(2,1)S(1)}, bf16[128,1536]{1,0:T(8,128)(2,1)S(1)}, u32[]{:S(2)}, u32[]{:S(2)}) collective-permute-start(bf16[128,1536]{1,0:T(8,128)(2,1)S(1)} %copy-done.27), channel_id=1, source_target_pairs={{0,1},{3,2},{4,5},{7,6},{8,9},{11,10},{12,13},{15,14},{16,17},{19,... | collective-permute-start | bytes 1179656 | tf_op jit(solution)/shard_map/ppermute | solution.py:960
  623.8 130.2 %all-to-all-start.9 = ((bf16[8,192,1280]{2,1,0:T(8,128)(2,1)}), bf16[8,192,1280]{2,1,0:T(8,128)(2,1)}, u32[]{:S(2)}, u32[]{:S(2)}) async-start(bf16[8,192,1280]{2,1,0:T(8,128)(2,1)} %bitcast.109), calls=%async_computation.11 | async-start | bytes 7864320 | tf_op jit(solution)/shard_map/all_to_all | solution.py:974
  628.6 47.8 %collective-permute-start.15 = (bf16[128,1536]{1,0:T(8,128)(2,1)S(1)}, bf16[128,1536]{1,0:T(8,128)(2,1)S(1)}, u32[]{:S(2)}, u32[]{:S(2)}) collective-permute-start(bf16[128,1536]{1,0:T(8,128)(2,1)S(1)} %add.146), channel_id=1, source_target_pairs={{1,2},{2,1},{5,6},{6,5},{9,10},{10,9},{13,14},{14,13},{17,18},{18,... | collective-permute-start | bytes 1179656 | tf_op jit(solution)/shard_map/ppermute | solution.py:960
  629.3 44.7 %collective-permute-start.21 = (f32[1,3352]{1,0:T(1,128)S(1)}, f32[1,3352]{1,0:T(1,128)S(1)}, u32[]{:S(2)}, u32[]{:S(2)}) collective-permute-start(f32[1,3352]{1,0:T(1,128)S(1)} %fusion.27), channel_id=1, source_target_pairs={{0,8},{4,12},{8,0},{12,4},{16,24},{20,28},{24,16},{28,20},{1,9},{5... | collective-permute-start | bytes 40232 | tf_op jit(solution)/shard_map/ppermute | solution.py:970
  675.7 29.5 %collective-permute-start.9 = (bf16[128,1536]{1,0:T(8,128)(2,1)S(1)}, bf16[128,1536]{1,0:T(8,128)(2,1)S(1)}, u32[]{:S(2)}, u32[]{:S(2)}) collective-permute-start(bf16[128,1536]{1,0:T(8,128)(2,1)S(1)} %add.143), channel_id=1, source_target_pairs={{1,2},{2,1},{5,6},{6,5},{9,10},{10,9},{13,14},{14,13},{17,18},{18,... | collective-permute-start | bytes 1179656 | tf_op jit(solution)/shard_map/ppermute | solution.py:960
  676.5 30.1 %collective-permute-start.16 = (bf16[128,1536]{1,0:T(8,128)(2,1)S(1)}, bf16[128,1536]{1,0:T(8,128)(2,1)S(1)}, u32[]{:S(2)}, u32[]{:S(2)}) collective-permute-start(bf16[128,1536]{1,0:T(8,128)(2,1)S(1)} %add.147), channel_id=1, source_target_pairs={{2,3},{1,0},{6,7},{5,4},{10,11},{9,8},{14,15},{13,12},{18,19},{17,... | collective-permute-start | bytes 1179656 | tf_op jit(solution)/shard_map/ppermute | solution.py:960
  (64 other events, 748.3 us)
Sparse Core Ops, SparseCore 0:
  14.3 43.2 all-gather.3
  59.5 81.4 all-gather.7
  143.4 97.4 all-gather.5
  424.1 53.2 reduce-scatter.4
  481.2 87.6 reduce-scatter.2
  613.5 86.6 all-reduce.12

commit v3 on v2

--- a/solution.py
+++ b/solution.py
@@ -28,15 +28,12 @@
     return pltpu.CompilerParams(vmem_limit_bytes=60 * MIB)
 
 
-def linked(kernel, inputs, extra, outputs):
+def linked(kernel, inputs, extra, outputs, carried):
     def body(*refs):
-        token = refs[inputs + extra + outputs]
+        first = inputs + extra
+        token = refs[first + outputs + carried]
         token[...] = jnp.zeros_like(token)
-        kernel(
-            *refs[:inputs],
-            *refs[inputs + extra : inputs + extra + outputs],
-            *refs[inputs + extra + outputs + 1 :],
-        )
+        kernel(*refs[:inputs], *refs[first : first + outputs], *refs[first + outputs + carried + 1 :])
 
     return body
 
@@ -45,27 +42,35 @@
     def __init__(self):
         self.tokens = []
 
-    def call(self, kernel, name, grid, ins, outs, us, scratch=(), before=(), scalars=(), after=()):
+    def call(
+        self, kernel, name, grid, ins, outs, us, scratch=(), before=(), scalars=(), after=(), carry=()
+    ):
         arrays = list(scalars) + [array for array, _ in ins]
-        extra = list(before) + list(after) + self.tokens
+        extra = list(before) + list(carry) + list(after) + self.tokens
         count = len(arrays)
         whole = lambda *at: (0, 0)
-        out_specs = [spec for _, _, spec in outs] + [pl.BlockSpec((8, LANES), whole)]
+        anywhere = pl.BlockSpec(memory_space=pl.ANY)
+        out_specs = [spec for _, _, spec in outs] + [anywhere] * len(carry)
+        out_specs.append(pl.BlockSpec((8, LANES), whole))
         out_shape = [jax.ShapeDtypeStruct(shape, kind) for shape, kind, _ in outs]
+        out_shape += [jax.ShapeDtypeStruct(array.shape, array.dtype) for array in carry]
         out_shape.append(jax.ShapeDtypeStruct((8, LANES), F32))
+        aliases = {count + i: i for i in range(len(before))}
+        for i in range(len(carry)):
+            aliases[count + len(before) + i] = len(outs) + i
         *results, token = pl.pallas_call(
-            linked(kernel, count, len(extra), len(outs)),
+            linked(kernel, count, len(extra), len(outs), len(carry)),
             grid_spec=pltpu.PrefetchScalarGridSpec(
                 num_scalar_prefetch=len(scalars),
                 grid=grid,
-                in_specs=[spec for _, spec in ins] + [pl.BlockSpec(memory_space=pl.ANY)] * len(extra),
+                in_specs=[spec for _, spec in ins] + [anywhere] * len(extra),
                 out_specs=out_specs,
                 scratch_shapes=list(scratch),
             ),
             out_shape=out_shape,
-            input_output_aliases={count + i: i for i in range(len(before))},
+            input_output_aliases=aliases,
             compiler_params=params(),
-            cost_estimate=pl.CostEstimate(flops=int(us * 0.45e9), bytes_accessed=0, transcendentals=0),
+            cost_estimate=pl.CostEstimate(flops=int(us * 0.3e9), bytes_accessed=0, transcendentals=0),
             name=name,
         )(*arrays, *extra)
         self.tokens = [token]
@@ -125,6 +130,20 @@
 
 def merge_swapped(low, first, second):
     return jnp.where(low, swap_halves(first), second)
+
+
+def put_pair(refs, pair, block, column=0, start=0):
+    owners = refs[0].shape[0]
+    owner, place = lax.rem(pair, owners), lax.div(pair, owners)
+    width = block.shape[1]
+    for ref in refs:
+        stop = start + ref.shape[1]
+
+        @pl.when((place >= start) & (place < stop))
+        def _(ref=ref, start=start):
+            ref[owner, place - start, :, column : column + width] = block
+
+        start = stop
 
 
 def unpack_rows(low_half, first, second):
@@ -148,7 +167,7 @@
 
 
 def project_kernel(
-    heads, idle, x_ref, w_ref, bias_ref, gain_ref, gq_ref, gk_ref, a_ref, raw_ref, gl_ref, pay_ref
+    heads, idle, x_ref, w_ref, bias_ref, gain_ref, gq_ref, gk_ref, a_ref, raw_ref, gl_ref, *pay_refs
 ):
     x = x_ref[...].astype(F32)
     rows = x.shape[0]
@@ -180,15 +199,13 @@
                 both = merge_swapped(low, query, key)
                 rest = jnp.where(low, swap_halves(value), zl)
             pair = pl.program_id(0) * heads + head
-            owner, place = lax.rem(pair, pay_ref.shape[0]), lax.div(pair, pay_ref.shape[0])
-            pay_ref[owner, place, :, :LANES] = both.astype(BF16)
-            pay_ref[owner, place, :, LANES:] = rest.astype(BF16)
+            put_pair(pay_refs, pair, both.astype(BF16))
+            put_pair(pay_refs, pair, rest.astype(BF16), LANES)
 
     @pl.when(pl.program_id(0) == 0)
     def _():
         for pair in idle:
-            owner, place = pair % pay_ref.shape[0], pair // pay_ref.shape[0]
-            pay_ref[owner, place] = jnp.zeros(pay_ref.shape[2:], BF16)
+            put_pair(pay_refs, pair, jnp.zeros((rows, 2 * LANES), BF16))
 
 
 def project(order, heads, cols, owners, x, weights, bias_row, gain_row, gq_row, gk_row, micros, after):
@@ -200,7 +217,8 @@
     row = pl.BlockSpec((1, LANES), whole)
     pairs = -(-micros * heads // owners)
     idle = range(micros * heads, pairs * owners)
-    sent = (owners, pairs, rows, 2 * LANES)
+    parts = [pairs - 1, 1] if pairs > 1 else [1]
+    sent = [(owners, part, rows, 2 * LANES) for part in parts]
     return order.call(
         functools.partial(project_kernel, heads, idle),
         "project",
@@ -217,8 +235,8 @@
             ((total, width), BF16, pl.BlockSpec((rows, width), part)),
             ((total, 2 * cols), F32, pl.BlockSpec((rows, 2 * cols), part)),
             ((total, cols), F32, pl.BlockSpec((rows, cols), part)),
-            (sent, BF16, pl.BlockSpec(sent, lambda m: (0, 0, 0, 0))),
-        ],
+        ]
+        + [(shape, BF16, pl.BlockSpec(shape, lambda m: (0, 0, 0, 0))) for shape in sent],
         13,
         after=after,
     )
@@ -257,8 +275,8 @@
     half_low = lanes_of(STRIP) < HEAD_SIZE
     lane_here = lanes_of(size)
 
-    def one_block(qi, carry):
-        at = pl.ds(pl.multiple_of(qi * size, size), size)
+    def one_block(qi):
+        at = pl.ds(qi * size, size)
         query = q_ref[0, at, :]
 
         def absorb(key, value, total, masked=False):
@@ -272,11 +290,9 @@
             here = pl.ds(t * size, size)
             total = absorb(tk_ref[0, here, :], tv_ref[0, here, :], total)
 
-        def earlier(ki, total):
-            here = pl.ds(pl.multiple_of(ki * size, size), size)
-            return absorb(k_ref[0, here, :], v_ref[0, here, :], total)
-
-        total = lax.fori_loop(0, qi, earlier, total)
+        for ki in range(qi):
+            here = pl.ds(ki * size, size)
+            total = absorb(k_ref[0, here, :], v_ref[0, here, :], total)
         total = absorb(k_ref[0, at, :], v_ref[0, at, :], total, True)
         weight = total[:, 64:65]
         mixture = total / weight
@@ -288,19 +304,19 @@
         old = query.astype(F32)
         shifted = forget_column(old) - jnp.log(weight)
         q_ref[0, at, :] = at_lanes(lane_here, 64, in_three(shifted), old).astype(BF16)
-        return carry
-
-    lax.fori_loop(0, length // size, one_block, 0)
-
-
-def attend(order, pay, tail_key, tail_value):
+
+    for qi in range(length // size):
+        one_block(qi)
+
+
+def attend(order, pay, tail_key, tail_value, first):
     blocks, pairs, rows, _ = pay.shape
     length = blocks * rows
     tail_length = tail_key.shape[1]
     size = min(512, length)
     pair = lambda j: (j, 0, 0)
     across = lambda j: (0, j, 0, 0)
-    tail = pl.BlockSpec((1, tail_length, LANES), pair)
+    tail = pl.BlockSpec((1, tail_length, LANES), lambda j: (first + j, 0, 0))
     whole = pl.BlockSpec((1, length, LANES), pair)
     return order.call(
         functools.partial(attend_kernel, size),
@@ -366,7 +382,7 @@
     count = length // size
 
     def block_at(i):
-        return pl.ds(pl.multiple_of(i * size, size), size)
+        return pl.ds(i * size, size)
 
     def pieces(key, value, at, masked=False):
         scores = dot(key, q_ref[0, at, :], NT)
@@ -379,7 +395,7 @@
     tail_length = tk_ref.shape[1]
     tail_count = tail_length // size
 
-    def tail_block(qi, carry):
+    for qi in range(count):
         at = block_at(qi)
         total = jnp.zeros((LANES, size), F32)
         for t in range(tail_count):
@@ -387,19 +403,17 @@
             _, score_grad = pieces(key, tv_ref[0, pl.ds(t * size, size), :], at)
             total = total + dot(key.T, score_grad)
         dqt_ref[:, at] = total
-        return carry
-
-    lax.fori_loop(0, count, tail_block, 0)
+
     lane_here = lanes_of(size)
     low_here = lane_here < HEAD_SIZE
 
-    def key_block(ki, carry):
+    for ki in range(count):
         own = block_at(ki)
         key = k_ref[0, own, :]
         value = v_ref[0, own, :]
         key_turned = key.T
 
-        def one(at, sums, masked=False):
+        def one(at, sums, masked=False, key=key, value=value, key_turned=key_turned):
             key_sum, value_sum = sums
             prob, score_grad = pieces(key, value, at, masked)
             dqt_ref[:, at] += dot(key_turned, score_grad)
@@ -410,16 +424,13 @@
 
         start = (jnp.zeros((size, LANES), F32), jnp.zeros((size, LANES), F32))
         sums = one(own, start, True)
-        key_sum, value_sum = lax.fori_loop(
-            ki + 1, count, lambda qi, sums: one(block_at(qi), sums), sums
-        )
+        for qi in range(ki + 1, count):
+            sums = one(block_at(qi), sums)
+        key_sum, value_sum = sums
         sums_ref[own, :] = key_sum
         for piece in range(size // rows):
             here = slice(piece * rows, (piece + 1) * rows)
             g_ref[ki * (size // rows) + piece, 0, :, LANES:] = value_sum[here].astype(BF16)
-        return carry
-
-    lax.fori_loop(0, count, key_block, 0)
 
     tri = triangle(rows, False)
 
@@ -441,14 +452,16 @@
     lax.fori_loop(0, blocks, finish, jnp.zeros((1, 1), F32))
 
 
-def attend_back(order, saved, tail_key, tail_value, mixture, packed_grad, pay, place, grad_place):
+def attend_back(
+    order, saved, tail_key, tail_value, mixture, packed_grad, pay, place, saved_place, grad_place, carry, after
+):
     blocks, _, rows, _ = pay.shape
     length = blocks * rows
     tail_length = tail_key.shape[1]
     size = min(512, length)
     pair = lambda j: (place, 0, 0)
     tail = pl.BlockSpec((1, tail_length, LANES), pair)
-    whole = pl.BlockSpec((1, length, LANES), pair)
+    whole = pl.BlockSpec((1, length, LANES), lambda j: (saved_place, 0, 0))
     grad = pl.BlockSpec((blocks, 1, rows // 2, LANES), lambda j: (0, grad_place, 0, 0))
     sent = (blocks, 1, rows, 2 * LANES)
     return order.call(
@@ -461,7 +474,7 @@
             (tail_value, tail),
             (mixture, whole),
             (packed_grad, grad),
-            (pay, pl.BlockSpec((blocks, 1, rows, LANES), lambda j: (0, place, 0, 1))),
+            (pay, pl.BlockSpec((blocks, 1, rows, LANES), lambda j: (0, saved_place, 0, 1))),
         ],
         [(sent, BF16, pl.BlockSpec(sent, lambda j: (0, 0, 0, 0)))],
         22,
@@ -470,7 +483,9 @@
             pltpu.VMEM((LANES, length), F32),
             pltpu.VMEM((length, LANES), F32),
         ],
-    )[0]
+        carry=carry,
+        after=after,
+    )
 
 
 def group_of(heads, ref, first_pair, group, low_half):
@@ -680,7 +695,9 @@
 
 def hidden_back_kernel(
     heads,
-    pair,
+    first,
+    start,
+    with_old,
     dc_ref,
     dc_other_ref,
     hid_ref,
@@ -689,13 +706,19 @@
     w_ref,
     gl_ref,
     ap_ref,
-    dhb_ref,
-    dgl_ref,
-    dh_ref,
-    dap_ref,
-    dg_ref,
+    *refs,
 ):
+    if with_old:
+        old_ref, *refs = refs
+    dhb_ref, dgl_ref, dh_ref, dg_ref, *dap_refs = refs
     rows, cols = gl_ref.shape
+    pair = (first + pl.program_id(0)) * heads
+    if with_old:
+
+        @pl.when(pl.program_id(0) == 0)
+        def _():
+            dap_refs[0][...] = old_ref[...]
+
     hidden = hid_ref[...]
     factor = rms_factor(hidden)
     dc = dc_ref[...].astype(F32) + dc_other_ref[...].astype(F32)
@@ -712,43 +735,47 @@
         gate_value = jax.nn.sigmoid(gl_ref[:, at])
         grad = gated_grad[:, at]
         dgl_ref[:, at] = (grad * mixture * gate_value * (1.0 - gate_value)).astype(BF16)
-        first, second = pack_rows(half_low, grad * gate_value)
-        dap_ref[2 * group] = first.astype(BF16)
-        if 2 * group + 1 < heads:
-            dap_ref[2 * group + 1] = second.astype(BF16)
-
-
-def hidden_back(order, heads, dc, dc_other, hidden, dy, gain_row, weights, gl, packed, rows, micro, place, before):
+        for half, packed in enumerate(pack_rows(half_low, grad * gate_value)):
+            if 2 * group + half < heads:
+                put_pair(dap_refs, pair + 2 * group + half, packed.astype(BF16), start=start)
+
+
+def hidden_back(
+    order, heads, dc, dc_other, hidden, dy, gain_row, weights, gl, packed, rows, first, places, old, before, carry
+):
     total, cols = gl.shape
-    width = dc.shape[1]
-    half = rows // 2
+    group, width = dc.shape
+    count = group // rows
     whole = lambda i: (0, 0)
-    here = lambda i: (2 * micro + i, 0)
-    part = pl.BlockSpec((half, width), lambda i: (2 * place + i, 0))
-    strips = pl.BlockSpec((heads, half // 2, LANES), lambda i: (0, i, 0))
+    here = lambda i: (first + i, 0)
+    part = pl.BlockSpec((rows, width), lambda i: (i, 0))
+    every = lambda shape: pl.BlockSpec(shape, lambda i: (0,) * len(shape))
+    sent = [(packed.shape[0], stop - start, rows // 2, LANES) for start, stop in places]
     return order.call(
-        functools.partial(hidden_back_kernel, heads, micro * heads),
+        functools.partial(hidden_back_kernel, heads, first, places[0][0], bool(old)),
         "hidden_back",
-        (2,),
+        (count,),
         [
             (dc, part),
             (dc_other, part),
             (hidden, part),
-            (dy, pl.BlockSpec((half, width), here)),
+            (dy, pl.BlockSpec((rows, width), here)),
             (gain_row, pl.BlockSpec((1, width), whole)),
             (weights, pl.BlockSpec((width, cols), whole)),
-            (gl, pl.BlockSpec((half, cols), here)),
-            (packed, pl.BlockSpec(packed.shape[:2] + (half // 2, LANES), lambda i: (0, 0, i, 0))),
-        ],
+            (gl, pl.BlockSpec((rows, cols), here)),
+            (packed, every(packed.shape)),
+        ]
+        + [(array, every(array.shape)) for array in old],
         [
-            ((total, width), BF16, pl.BlockSpec((half, width), here)),
-            ((total, cols), BF16, pl.BlockSpec((half, cols), here)),
-            ((rows, width), F32, pl.BlockSpec((half, width), lambda i: (i, 0))),
-            ((heads, half, LANES), BF16, strips),
-            ((2, 1, width), F32, pl.BlockSpec((1, 1, width), lambda i: (i, 0, 0))),
-        ],
-        4,
+            ((total, width), BF16, pl.BlockSpec((rows, width), here)),
+            ((total, cols), BF16, pl.BlockSpec((rows, cols), here)),
+            ((group, width), F32, part),
+            ((count, 1, width), F32, pl.BlockSpec((1, 1, width), lambda i: (i, 0, 0))),
+        ]
+        + [(shape, BF16, every(shape)) for shape in sent],
+        4 * count,
         before=before,
+        carry=carry,
     )
 
 
@@ -765,7 +792,7 @@
     grads_ref,
     *refs,
 ):
-    *da_refs, sums_ref, all_ref = refs
+    *da_refs, sums_ref, all_ref, da_ref = refs
     rows, cols = dgl_ref.shape
     width = x_ref.shape[1]
     lane = lanes_of(rows)
@@ -809,12 +836,11 @@
     if len(da_refs) == 1:
         da_refs[0][...] = da.astype(BF16)
     else:
-        is_kept = pl.program_id(0) == upper_ref[0]
-        for ref, chosen in zip(da_refs, (is_kept, jnp.logical_not(is_kept))):
-
-            @pl.when(chosen)
-            def _(ref=ref):
-                ref[...] = da.astype(BF16)
+        da_ref[...] = da
+        half = rows // 2
+        upper = upper_ref[0]
+        for ref, part in zip(da_refs, (upper, 1 - upper)):
+            ref[0] = da_ref[pl.ds(pl.multiple_of(part * half, half), half), :].astype(BF16)
 
     x = x_ref[...].astype(F32)
     sums_ref[0, :, :width] = jnp.sum(da * x * rms_factor(x), axis=0, keepdims=True)
@@ -823,39 +849,42 @@
     sums_ref[0, :, width + 2 * LANES :] = jnp.sum(forget, axis=0, keepdims=True)
 
 
-def project_back(order, heads, upper, returned, raw, x, dgl, weights, gq_row, gk_row, rows, micro, halves, before, after):
+def project_back(
+    order, heads, upper, returned, raw, x, dgl, weights, gq_row, gk_row, rows, first, count, halves, before, after, carry
+):
     total, cols = dgl.shape
     width, wide = weights.shape
     half = rows // 2
     whole = lambda i, upper: (0, 0)
-    here = lambda i, upper: (2 * micro + i, 0)
+    here = lambda i, upper: (first + i, 0)
     row = pl.BlockSpec((1, LANES), whole)
     sums = width + 3 * LANES
     if halves:
-        da = [((half, width), BF16, pl.BlockSpec((half, width), whole))] * 2
+        da = [((count, half, width), BF16, pl.BlockSpec((1, half, width), lambda i, upper: (i, 0, 0)))] * 2
     else:
-        da = [((rows, width), BF16, pl.BlockSpec((half, width), lambda i, upper: (i, 0)))]
+        da = [((count * rows, width), BF16, pl.BlockSpec((rows, width), lambda i, upper: (i, 0)))]
     return order.call(
         functools.partial(project_back_kernel, heads),
         "project_back",
-        (2,),
+        (count,),
         [
-            (returned, pl.BlockSpec((heads, half, 2 * LANES), lambda i, upper: (0, i, 0))),
-            (raw, pl.BlockSpec((half, 2 * cols), here)),
-            (x, pl.BlockSpec((half, width), here)),
-            (dgl, pl.BlockSpec((half, cols), here)),
+            (returned, pl.BlockSpec((heads, rows, 2 * LANES), lambda i, upper: (i, 0, 0))),
+            (raw, pl.BlockSpec((rows, 2 * cols), here)),
+            (x, pl.BlockSpec((rows, width), here)),
+            (dgl, pl.BlockSpec((rows, cols), here)),
             (weights, pl.BlockSpec((width, wide), whole)),
             (gq_row, row),
             (gk_row, row),
         ],
-        [((total, wide - cols), BF16, pl.BlockSpec((half, wide - cols), here))]
+        [((total, wide - cols), BF16, pl.BlockSpec((rows, wide - cols), here))]
         + da
-        + [((2, 1, sums), F32, pl.BlockSpec((1, 1, sums), lambda i, upper: (i, 0, 0)))],
-        6,
-        scratch=[pltpu.VMEM((half, wide), BF16)],
+        + [((count, 1, sums), F32, pl.BlockSpec((1, 1, sums), lambda i, upper: (i, 0, 0)))],
+        6 * count,
+        scratch=[pltpu.VMEM((rows, wide), BF16), pltpu.VMEM((rows, width), F32)],
         before=before,
         scalars=(upper,),
         after=after,
+        carry=carry,
     )
 
 
@@ -870,23 +899,24 @@
     out_ref[...] = dh_ref[...] + norm_back(x, rms_factor(x), gain_ref[...], da)
 
 
-def input_back(order, rank, summed, x, dh, gain_row, micro, before):
+def input_back(order, rank, summed, place, x, dh, dh_place, gain_row, rows, micro, before, after):
     total, width = x.shape
-    rows = dh.shape[0]
     half = rows // 2
     here = pl.BlockSpec((half, width), lambda i, rank: (2 * micro + i, 0))
-    one = pl.BlockSpec((half, width), lambda i, rank: (i, 0))
+    one = pl.BlockSpec((half, width), lambda i, rank: (2 * place + i, 0))
+    mine = pl.BlockSpec((half, width), lambda i, rank: (2 * dh_place + i, 0))
     passing = pl.BlockSpec((half, width), lambda i, rank: (0, 0))
     return order.call(
         input_back_kernel,
         "input_back",
         (2,),
-        [(x, here), (dh, one), (gain_row, pl.BlockSpec((1, width), lambda i, rank: (0, 0)))]
+        [(x, here), (dh, mine), (gain_row, pl.BlockSpec((1, width), lambda i, rank: (0, 0)))]
         + [(block, one if len(summed) == 1 else passing) for block in summed],
         [((total, width), F32, here)],
         4,
         before=before,
         scalars=(rank,),
+        after=after,
     )
 
 
@@ -895,7 +925,7 @@
     out_ref[...] = total.astype(BF16)
 
 
-def layer_output(order, hidden, part, other, group, total, before):
+def layer_output(order, hidden, part, other, group, total, before, after):
     rows, width = hidden.shape
     tiles = 4
     tile = rows // tiles
@@ -908,6 +938,7 @@
         [((total, width), BF16, pl.BlockSpec((tile, width), lambda i: (tiles * group + i, 0)))],
         4,
         before=before,
+        after=after,
     )
 
 
@@ -948,6 +979,36 @@
     )[0]
 
 
+def owned_kernel(own, left_ref, right_ref, sums_ref, out_ref):
+    product = lax.dot_general(
+        left_ref[...], right_ref[...], (((0,), (0,)), ((), ())), preferred_element_type=F32
+    ).astype(BF16)
+    for i in range(out_ref.shape[0]):
+        out_ref[i, :own] = product[i * own : (i + 1) * own]
+        out_ref[i, own:] = sums_ref[i]
+
+
+def owned_product(order, left, right, sums, us):
+    rows, height = left.shape
+    owners, extra, wide = sums.shape
+    own = height // owners
+    step = 1
+    while own * step % LANES:
+        step += 1
+    return order.call(
+        functools.partial(owned_kernel, own),
+        "owned_product",
+        (owners // step,),
+        [
+            (left, pl.BlockSpec((rows, own * step), lambda i: (0, i))),
+            (right, pl.BlockSpec((rows, wide), lambda i: (0, 0))),
+            (sums, pl.BlockSpec((step, extra, wide), lambda i: (i, 0, 0))),
+        ],
+        [((owners, own + extra, wide), BF16, pl.BlockSpec((step, own + extra, wide), lambda i: (i, 0, 0)))],
+        us,
+    )[0]
+
+
 def line_steps(count):
     return [((t - 1, t), (count - t, count - 1 - t)) for t in range(1, count)]
 
@@ -974,12 +1035,11 @@
     return lax.all_to_all(array, axis, 0, 0, tiled=True)
 
 
-def small_sum(row):
-    for axis in ("seq", "head"):
-        flip = 1
-        while flip < lax.axis_size(axis):
-            row = row + exchanged(row, axis, flip)
-            flip *= 2
+def small_sum(row, axis):
+    flip = 1
+    while flip < lax.axis_size(axis):
+        row = row + exchanged(row, axis, flip)
+        flip *= 2
     return row
 
 
@@ -1036,10 +1096,10 @@
     flip = 1
     while flip < head_count:
         outs.append(exchanged(jnp.concatenate(outs, axis=1), "head", flip))
-        early.append(outs[-1])
-        if flip > 1:
+        if flip == 1:
+            early.append(outs[-1])
+        else:
             units += [tuple(exchanged(part, "head", flip) for part in unit) for unit in units]
-            early += [first_part for first_part, _ in units[len(units) // 2 :]]
         flip *= 2
     far_parts = outs + [part for unit in units[1:] for part in unit]
     rank = head_rank.astype(jnp.int32)[None]
@@ -1083,41 +1143,44 @@
                 taken.append(stage[start:stop, 0])
         return jnp.concatenate(taken, axis=0)
 
-    def stage_of(blocks, j):
-        low, high = j * seq_count, min((j + 1) * seq_count, pair_total)
-        taken = []
-        for m in range(low // heads, (high - 1) // heads + 1):
-            taken.append(blocks[m][max(low - m * heads, 0) : min(high - m * heads, heads)])
-        return pad_to(jnp.concatenate(taken, axis=0), seq_count, 0)[:, None]
-
-    def ready(stages):
-        return len(stages) * seq_count // heads if len(stages) < pairs else micros
-
-    a, raw, gl, pay = project(
+    a, raw, gl, *pays = project(
         order, heads, cols, seq_count, x, first, bias_row, gain_one_row, gq_row, gk_row, micros, early
     )
-    pay = to_all(pay, "seq")
+    pays = [to_all(pay, "seq") for pay in pays]
     far = lax.all_gather(pack(order, far_parts), "seq", axis=0, tiled=True)
-    packed, mixture, *saved = attend(order, pay, tail_key, tail_value)
-    packed = to_all(packed, "seq")
+    kept, returned = [], []
+    at = 0
+    for pay in pays:
+        packed, *saved = attend(order, pay, tail_key, tail_value, at)
+        kept += [(saved, pay, place) for place in range(pay.shape[1])]
+        returned.append(to_all(packed, "seq"))
+        at = len(kept)
+    packed = jnp.concatenate(returned, axis=1)
 
     size = 2 if micros % 2 == 0 else 1
     groups = micros // size
+    chunk = min(512, ff)
     gated, o_alls = (), []
     for g in range(groups):
-        *gated, sent = gate(order, heads, packed, gl, rows, g * size, size, head_count, gated)
+        enough = (g + 1) * size * heads <= (pairs - 1) * seq_count
+        *gated, sent = gate(
+            order, heads, returned[0] if enough else packed, gl, rows, g * size, size, head_count, gated
+        )
         o_alls.append(to_all(sent, "head"))
     o = gated[0]
 
-    chunk = min(512, ff)
     hiddens, out_parts, dc_parts, dc_others = [], [], [], []
-    dhs, daps, gains_two = [], [], []
-    fed, backed, returned_stages = (), (), []
-
-    def back_to_heads(m):
-        nonlocal backed
-        g = m // size
-        *backed, dh, dap, gain = hidden_back(
+    dhs, gains_two = [], []
+    late = ()
+    early_places = size * heads // seq_count if groups > 1 else 0
+    fed, backed = (), ()
+
+    def back_to_heads(g):
+        nonlocal backed, late
+        places = [(early_places, pairs)]
+        if g == 0 and early_places > 0:
+            places = [(0, early_places)] + places
+        dhb, dgl, dh, gain, *sent, out_parts[g] = hidden_back(
             order,
             heads,
             dc_parts[g],
@@ -1129,122 +1192,113 @@
             gl,
             packed,
             rows,
-            m,
-            m % size,
+            g * size,
+            places,
+            late,
             backed,
+            (out_parts[g],),
         )
+        backed, late = (dhb, dgl), (sent[-1],)
         dhs.append(dh)
-        daps.append(dap)
         gains_two.append(gain)
+        return sent[0]
+
+    def scattered(grad):
+        return lax.psum_scatter(grad, "seq", scatter_dimension=0, tiled=True)
 
     for g in range(groups):
         *fed, hidden, out_part, dc_part = feed(
-            order,
-            rank,
-            x,
-            dy,
-            o_alls[g],
-            near,
-            far,
-            gain_two_row,
-            ff,
-            chunk,
-            g,
-            fed,
+            order, rank, x, dy, o_alls[g], near, far, gain_two_row, ff, chunk, g, fed
         )
         hiddens.append(hidden)
         out_parts.append(out_part)
         dc_parts.append(dc_part)
         dc_others.append(exchanged(dc_part, "head", 1))
         if g > 0:
-            for m in range((g - 1) * size, g * size):
-                back_to_heads(m)
+            early_grads = back_to_heads(g - 1)
     c, u, dgu = fed
-
-    def scattered(grad):
-        return lax.psum_scatter(grad, "seq", scatter_dimension=0, tiled=True)
-
     unit_grads = scattered(turned_products(order, [(c, dgu), (dy, u)], 13))
 
-    grads, da_sums, gains_one = (), [], []
-    last_group = (groups - 1) * size
-    da_group = []
-
-    after = ()
-
-    def back_to_input():
-        nonlocal grads, da_group, after
-        for m in range(len(gains_one), ready(returned_stages)):
-            by_line = m >= last_group
-            *out, gain = project_back(
-                order,
-                heads,
-                upper,
-                pairs_of(returned_stages, m, 1),
-                raw,
-                x,
-                backed[1],
-                first,
-                gq_row,
-                gk_row,
-                rows,
-                m,
-                by_line,
-                grads,
-                after,
-            )
-            grads, da = out[:1], out[1:]
-            gains_one.append(gain)
-            after = ()
-            if by_line:
-                da_sums.append(line_sum(*da, "head"))
-            else:
-                da_group += da
-                if len(da_group) == size:
-                    total_da = lax.psum(jnp.concatenate(da_group, axis=0), "head")
-                    da_sums.extend([total_da[i * rows : (i + 1) * rows]] for i in range(size))
-                    da_group = []
-
     layer_out = ()
 
-    def put_out(g):
+    def put_out(g, after=()):
         nonlocal layer_out
         other = exchanged(out_parts[g], "head", 1)
-        layer_out = layer_output(order, hiddens[g], out_parts[g], other, g, total, layer_out)
-
-    sent_grads = []
+        layer_out = layer_output(order, hiddens[g], out_parts[g], other, g, total, layer_out, after)
+
+    if early_places > 0:
+        early_grads = to_all(early_grads, "seq")
+    returned = []
+    mixed = ()
     for j in range(pairs):
-        needed = (min((j + 1) * seq_count, pair_total) - 1) // heads
-        if needed >= len(daps):
-            for m in range(len(daps), micros):
-                back_to_heads(m)
-            mixed_grads = scattered(turned_products(order, [(backed[0], o), (a, backed[1])], 8))
-        if j == len(sent_grads):
-            here = [k for k in range(j, pairs) if (min((k + 1) * seq_count, pair_total) - 1) // heads < len(daps)]
-            stages = jnp.concatenate([stage_of(daps, k) for k in here], axis=1)
-            stages = to_all(stages, "seq")
-            sent_grads += [(stages, k - j) for k in here]
-        returned = attend_back(
-            order, saved, tail_key, tail_value, mixture, sent_grads[j][0], pay, j, sent_grads[j][1]
+        if j == early_places:
+            back_to_heads(groups - 1)
+            mixed = (turned_products(order, [(backed[0], o), (a, backed[1])], 8),)
+            late_grads = to_all(late[0], "seq")
+        sent = (early_grads, j) if j < early_places else (late_grads, j - early_places)
+        saved, pay, place = kept[j]
+        waited = tuple(returned[: j - 1]) if j >= 2 else ()
+        grad, *mixed = attend_back(
+            order, saved[1:], tail_key, tail_value, saved[0], sent[0], pay, j, place, sent[1], mixed, waited
         )
-        returned_stages.append(to_all(returned, "seq"))
-    put_out(0)
-    after = (unit_grads,)
-    last_stage = returned_stages.pop()
-    back_to_input()
-    for g in range(1, groups):
-        put_out(g)
-    returned_stages.append(last_stage)
-    after = (mixed_grads,)
-    back_to_input()
-    head_grads = turned_products(order, [(a, grads[0])], 9)
-
-    input_grad = ()
-    for m in range(micros):
-        input_grad = input_back(order, rank, da_sums[m], x, dhs[m], gain_one_row, m, input_grad)
-
-    head_grads = head_grads.reshape(seq_count, -1, head_grads.shape[1])
+        returned.append(to_all(grad, "seq"))
+
+    put_out(0, tuple(returned[:-1]))
+
+    grads, da_sums, gains_one = (), [], []
+    for g in range(groups):
+        last = g == groups - 1
+        results = project_back(
+            order,
+            heads,
+            upper,
+            pairs_of(returned, g * size, size),
+            raw,
+            x,
+            backed[1],
+            first,
+            gq_row,
+            gk_row,
+            rows,
+            g * size,
+            size,
+            last,
+            grads,
+            (unit_grads,) if g == 0 else (),
+            mixed,
+        )
+        count = 2 if last else 1
+        grads, da, gain, mixed = results[:1], results[1 : 1 + count], results[1 + count], results[2 + count :]
+        gains_one.append(gain)
+        if last:
+            da_sums += [(line_sum(da[0][i], da[1][i], "head"), 0) for i in range(size)]
+        else:
+            total_da = lax.psum(da[0], "head")
+            da_sums += [([total_da], i) for i in range(size)]
+        if g == 0:
+            mixed_grads = scattered(mixed[0])
+            mixed = ()
+            for out in range(1, groups):
+                put_out(out)
+
+    one_sums = jnp.sum(jnp.concatenate(gains_one, axis=0), axis=0)
+    two_sums = jnp.sum(jnp.concatenate(gains_two, axis=0), axis=0) * (1.0 / head_count)
+    own_rows = gain_one.shape[0]
+    shared = pad_to(one_sums[:, width:], 3 * LANES, 1)
+    owned_sums = jnp.concatenate(
+        [
+            one_sums[:, :width].reshape(seq_count, own_rows),
+            two_sums.reshape(seq_count, own_rows),
+            jnp.broadcast_to(shared, (seq_count, 3 * LANES)),
+        ],
+        axis=1,
+    ).astype(BF16)
+    owned_sums = jnp.pad(owned_sums[:, None], ((0, 0), (0, 15), (0, grads[0].shape[1] - owned_sums.shape[1])))
+    head_grads = owned_product(order, a, grads[0], owned_sums, 9)
+
     head_grads = jnp.sum(to_all(head_grads, "seq").astype(F32), axis=0)
+    sums = head_grads[own_rows : own_rows + 1]
+    head_grads = head_grads[:own_rows]
     unit_grads, mixed_grads = unit_grads.astype(F32), mixed_grads.astype(F32)
     strips = [unit_grads[:, i * chunk : (i + 1) * chunk] for i in range(2 * ff // chunk)]
     grad_gate = jnp.concatenate(strips[0::2], axis=1)
@@ -1252,26 +1306,30 @@
     grad_down = unit_grads[:, 2 * ff :].T
     grad_out = mixed_grads[:, :own_cols].T
 
-    one_sums = jnp.sum(jnp.concatenate(gains_one, axis=0), axis=0)
-    two_sums = jnp.sum(jnp.concatenate(gains_two, axis=0), axis=0) * (1.0 / head_count)
+    gain_lanes = 2 * own_rows
+    bias_at = gain_lanes + 2 * LANES
     bias_full = lax.dynamic_update_slice(
-        jnp.zeros((1, forget_bias.shape[0]), F32),
-        one_sums[:, width + 2 * LANES : width + 2 * LANES + heads],
-        (0, head_rank * heads),
-    )
-    sums = small_sum(jnp.concatenate([one_sums[:, : width + 2 * LANES], two_sums, bias_full], axis=1))[0]
-    gq_total = sums[width : width + HEAD_SIZE] + sums[width + HEAD_SIZE : width + LANES]
-    gk_total = sums[width + LANES : width + LANES + HEAD_SIZE] + sums[width + LANES + HEAD_SIZE : width + 2 * LANES]
-    bias_total = sums[2 * width + 2 * LANES :]
+        jnp.zeros((1, forget_bias.shape[0]), F32), sums[:, bias_at : bias_at + heads], (0, head_rank * heads)
+    )
+    sums = small_sum(jnp.concatenate([sums[:, :bias_at], bias_full], axis=1), "head")[0]
+    halves = sums[gain_lanes:bias_at].reshape(4, HEAD_SIZE)
+    gq_total, gk_total = halves[0] + halves[1], halves[2] + halves[3]
+    bias_total = sums[bias_at:]
+
+    input_grad = ()
+    for m in range(micros):
+        summed, place = da_sums[m]
+        input_grad = input_back(
+            order, rank, summed, place, x, dhs[m // size], m % size, gain_one_row, rows, m, input_grad, ()
+        )
+
     input_grad, layer_out = input_grad[0], layer_out[0]
-    own_rows = gain_one.shape[0]
-    own = lambda at: lax.dynamic_slice_in_dim(sums[at : at + width], seq_rank * own_rows, own_rows, 0)
     shape = inputs.shape
     return (
         layer_out.reshape(shape),
         input_grad.reshape(shape),
-        own(0),
-        own(width + 2 * LANES),
+        sums[:own_rows],
+        sums[own_rows:gain_lanes],
         head_grads[:, :own_cols],
         head_grads[:, cols : cols + own_cols],
         head_grads[:, 2 * cols : 2 * cols + own_cols],

time: 777 us -> 692 us (0.89)
  waiting for transfers between devices: 242 us -> 205 us
  Pallas kernels: 324 us -> 296 us
  other arithmetic: 32.6 us -> 24 us
    ppermute x13 -> x10, waiting for transfers between devices: 90.7 us -> 13.1 us  [exchanged(): return lax.ppermute(array, axis, [(i, i ^ flip) for i in range(count)])]
    ppermute x6, waiting for transfers between devices: 4.17 us -> 72.5 us  [line_sum(): arrived = lax.ppermute(moving, axis, hops)]
    all_to_all x9 -> x10, waiting for transfers between devices: 96.5 us -> 68.1 us  [to_all(): return lax.all_to_all(array, axis, 0, 0, tiled=True)]
    pallas_call x27 -> x24, Pallas kernels: 324 us -> 296 us  [call(): pl.pallas_call(linked(kernel, count, len(extra), len(outs), len(carry)),...]
    reduce_scatter x2, waiting for transfers between devices: 22 us -> 0.01 us  [scattered(): return lax.psum_scatter(grad, 'seq', scatter_dimension=0, tiled=True)]
    all_gather x1, waiting for transfers between devices: 16.1 us -> 31.2 us  [shards(): first = lax.all_gather(first_shard, 'seq', axis=0, tiled=True)]
    all_to_all x9 -> x10, starting transfers between devices: 35.8 us -> 41.4 us  [to_all(): return lax.all_to_all(array, axis, 0, 0, tiled=True)]
    ppermute x13 -> x10, starting transfers between devices: 21.6 us -> 18.5 us  [exchanged(): return lax.ppermute(array, axis, [(i, i ^ flip) for i in range(count)])]
  transfers between devices with their start and end apart: 40 -> 38, of which waited for: 17 -> 18; matrix products, arithmetic and copies ran while one was open for 8% -> 7% of each run, Pallas kernels for 37% -> 40%
where the time goes in v3:
time: 692 us; the launch traced here: 683 us
  Pallas kernels  296 us (43%)
  waiting for transfers between devices  205 us (30%)
  starting transfers between devices  75.9 us (11%)
  local copies, waits for them, and re-layouts  42.2 us (6%)
  blocking collectives  24.2 us (3%)
  other arithmetic  24 us (3%)
  between operations  15.4 us (2%)
    pallas_call x24, Pallas kernels, call(): pl.pallas_call(linked(kernel, count, len(extra), len(outs), len(carry)),...  296 us
    ppermute x6, waiting for transfers between devices, line_sum(): arrived = lax.ppermute(moving, axis, hops)  72.5 us
    all_to_all x10, waiting for transfers between devices, to_all(): return lax.all_to_all(array, axis, 0, 0, tiled=True)  68.1 us
    all_to_all x10, starting transfers between devices, to_all(): return lax.all_to_all(array, axis, 0, 0, tiled=True)  41.4 us
    all_gather x1, waiting for transfers between devices, shards(): first = lax.all_gather(first_shard, 'seq', axis=0, tiled=True)  31.2 us
    all_to_all x2, blocking collectives, to_all(): return lax.all_to_all(array, axis, 0, 0, tiled=True)  24.2 us
    ppermute x6, waiting for transfers between devices, line_sum(): passed.append(lax.ppermute(passed[-1], axis, hops))  19.3 us
    ppermute x10, starting transfers between devices, exchanged(): return lax.ppermute(array, axis, [(i, i ^ flip) for i in range(count)])  18.5 us
  transfers between devices with their start and end apart: 38, of which 18 were waited for; matrix products, arithmetic and copies ran while one was open for 7% of the time, Pallas kernels for 40%

profile of v3, /device:TPU:0, one launch (start us, length us, event | category | flops | bytes accessed | tf_op | source)
XLA Modules:
  0.0 682.7 jit_solution(17485611190115869305)
XLA Ops:
  26.4 31.2 %all-gather.4.cloned.1.call-done.refs_1_.refs_5_ = bf16[1536,1664]{1,0:T(8,128)(2,1)} async-done(((bf16[192,1664]{1,0:T(8,128)(2,1)}), bf16[1536,1664]{1,0:T(8,128)(2,1)}) %all-gather.4.cloned.1.call-update) | async-done | bytes 5111824 | tf_op jit(solution)/shard_map/all_gather | solution.py:1091
  59.9 17.7 %project.1 = (bf16[1024,1536]{1,0:T(8,128)(2,1)}, f32[1024,768]{1,0:T(8,128)}, f32[1024,384]{1,0:T(8,128)}, bf16[8,2,256,256]{3,2,1,0:T(8,128)(2,1)}, bf16[8,1,2...) custom-call(bf16[1024,1536]{1,0:T(8,128)(2,1)} %bitcast.84, bf16[1536,1664]{1,0:T(8,128)(2,1)} %all-gather.4.cloned.1.call-done.refs_1_.refs_5_, ...), custom_call_target="tpu_custom_call" | custom-call | flops 3900000000 | tf_op jit(solution)/shard_map/project/pallas_call | solution.py:61
  77.5 7.5 %collective-permute-done.1.refs_2_ = bf16[192,768]{1,0:T(8,128)(2,1)S(1)} collective-permute-done((bf16[192,768]{1,0:T(8,128)(2,1)S(1)}, bf16[192,768]{1,0:T(8,128)(2,1)S(1)}, u32[]{:S(2)}, u32[]{:S(2)}) %collective-permute-start.1) | collective-permute-done | bytes 294944 | tf_op jit(solution)/shard_map/ppermute | solution.py:1031
  117.2 22.5 %all-to-all-done.refs_0_.refs_7_ = bf16[8,2,256,256]{3,2,1,0:T(8,128)(2,1)S(1)} async-done(((bf16[8,2,256,256]{3,2,1,0:T(8,128)(2,1)}), bf16[8,2,256,256]{3,2,1,0:T(8,128)(2,1)S(1)}, u32[]{:S(2)}, u32[]{:S(2)}) %all-to-all-start) | async-done | bytes 2097184 | tf_op jit(solution)/shard_map/all_to_all | solution.py:1035
  143.4 25.3 %attend.2 = (bf16[8,2,128,128]{3,2,1,0:T(8,128)(2,1)}, f32[2,2048,128]{2,1,0:T(8,128)}, bf16[2,2048,128]{2,1,0:T(8,128)(2,1)}, bf16[2,2048,128]{2,1,0:T(8,128)(2...) custom-call(bf16[8,2,256,256]{3,2,1,0:T(8,128)(2,1)} %copy-done.11, ...), custom_call_target="tpu_custom_call" | custom-call | flops 10200000512 | tf_op jit(solution)/shard_map/attend/pallas_call | solution.py:61
  174.1 13.9 %attend.3 = (bf16[8,1,128,128]{3,2,1,0:T(8,128)(2,1)}, f32[1,2048,128]{2,1,0:T(8,128)}, bf16[1,2048,128]{2,1,0:T(8,128)(2,1)}, bf16[1,2048,128]{2,1,0:T(8,128)(2...) custom-call(bf16[8,1,256,256]{3,2,1,0:T(8,128)(2,1)} %copy-done.27, ...), custom_call_target="tpu_custom_call" | custom-call | flops 5100000256 | tf_op jit(solution)/shard_map/attend/pallas_call | solution.py:61
  210.6 30.6 %all-to-all-done.5.refs_11_ = bf16[4,512,384]{2,1,0:T(8,128)(2,1)S(1)} async-done(((bf16[4,512,384]{2,1,0:T(8,128)(2,1)}), bf16[4,512,384]{2,1,0:T(8,128)(2,1)S(1)}, u32[]{:S(2)}, u32[]{:S(2)}) %all-to-all-start.5) | async-done | bytes 1572896 | tf_op jit(solution)/shard_map/all_to_all | solution.py:1035
  245.8 36.8 %feed.2 = (bf16[1024,1536]{1,0:T(8,128)(2,1)}, bf16[1024,1024]{1,0:T(8,128)(2,1)}, bf16[1024,2048]{1,0:T(8,128)(2,1)}, f32[512,1536]{1,0:T(8,128)}, bf16[512,153...) custom-call(s32[1]{0:T(128)} %bitcast.refs_0_, bf16[1024,1536]{1,0:T(8,128)(2,1)} %bitcast.85, ...), custom_call_target="tpu_custom_call" | custom-call | flops 11100000256 | tf_op jit(solution)/shard_map/feed/pallas_call | solution.py:61
  285.8 37.1 %feed.3 = (bf16[1024,1536]{1,0:T(8,128)(2,1)}, bf16[1024,1024]{1,0:T(8,128)(2,1)}, bf16[1024,2048]{1,0:T(8,128)(2,1)}, f32[512,1536]{1,0:T(8,128)}, bf16[512,153...) custom-call(s32[1]{0:T(128)} %bitcast.refs_0_, ...), custom_call_target="tpu_custom_call", output_to_operand_aliasing={{0}: (12, {}), {1}: (13, {}), {2}: (14, {})} | custom-call | flops 11100000256 | tf_op jit(solution)/shard_map/feed/pallas_call | solution.py:61
  324.0 8.3 %hidden_back.2 = (bf16[1024,1536]{1,0:T(8,128)(2,1)}, bf16[1024,384]{1,0:T(8,128)(2,1)}, f32[512,1536]{1,0:T(8,128)}, f32[2,1,1536]{2,1,0:T(1,128)}, bf16[8,1,12...) custom-call(bf16[512,1536]{1,0:T(8,128)(2,1)} %get-tuple-element.127, ...), custom_call_target="tpu_custom_call", output_to_operand_aliasing={{6}: (8, {})} | custom-call | flops 2400000000 | tf_op jit(solution)/shard_map/hidden_back/pallas_call | solution.py:61
  332.3 15.5 %turned_products.2 = (bf16[1536,3072]{1,0:T(8,128)(2,1)}, f32[8,128]{1,0:T(8,128)}) custom-call(bf16[1024,1536]{1,0:T(8,128)(2,1)} %get-tuple-element.140.refs_0_, bf16[1024,2048]{1,0:T(8,128)(2,1)} %get-tuple-element.141.refs_1_, bf16[1024,1536]{1,0:T(8,128)(2,1)} %bitcast.97, bf16[1024,1024]{1,0:T(8,128)(2,1)} %get-tuple-element.142.refs_3_, ...), custom_call_target="tpu_custom_call" | custom-call | flops 3900000000 | tf_op jit(solution)/shard_map/turned_products/pallas_call | solution.py:61
  349.3 10.3 %all_to_all.60.refs_6_ = bf16[8,1,128,128]{3,2,1,0:T(8,128)(2,1)} all-to-all(bf16[8,1,128,128]{3,2,1,0:T(8,128)(2,1)S(1)} %copy-done.36), channel_id=1, replica_groups=mesh['seq'=8,'head'=4] {'seq'}, dimensions={0} | all-to-all | bytes 524288 | tf_op jit(solution)/shard_map/all_to_all | solution.py:1035
  359.7 21.0 %attend_back.3 = (bf16[8,1,256,256]{3,2,1,0:T(8,128)(2,1)}, f32[8,128]{1,0:T(8,128)}) custom-call(bf16[2,2048,128]{2,1,0:T(8,128)(2,1)} %get-tuple-element.135.refs_0_, bf16[2,2048,128]{2,1,0:T(8,128)(2,1)} %get-tuple-element.136.refs_1_, bf16[2,2048,128]{2,1,0:T(8,128)(2,1)} %get-tuple-element.137.refs_2_, ...), custom_call_target="tpu_custom_call" | custom-call | flops 6600000000 | tf_op jit(solution)/shard_map/attend_back/pallas_call | solution.py:61
  385.2 8.7 %hidden_back.3 = (bf16[1024,1536]{1,0:T(8,128)(2,1)}, bf16[1024,384]{1,0:T(8,128)(2,1)}, f32[512,1536]{1,0:T(8,128)}, f32[2,1,1536]{2,1,0:T(1,128)}, bf16[8,2,12...) custom-call(bf16[512,1536]{1,0:T(8,128)(2,1)} %get-tuple-element.126, ...), custom_call_target="tpu_custom_call", output_to_operand_aliasing={{0}: (9, {}), {1}: (10, {}), {5}: (11, {})} | custom-call | flops 2400000000 | tf_op jit(solution)/shard_map/hidden_back/pallas_call | solution.py:61
  393.9 13.9 %all_to_all.61.refs_6_ = bf16[8,2,128,128]{3,2,1,0:T(8,128)(2,1)} all-to-all(bf16[8,2,128,128]{3,2,1,0:T(8,128)(2,1)} %get-tuple-element.149), channel_id=1, replica_groups=mesh['seq'=8,'head'=4] {'seq'}, dimensions={0} | all-to-all | bytes 1048576 | tf_op jit(solution)/shard_map/all_to_all | solution.py:1035
  413.0 8.4 %turned_products.3 = (bf16[1536,768]{1,0:T(8,128)(2,1)}, f32[8,128]{1,0:T(8,128)}) custom-call(bf16[1024,1536]{1,0:T(8,128)(2,1)} %get-tuple-element.150.refs_0_, bf16[1024,384]{1,0:T(8,128)(2,1)} %get-tuple-element.151.refs_1_, bf16[1024,1536]{1,0:T(8,128)(2,1)} %get-tuple-element.152.refs_2_.refs_0_, bf16[1024,384]{1,0:T(8,128)(2,1)} %get-tuple-element.153.refs_3_.refs_4_, ...), custom_call_target="tpu_custom_call" | custom-call | flops 2400000000 | tf_op jit(solution)/shard_map/turned_products/pallas_call | solution.py:61
  421.4 20.2 %attend_back.4 = (bf16[8,1,256,256]{3,2,1,0:T(8,128)(2,1)}, bf16[1536,768]{1,0:T(8,128)(2,1)}, f32[8,128]{1,0:T(8,128)}) custom-call(bf16[2,2048,128]{2,1,0:T(8,128)(2,1)} %get-tuple-element.135.refs_0_, bf16[2,2048,128]{2,1,0:T(8,128)(2,1)} %get-tuple-element.136.refs_1_, ...), custom_call_target="tpu_custom_call", output_to_operand_aliasing={{1}: (8, {})} | custom-call | flops 6600000000 | tf_op jit(solution)/shard_map/attend_back/pallas_call | solution.py:61
  446.9 20.2 %attend_back.5 = (bf16[8,1,256,256]{3,2,1,0:T(8,128)(2,1)}, bf16[1536,768]{1,0:T(8,128)(2,1)}, f32[8,128]{1,0:T(8,128)}) custom-call(bf16[1,2048,128]{2,1,0:T(8,128)(2,1)} %get-tuple-element.158.refs_0_, bf16[1,2048,128]{2,1,0:T(8,128)(2,1)} %get-tuple-element.159.refs_1_, ...), custom_call_target="tpu_custom_call", output_to_operand_aliasing={{1}: (8, {})} | custom-call | flops 6600000000 | tf_op jit(solution)/shard_map/attend_back/pallas_call | solution.py:61
  479.2 7.6 %all-to-all-done.10 = bf16[8,1,256,256]{3,2,1,0:T(8,128)(2,1)S(1)} async-done(((bf16[8,1,256,256]{3,2,1,0:T(8,128)(2,1)}), bf16[8,1,256,256]{3,2,1,0:T(8,128)(2,1)S(1)}, u32[]{:S(2)}, u32[]{:S(2)}) %all-to-all-start.10) | async-done | bytes 1048608 | tf_op jit(solution)/shard_map/all_to_all | solution.py:1035
  488.0 11.4 %project_back.2 = (bf16[1024,1280]{1,0:T(8,128)(2,1)}, bf16[512,1536]{1,0:T(8,128)(2,1)}, f32[2,1,1920]{2,1,0:T(1,128)}, bf16[1536,768]{1,0:T(8,128)(2,1)}, f32[8,128]{1,0:T(8,128)}) custom-call(s32[1]{0:T(128)S(6)} %convert_element_type.75.refs_0_, bf16[12,256,256]{2,1,0:T(8,128)(2,1)} %pad_maximum_fusion.refs_1_, ...), custom_call_target="tpu_custom_call", output_to_operand_aliasing={{3}: (8, {})} | custom-call | flops 3600000000 | tf_op jit(solution)/shard_map/project_back/pallas_call | solution.py:61
  504.1 11.6 %project_back.3 = (bf16[1024,1280]{1,0:T(8,128)(2,1)}, bf16[2,128,1536]{2,1,0:T(8,128)(2,1)}, bf16[2,128,1536]{2,1,0:T(8,128)(2,1)}, f32[2,1,1920]{2,1,0:T(1,128)}, f32[8,128]{1,0:T(8,128)}) custom-call(s32[1]{0:T(128)S(6)} %convert_element_type.75.refs_0_, bf16[12,256,256]{2,1,0:T(8,128)(2,1)} %pad_maximum_fusion.1.refs_1_, ...), custom_call_target="tpu_custom_call", output_to_operand_aliasing={{0}: (8, {})} | custom-call | flops 3600000000 | tf_op jit(solution)/shard_map/project_back/pallas_call | solution.py:61
  523.1 8.6 %owned_product.1 = (bf16[8,208,1280]{2,1,0:T(8,128)(2,1)}, f32[8,128]{1,0:T(8,128)}) custom-call(bf16[1024,1536]{1,0:T(8,128)(2,1)} %get-tuple-element.152.refs_2_.refs_0_, bf16[1024,1280]{1,0:T(8,128)(2,1)} %get-tuple-element.180.refs_1_, bf16[8,16,1280]{2,1,0:T(8,128)(2,1)} %pad.43.refs_2_, f32[8,128]{1,0:T(8,128)} %get-tuple-element.185.refs_3_), custom_call_target="tpu_custom_call" | custom-call | flops 2700000000 | tf_op jit(solution)/shard_map/owned_product/pallas_call | solution.py:61
  550.2 56.1 %collective-permute-done.10 = bf16[128,1536]{1,0:T(8,128)(2,1)S(1)} collective-permute-done((bf16[128,1536]{1,0:T(8,128)(2,1)S(1)}, bf16[128,1536]{1,0:T(8,128)(2,1)S(1)}, u32[]{:S(2)}, u32[]{:S(2)}) %collective-permute-start.10) | collective-permute-done | bytes 393248 | tf_op jit(solution)/shard_map/ppermute | solution.py:1021
  616.7 8.2 %collective-permute-done.17.refs_5_ = bf16[128,1536]{1,0:T(8,128)(2,1)S(1)} collective-permute-done((bf16[128,1536]{1,0:T(8,128)(2,1)S(1)}, bf16[128,1536]{1,0:T(8,128)(2,1)S(1)}, u32[]{:S(2)}, u32[]{:S(2)}) %collective-permute-start.17) | collective-permute-done | bytes 393248 | tf_op jit(solution)/shard_map/ppermute | solution.py:1025
  (281 shorter events, 214.9 us)
Async XLA Ops:
  7.2 50.3 %all-gather.4.cloned.1.call-start = ((), (), s32[]{:S(2)}) async-start(), calls=%async_computation.14 | async-start | bytes 5750784 | tf_op jit(solution)/shard_map/all_gather | solution.py:1091
  14.2 231.7 %all-gather.8.cloned.1.call-start = ((), (), s32[]{:S(2)}) async-start(), calls=%async_computation.16 | async-start | bytes 10616832 | tf_op jit(solution)/shard_map/all_gather | solution.py:1093
  15.4 230.5 %all-gather.6.cloned.1.call-start = ((), (), s32[]{:S(2)}) async-start(), calls=%async_computation.15 | async-start | bytes 15925248 | tf_op jit(solution)/shard_map/all_gather | solution.py:1150
  18.6 66.4 %collective-permute-start.2 = (bf16[192,1536]{1,0:T(8,128)(2,1)S(1)}, bf16[192,1536]{1,0:T(8,128)(2,1)S(1)}, u32[]{:S(2)}, u32[]{:S(2)}) collective-permute-start(bf16[192,1536]{1,0:T(8,128)(2,1)S(1)} %get-tuple-element.301), channel_id=1, source_target_pairs={{0,2},{1,3},{2,0},{3,1},{4,6},{5,7},{6,4},{7,5},{8,10},{9,11},{10,... | collective-permute-start | bytes 1769480 | tf_op jit(solution)/shard_map/ppermute | solution.py:1031
  21.3 63.7 %collective-permute-start.3 = (bf16[192,1536]{1,0:T(8,128)(2,1)S(1)}, bf16[192,1536]{1,0:T(8,128)(2,1)S(1)}, u32[]{:S(2)}, u32[]{:S(2)}) collective-permute-start(bf16[192,1536]{1,0:T(8,128)(2,1)S(1)} %get-tuple-element.300), channel_id=1, source_target_pairs={{0,2},{1,3},{2,0},{3,1},{4,6},{5,7},{6,4},{7,5},{8,10},{9,11},{10,... | collective-permute-start | bytes 1769480 | tf_op jit(solution)/shard_map/ppermute | solution.py:1031
  24.6 60.4 %collective-permute-start.1 = (bf16[192,768]{1,0:T(8,128)(2,1)S(1)}, bf16[192,768]{1,0:T(8,128)(2,1)S(1)}, u32[]{:S(2)}, u32[]{:S(2)}) collective-permute-start(bf16[192,768]{1,0:T(8,128)(2,1)S(1)} %pad_maximum_fusion.9), channel_id=1, source_target_pairs={{0,2},{1,3},{2,0},{3,1},{4,6},{5,7},{6,4},{7,5},{8,10},{9,11},{10,... | collective-permute-start | bytes 884744 | tf_op jit(solution)/shard_map/ppermute | solution.py:1031
  96.1 43.5 %all-to-all-start = ((bf16[8,2,256,256]{3,2,1,0:T(8,128)(2,1)}), bf16[8,2,256,256]{3,2,1,0:T(8,128)(2,1)S(1)}, u32[]{:S(2)}, u32[]{:S(2)}) async-start(bf16[8,2,256,256]{3,2,1,0:T(8,128)(2,1)} %get-tuple-element.108), calls=%async_computation | async-start | bytes 4194304 | tf_op jit(solution)/shard_map/all_to_all | solution.py:1035
  139.6 29.1 %all-to-all-start.2 = ((bf16[8,1,256,256]{3,2,1,0:T(8,128)(2,1)}), bf16[8,1,256,256]{3,2,1,0:T(8,128)(2,1)S(1)}, u32[]{:S(2)}, u32[]{:S(2)}) async-start(bf16[8,1,256,256]{3,2,1,0:T(8,128)(2,1)} %get-tuple-element.111), calls=%async_computation.2 | async-start | bytes 2097152 | tf_op jit(solution)/shard_map/all_to_all | solution.py:1035
  202.3 38.9 %all-to-all-start.5 = ((bf16[4,512,384]{2,1,0:T(8,128)(2,1)}), bf16[4,512,384]{2,1,0:T(8,128)(2,1)S(1)}, u32[]{:S(2)}, u32[]{:S(2)}) async-start(bf16[4,512,384]{2,1,0:T(8,128)(2,1)} %get-tuple-element.119), calls=%async_computation.5 | async-start | bytes 3145728 | tf_op jit(solution)/shard_map/all_to_all | solution.py:1035
  241.2 43.4 %all-to-all-start.4 = ((bf16[4,512,384]{2,1,0:T(8,128)(2,1)}), bf16[4,512,384]{2,1,0:T(8,128)(2,1)S(1)}, u32[]{:S(2)}, u32[]{:S(2)}) async-start(bf16[4,512,384]{2,1,0:T(8,128)(2,1)} %get-tuple-element.118), calls=%async_computation.4 | async-start | bytes 3145728 | tf_op jit(solution)/shard_map/all_to_all | solution.py:1035
  244.8 243.3 %reduce-scatter.3.cloned.1.call-start = ((), (), s32[]{:S(2)}) async-start(), calls=%async_computation.17 | async-start | bytes 10616832 | tf_op jit(solution)/shard_map/reduce_scatter | solution.py:1207
  282.6 40.3 %collective-permute-start.5 = (bf16[512,1536]{1,0:T(8,128)(2,1)}, bf16[512,1536]{1,0:T(8,128)(2,1)S(1)}, u32[]{:S(2)}, u32[]{:S(2)}) collective-permute-start(bf16[512,1536]{1,0:T(8,128)(2,1)} %get-tuple-element.127.refs_0_), channel_id=1, source_target_pairs={{0,1},{1,0},{2,3},{3,2},{4,5},{5,4},{6,7},{7,6},{8,9},{9,8},{10,11... | collective-permute-start | bytes 4718600 | tf_op jit(solution)/shard_map/ppermute | solution.py:1031
  349.2 34.8 %collective-permute-start.4 = (bf16[512,1536]{1,0:T(8,128)(2,1)S(1)}, bf16[512,1536]{1,0:T(8,128)(2,1)S(1)}, u32[]{:S(2)}, u32[]{:S(2)}) collective-permute-start(bf16[512,1536]{1,0:T(8,128)(2,1)S(1)} %copy-done.15), channel_id=1, source_target_pairs={{0,1},{1,0},{2,3},{3,2},{4,5},{5,4},{6,7},{7,6},{8,9},{9,8},{10,11... | collective-permute-start | bytes 4718600 | tf_op jit(solution)/shard_map/ppermute | solution.py:1031
  407.8 33.8 %all-to-all-start.7 = ((bf16[8,1,256,256]{3,2,1,0:T(8,128)(2,1)}), bf16[8,1,256,256]{3,2,1,0:T(8,128)(2,1)S(1)}, u32[]{:S(2)}, u32[]{:S(2)}) async-start(bf16[8,1,256,256]{3,2,1,0:T(8,128)(2,1)} %get-tuple-element.148), calls=%async_computation.7 | async-start | bytes 2097152 | tf_op jit(solution)/shard_map/all_to_all | solution.py:1035
  411.8 59.8 %collective-permute-start.7 = (bf16[512,1536]{1,0:T(8,128)(2,1)}, bf16[512,1536]{1,0:T(8,128)(2,1)}, u32[]{:S(2)}, u32[]{:S(2)}) collective-permute-start(bf16[512,1536]{1,0:T(8,128)(2,1)} %get-tuple-element.147.refs_1_), channel_id=1, source_target_pairs={{0,1},{1,0},{2,3},{3,2},{4,5},{5,4},{6,7},{7,6},{8,9},{9,8},{10,11... | collective-permute-start | bytes 4718600 | tf_op jit(solution)/shard_map/ppermute | solution.py:1031
  441.6 25.5 %all-to-all-start.9 = ((bf16[8,1,256,256]{3,2,1,0:T(8,128)(2,1)}), bf16[8,1,256,256]{3,2,1,0:T(8,128)(2,1)S(1)}, u32[]{:S(2)}, u32[]{:S(2)}) async-start(bf16[8,1,256,256]{3,2,1,0:T(8,128)(2,1)} %get-tuple-element.157), calls=%async_computation.9 | async-start | bytes 2097152 | tf_op jit(solution)/shard_map/all_to_all | solution.py:1035
  446.0 53.5 %collective-permute-start.6 = (bf16[512,1536]{1,0:T(8,128)(2,1)}, bf16[512,1536]{1,0:T(8,128)(2,1)}, u32[]{:S(2)}, u32[]{:S(2)}) collective-permute-start(bf16[512,1536]{1,0:T(8,128)(2,1)} %get-tuple-element.146.refs_1_), channel_id=1, source_target_pairs={{0,1},{1,0},{2,3},{3,2},{4,5},{5,4},{6,7},{7,6},{8,9},{9,8},{10,11... | collective-permute-start | bytes 4718600 | tf_op jit(solution)/shard_map/ppermute | solution.py:1031
  471.3 166.3 %all-reduce.14.cloned.1.call-start = ((), (), s32[]{:S(2)}) async-start(), calls=%async_computation.18 | async-start | bytes 3145728 | tf_op jit(solution)/shard_map/psum | solution.py:1276
  517.7 21.0 %collective-permute-start.14 = (bf16[128,1536]{1,0:T(8,128)(2,1)S(1)}, bf16[128,1536]{1,0:T(8,128)(2,1)S(1)}, u32[]{:S(2)}, u32[]{:S(2)}) collective-permute-start(bf16[128,1536]{1,0:T(8,128)(2,1)S(1)} %get-tuple-element.289), channel_id=1, source_target_pairs={{0,1},{3,2},{4,5},{7,6},{8,9},{11,10},{12,13},{15,14},{16,17},{19,... | collective-permute-start | bytes 1179656 | tf_op jit(solution)/shard_map/ppermute | solution.py:1021
  520.9 24.9 %collective-permute-start.8 = (bf16[128,1536]{1,0:T(8,128)(2,1)S(1)}, bf16[128,1536]{1,0:T(8,128)(2,1)S(1)}, u32[]{:S(2)}, u32[]{:S(2)}) collective-permute-start(bf16[128,1536]{1,0:T(8,128)(2,1)S(1)} %get-tuple-element.290), channel_id=1, source_target_pairs={{0,1},{3,2},{4,5},{7,6},{8,9},{11,10},{12,13},{15,14},{16,17},{19,... | collective-permute-start | bytes 1179656 | tf_op jit(solution)/shard_map/ppermute | solution.py:1021
  531.7 128.2 %all-to-all-start.11 = ((bf16[8,208,1280]{2,1,0:T(8,128)(2,1)}), bf16[8,208,1280]{2,1,0:T(8,128)(2,1)}, u32[]{:S(2)}, u32[]{:S(2)}) async-start(bf16[8,208,1280]{2,1,0:T(8,128)(2,1)} %get-tuple-element.194), calls=%async_computation.12 | async-start | bytes 8519680 | tf_op jit(solution)/shard_map/all_to_all | solution.py:1035
  536.3 122.6 %reduce-scatter.5.cloned.1.call-start = ((), (), s32[]{:S(2)}) async-start(), calls=%async_computation.19 | async-start | bytes 2654208 | tf_op jit(solution)/shard_map/reduce_scatter | solution.py:1207
  547.5 58.9 %collective-permute-start.10 = (bf16[128,1536]{1,0:T(8,128)(2,1)S(1)}, bf16[128,1536]{1,0:T(8,128)(2,1)S(1)}, u32[]{:S(2)}, u32[]{:S(2)}) collective-permute-start(bf16[128,1536]{1,0:T(8,128)(2,1)S(1)} %get-tuple-element.286), channel_id=1, source_target_pairs={{2,3},{1,0},{6,7},{5,4},{10,11},{9,8},{14,15},{13,12},{18,19},{17,... | collective-permute-start | bytes 1179656 | tf_op jit(solution)/shard_map/ppermute | solution.py:1021
  548.9 64.9 %collective-permute-start.16 = (bf16[128,1536]{1,0:T(8,128)(2,1)S(1)}, bf16[128,1536]{1,0:T(8,128)(2,1)S(1)}, u32[]{:S(2)}, u32[]{:S(2)}) collective-permute-start(bf16[128,1536]{1,0:T(8,128)(2,1)S(1)} %get-tuple-element.285), channel_id=1, source_target_pairs={{2,3},{1,0},{6,7},{5,4},{10,11},{9,8},{14,15},{13,12},{18,19},{17,... | collective-permute-start | bytes 1179656 | tf_op jit(solution)/shard_map/ppermute | solution.py:1021
  (61 other events, 490.9 us)
Sparse Core Ops, SparseCore 0:
  14.3 43.2 all-gather.3
  59.5 75.6 all-gather.7
  137.6 89.9 all-gather.5
  348.0 88.0 reduce-scatter.2
  499.6 90.8 all-reduce.13
  593.7 40.6 reduce-scatter.4

commit v4 on v3

--- a/solution.py
+++ b/solution.py
@@ -70,7 +70,7 @@
             out_shape=out_shape,
             input_output_aliases=aliases,
             compiler_params=params(),
-            cost_estimate=pl.CostEstimate(flops=int(us * 0.3e9), bytes_accessed=0, transcendentals=0),
+            cost_estimate=pl.CostEstimate(flops=int(us * 8e9), bytes_accessed=0, transcendentals=0),
             name=name,
         )(*arrays, *extra)
         self.tokens = [token]
@@ -217,7 +217,7 @@
     row = pl.BlockSpec((1, LANES), whole)
     pairs = -(-micros * heads // owners)
     idle = range(micros * heads, pairs * owners)
-    parts = [pairs - 1, 1] if pairs > 1 else [1]
+    parts = [1] * pairs
     sent = [(owners, part, rows, 2 * LANES) for part in parts]
     return order.call(
         functools.partial(project_kernel, heads, idle),
@@ -309,7 +309,7 @@
         one_block(qi)
 
 
-def attend(order, pay, tail_key, tail_value, first):
+def attend(order, pay, tail_key, tail_value, first, out_places, out_place, before):
     blocks, pairs, rows, _ = pay.shape
     length = blocks * rows
     tail_length = tail_key.shape[1]
@@ -329,16 +329,17 @@
         ],
         [
             (
-                (blocks, pairs, rows // 2, LANES),
+                (blocks, out_places, rows // 2, LANES),
                 BF16,
-                pl.BlockSpec((blocks, 1, rows // 2, LANES), across),
+                pl.BlockSpec((blocks, 1, rows // 2, LANES), lambda j: (0, out_place, 0, 0)),
             ),
             ((pairs, length, LANES), F32, whole),
             ((pairs, length, LANES), BF16, whole),
             ((pairs, length, LANES), BF16, whole),
             ((pairs, length, LANES), BF16, whole),
         ],
-        17 * pairs,
+        14 * pairs,
+        before=before,
     )
 
 
@@ -453,7 +454,7 @@
 
 
 def attend_back(
-    order, saved, tail_key, tail_value, mixture, packed_grad, pay, place, saved_place, grad_place, carry, after
+    order, saved, tail_key, tail_value, mixture, packed_grad, pay, place, saved_place, grad_place, out_places, out_place, before, carry, after
 ):
     blocks, _, rows, _ = pay.shape
     length = blocks * rows
@@ -463,7 +464,8 @@
     tail = pl.BlockSpec((1, tail_length, LANES), pair)
     whole = pl.BlockSpec((1, length, LANES), lambda j: (saved_place, 0, 0))
     grad = pl.BlockSpec((blocks, 1, rows // 2, LANES), lambda j: (0, grad_place, 0, 0))
-    sent = (blocks, 1, rows, 2 * LANES)
+    sent = (blocks, out_places, rows, 2 * LANES)
+    out = pl.BlockSpec((blocks, 1, rows, 2 * LANES), lambda j: (0, out_place, 0, 0))
     return order.call(
         functools.partial(attend_back_kernel, size),
         "attend_back",
@@ -476,16 +478,28 @@
             (packed_grad, grad),
             (pay, pl.BlockSpec((blocks, 1, rows, LANES), lambda j: (0, saved_place, 0, 1))),
         ],
-        [(sent, BF16, pl.BlockSpec(sent, lambda j: (0, 0, 0, 0)))],
+        [(sent, BF16, out)],
         22,
         scratch=[
             pltpu.VMEM((length, LANES), BF16),
             pltpu.VMEM((LANES, length), F32),
             pltpu.VMEM((length, LANES), F32),
         ],
+        before=before,
         carry=carry,
         after=after,
     )
+
+
+def take_pair(refs, pair):
+    owners = refs[0].shape[0]
+    owner, place = lax.rem(pair, owners), lax.div(pair, owners)
+    block, start = None, 0
+    for ref in refs:
+        here = ref[owner, jnp.clip(place - start, 0, ref.shape[1] - 1)]
+        block = here if block is None else jnp.where(place >= start, here, block)
+        start += ref.shape[1]
+    return block
 
 
 def group_of(heads, ref, first_pair, group, low_half):
@@ -781,18 +795,20 @@
 
 def project_back_kernel(
     heads,
+    first,
+    arrays,
     upper_ref,
-    g_ref,
     raw_ref,
     x_ref,
     dgl_ref,
     w_ref,
     gq_ref,
     gk_ref,
-    grads_ref,
     *refs,
 ):
-    *da_refs, sums_ref, all_ref, da_ref = refs
+    g_refs = refs[:arrays]
+    grads_ref, *da_refs, sums_ref, all_ref, da_ref = refs[arrays:]
+    first_pair = (first + pl.program_id(0)) * heads
     rows, cols = dgl_ref.shape
     width = x_ref.shape[1]
     lane = lanes_of(rows)
@@ -812,8 +828,9 @@
         at = group * LANES
         here = slice(at, at + LANES)
         pair = (2 * group, 2 * group + 1)
-        both = [g_ref[h, :, :LANES].astype(F32) if h < heads else zero for h in pair]
-        rest = [g_ref[h, :, LANES:].astype(F32) if h < heads else zero for h in pair]
+        held = [take_pair(g_refs, first_pair + h).astype(F32) if h < heads else None for h in pair]
+        both = [zero if block is None else block[:, :LANES] for block in held]
+        rest = [zero if block is None else block[:, LANES:] for block in held]
         query = head_back(raw_ref[:, here], merge_pair(low, *both), gq_ref[...], 0)
         key = head_back(
             raw_ref[:, cols + at : cols + at + LANES],
@@ -864,18 +881,18 @@
     else:
         da = [((count * rows, width), BF16, pl.BlockSpec((rows, width), lambda i, upper: (i, 0)))]
     return order.call(
-        functools.partial(project_back_kernel, heads),
+        functools.partial(project_back_kernel, heads, first, len(returned)),
         "project_back",
         (count,),
         [
-            (returned, pl.BlockSpec((heads, rows, 2 * LANES), lambda i, upper: (i, 0, 0))),
             (raw, pl.BlockSpec((rows, 2 * cols), here)),
             (x, pl.BlockSpec((rows, width), here)),
             (dgl, pl.BlockSpec((rows, cols), here)),
             (weights, pl.BlockSpec((width, wide), whole)),
             (gq_row, row),
             (gk_row, row),
-        ],
+        ]
+        + [(array, pl.BlockSpec(array.shape, lambda i, upper: (0, 0, 0, 0))) for array in returned],
         [((total, wide - cols), BF16, pl.BlockSpec((rows, wide - cols), here))]
         + da
         + [((count, 1, sums), F32, pl.BlockSpec((1, 1, sums), lambda i, upper: (i, 0, 0)))],
@@ -988,7 +1005,7 @@
         out_ref[i, own:] = sums_ref[i]
 
 
-def owned_product(order, left, right, sums, us):
+def owned_product(order, left, right, sums, us, carry):
     rows, height = left.shape
     owners, extra, wide = sums.shape
     own = height // owners
@@ -1006,7 +1023,8 @@
         ],
         [((owners, own + extra, wide), BF16, pl.BlockSpec((step, own + extra, wide), lambda i: (i, 0, 0)))],
         us,
-    )[0]
+        carry=carry,
+    )
 
 
 def line_steps(count):
@@ -1134,27 +1152,29 @@
         )
     tail_key, tail_value = jnp.stack(tail_key_parts), jnp.stack(tail_value_parts)
 
-    def pairs_of(stages, first_micro, count):
-        low, high = first_micro * heads, (first_micro + count) * heads
-        taken = []
-        for j, stage in enumerate(stages):
-            start, stop = max(low - j * seq_count, 0), min(high - j * seq_count, seq_count)
-            if start < stop:
-                taken.append(stage[start:stop, 0])
-        return jnp.concatenate(taken, axis=0)
-
     a, raw, gl, *pays = project(
         order, heads, cols, seq_count, x, first, bias_row, gain_one_row, gq_row, gk_row, micros, early
     )
     pays = [to_all(pay, "seq") for pay in pays]
-    far = lax.all_gather(pack(order, far_parts), "seq", axis=0, tiled=True)
     kept, returned = [], []
-    at = 0
-    for pay in pays:
-        packed, *saved = attend(order, pay, tail_key, tail_value, at)
-        kept += [(saved, pay, place) for place in range(pay.shape[1])]
-        returned.append(to_all(packed, "seq"))
-        at = len(kept)
+    most = max(pairs - 1, 1)
+    for j, pay in enumerate(pays):
+        in_most = j < most
+        packed, *saved = attend(
+            order,
+            pay,
+            tail_key,
+            tail_value,
+            j,
+            most if in_most else pairs - most,
+            j if in_most else j - most,
+            (packed,) if 0 < j < most else (),
+        )
+        kept.append((saved, pay, 0))
+        if j >= most - 1:
+            returned.append(to_all(packed, "seq"))
+        if j == 0:
+            far = lax.all_gather(pack(order, far_parts), "seq", axis=0, tiled=True)
     packed = jnp.concatenate(returned, axis=1)
 
     size = 2 if micros % 2 == 0 else 1
@@ -1162,7 +1182,7 @@
     chunk = min(512, ff)
     gated, o_alls = (), []
     for g in range(groups):
-        enough = (g + 1) * size * heads <= (pairs - 1) * seq_count
+        enough = (g + 1) * size * heads <= most * seq_count
         *gated, sent = gate(
             order, heads, returned[0] if enough else packed, gl, rows, g * size, size, head_count, gated
         )
@@ -1171,16 +1191,16 @@
 
     hiddens, out_parts, dc_parts, dc_others = [], [], [], []
     dhs, gains_two = [], []
-    late = ()
+    late, carried = (), None
     early_places = size * heads // seq_count if groups > 1 else 0
     fed, backed = (), ()
 
-    def back_to_heads(g):
-        nonlocal backed, late
+    def back_to_heads(g, carry=()):
+        nonlocal backed, late, carried
         places = [(early_places, pairs)]
         if g == 0 and early_places > 0:
             places = [(0, early_places)] + places
-        dhb, dgl, dh, gain, *sent, out_parts[g] = hidden_back(
+        *results, out_parts[g] = hidden_back(
             order,
             heads,
             dc_parts[g],
@@ -1196,8 +1216,11 @@
             places,
             late,
             backed,
-            (out_parts[g],),
+            carry + (out_parts[g],),
         )
+        if carry:
+            carried = results.pop()
+        dhb, dgl, dh, gain, *sent = results
         backed, late = (dhb, dgl), (sent[-1],)
         dhs.append(dh)
         gains_two.append(gain)
@@ -1229,7 +1252,7 @@
     if early_places > 0:
         early_grads = to_all(early_grads, "seq")
     returned = []
-    mixed = ()
+    mixed, grad = (), ()
     for j in range(pairs):
         if j == early_places:
             back_to_heads(groups - 1)
@@ -1237,13 +1260,27 @@
             late_grads = to_all(late[0], "seq")
         sent = (early_grads, j) if j < early_places else (late_grads, j - early_places)
         saved, pay, place = kept[j]
-        waited = tuple(returned[: j - 1]) if j >= 2 else ()
         grad, *mixed = attend_back(
-            order, saved[1:], tail_key, tail_value, saved[0], sent[0], pay, j, place, sent[1], mixed, waited
+            order,
+            saved[1:],
+            tail_key,
+            tail_value,
+            saved[0],
+            sent[0],
+            pay,
+            j,
+            place,
+            sent[1],
+            most if j < most else pairs - most,
+            j if j < most else j - most,
+            (grad,) if 0 < j < most else (),
+            tuple(mixed),
+            (),
         )
-        returned.append(to_all(grad, "seq"))
-
-    put_out(0, tuple(returned[:-1]))
+        if j >= most - 1:
+            returned.append(to_all(grad, "seq"))
+
+    put_out(0)
 
     grads, da_sums, gains_one = (), [], []
     for g in range(groups):
@@ -1252,7 +1289,7 @@
             order,
             heads,
             upper,
-            pairs_of(returned, g * size, size),
+            returned[:1] if (g + 1) * size * heads <= most * seq_count else returned,
             raw,
             x,
             backed[1],
@@ -1275,11 +1312,6 @@
         else:
             total_da = lax.psum(da[0], "head")
             da_sums += [([total_da], i) for i in range(size)]
-        if g == 0:
-            mixed_grads = scattered(mixed[0])
-            mixed = ()
-            for out in range(1, groups):
-                put_out(out)
 
     one_sums = jnp.sum(jnp.concatenate(gains_one, axis=0), axis=0)
     two_sums = jnp.sum(jnp.concatenate(gains_two, axis=0), axis=0) * (1.0 / head_count)
@@ -1294,7 +1326,10 @@
         axis=1,
     ).astype(BF16)
     owned_sums = jnp.pad(owned_sums[:, None], ((0, 0), (0, 15), (0, grads[0].shape[1] - owned_sums.shape[1])))
-    head_grads = owned_product(order, a, grads[0], owned_sums, 9)
+    head_grads, *mixed = owned_product(order, a, grads[0], owned_sums, 9, mixed)
+    mixed_grads = scattered(mixed[0]) if mixed else mixed_grads
+    for out in range(1, groups):
+        put_out(out)
 
     head_grads = jnp.sum(to_all(head_grads, "seq").astype(F32), axis=0)
     sums = head_grads[own_rows : own_rows + 1]

time: 692 us -> 649 us (0.938)
  blocking collectives: 24.2 us -> 0 us
  waiting for transfers between devices: 205 us -> 185 us
    all_to_all x2 -> x0, blocking collectives: 24.2 us -> none  [to_all(): return lax.all_to_all(array, axis, 0, 0, tiled=True)]
    all_gather x1, waiting for transfers between devices: 31.2 us -> 19.8 us  [shards(): first = lax.all_gather(first_shard, 'seq', axis=0, tiled=True)]
    ppermute x10, waiting for transfers between devices: 13.1 us -> 3.86 us  [exchanged(): return lax.ppermute(array, axis, [(i, i ^ flip) for i in range(count)])]
    all_to_all x10 -> x12, starting transfers between devices: 41.4 us -> 47.7 us  [to_all(): return lax.all_to_all(array, axis, 0, 0, tiled=True)]
    pallas_call x24 -> x25, Pallas kernels: 296 us -> 300 us  [call(): pl.pallas_call(linked(kernel, count, len(extra), len(outs), len(carry)),...]
    all_to_all x10 -> x12, waiting for transfers between devices: 68.1 us -> 71.7 us  [to_all(): return lax.all_to_all(array, axis, 0, 0, tiled=True)]
    unnamed x100 -> x80, local copies, waits for them, and re-layouts: 15 us -> 13.2 us
  transfers between devices with their start and end apart: 38 -> 40, of which waited for: 18 -> 19; matrix products, arithmetic and copies ran while one was open for 7% -> 7% of each run, Pallas kernels for 40% -> 47%
where the time goes in v4:
time: 649 us; the launch traced here: 639 us
  Pallas kernels  300 us (46%)
  waiting for transfers between devices  185 us (29%)
  starting transfers between devices  78.2 us (12%)
  local copies, waits for them, and re-layouts  35.3 us (5%)
  other arithmetic  25.2 us (4%)
  between operations  15.6 us (2%)
    pallas_call x25, Pallas kernels, call(): pl.pallas_call(linked(kernel, count, len(extra), len(outs), len(carry)),...  300 us
    all_to_all x12, waiting for transfers between devices, to_all(): return lax.all_to_all(array, axis, 0, 0, tiled=True)  71.7 us
    ppermute x6, waiting for transfers between devices, line_sum(): arrived = lax.ppermute(moving, axis, hops)  66.4 us
    all_to_all x12, starting transfers between devices, to_all(): return lax.all_to_all(array, axis, 0, 0, tiled=True)  47.7 us
    ppermute x6, waiting for transfers between devices, line_sum(): passed.append(lax.ppermute(passed[-1], axis, hops))  22.5 us
    all_gather x1, waiting for transfers between devices, shards(): first = lax.all_gather(first_shard, 'seq', axis=0, tiled=True)  19.8 us
    ppermute x10, starting transfers between devices, exchanged(): return lax.ppermute(array, axis, [(i, i ^ flip) for i in range(count)])  14.6 us
    unnamed x80, local copies, waits for them, and re-layouts  13.2 us
  transfers between devices with their start and end apart: 40, of which 19 were waited for; matrix products, arithmetic and copies ran while one was open for 7% of the time, Pallas kernels for 47%

profile of v4, /device:TPU:0, one launch (start us, length us, event | category | flops | bytes accessed | tf_op | source)
XLA Modules:
  0.0 639.4 jit_solution(1590392686160661846)
XLA Ops:
  37.8 19.8 %all-gather.4.cloned.1.call-done.refs_1_.refs_4_ = bf16[1536,1664]{1,0:T(8,128)(2,1)} async-done(((bf16[192,1664]{1,0:T(8,128)(2,1)}), bf16[1536,1664]{1,0:T(8,128)(2,1)}) %all-gather.4.cloned.1.call-update) | async-done | bytes 5111824 | tf_op jit(solution)/shard_map/all_gather | solution.py:1109
  59.9 17.9 %project.1 = (bf16[1024,1536]{1,0:T(8,128)(2,1)}, f32[1024,768]{1,0:T(8,128)}, f32[1024,384]{1,0:T(8,128)}, bf16[8,1,256,256]{3,2,1,0:T(8,128)(2,1)}, bf16[8,1,2...) custom-call(bf16[1024,1536]{1,0:T(8,128)(2,1)} %bitcast.101, ...), custom_call_target="tpu_custom_call" | custom-call | flops 103999995904 | tf_op jit(solution)/shard_map/project/pallas_call | solution.py:61
  92.8 9.4 %all-to-all-done.refs_0_.refs_7_ = bf16[8,1,256,256]{3,2,1,0:T(8,128)(2,1)S(1)} async-done(((bf16[8,1,256,256]{3,2,1,0:T(8,128)(2,1)}), bf16[8,1,256,256]{3,2,1,0:T(8,128)(2,1)S(1)}, u32[]{:S(2)}, u32[]{:S(2)}) %all-to-all-start) | async-done | bytes 1048608 | tf_op jit(solution)/shard_map/all_to_all | solution.py:1053
  106.0 14.1 %attend.3 = (bf16[8,2,128,128]{3,2,1,0:T(8,128)(2,1)}, f32[1,2048,128]{2,1,0:T(8,128)}, bf16[1,2048,128]{2,1,0:T(8,128)(2,1)}, bf16[1,2048,128]{2,1,0:T(8,128)(2...) custom-call(bf16[8,1,256,256]{3,2,1,0:T(8,128)(2,1)} %copy-done.12, ...), custom_call_target="tpu_custom_call" | custom-call | flops 112000000000 | tf_op jit(solution)/shard_map/attend/pallas_call | solution.py:61
  123.6 8.9 %all-to-all-done.1.refs_0_.refs_7_ = bf16[8,1,256,256]{3,2,1,0:T(8,128)(2,1)S(1)} async-done(((bf16[8,1,256,256]{3,2,1,0:T(8,128)(2,1)}), bf16[8,1,256,256]{3,2,1,0:T(8,128)(2,1)S(1)}, u32[]{:S(2)}, u32[]{:S(2)}) %all-to-all-start.1) | async-done | bytes 1048608 | tf_op jit(solution)/shard_map/all_to_all | solution.py:1053
  136.4 14.1 %attend.4 = (bf16[8,2,128,128]{3,2,1,0:T(8,128)(2,1)}, f32[1,2048,128]{2,1,0:T(8,128)}, bf16[1,2048,128]{2,1,0:T(8,128)(2,1)}, bf16[1,2048,128]{2,1,0:T(8,128)(2...) custom-call(bf16[8,1,256,256]{3,2,1,0:T(8,128)(2,1)} %copy-done.11, ...), custom_call_target="tpu_custom_call", output_to_operand_aliasing={{0}: (3, {})} | custom-call | flops 112000000000 | tf_op jit(solution)/shard_map/attend/pallas_call | solution.py:61
  158.5 13.9 %attend.5 = (bf16[8,1,128,128]{3,2,1,0:T(8,128)(2,1)}, f32[1,2048,128]{2,1,0:T(8,128)}, bf16[1,2048,128]{2,1,0:T(8,128)(2,1)}, bf16[1,2048,128]{2,1,0:T(8,128)(2...) custom-call(bf16[8,1,256,256]{3,2,1,0:T(8,128)(2,1)} %copy-done.13, ...), custom_call_target="tpu_custom_call" | custom-call | flops 112000000000 | tf_op jit(solution)/shard_map/attend/pallas_call | solution.py:61
  193.2 32.1 %all-to-all-done.6.refs_11_ = bf16[4,512,384]{2,1,0:T(8,128)(2,1)S(1)} async-done(((bf16[4,512,384]{2,1,0:T(8,128)(2,1)}), bf16[4,512,384]{2,1,0:T(8,128)(2,1)S(1)}, u32[]{:S(2)}, u32[]{:S(2)}) %all-to-all-start.6) | async-done | bytes 1572896 | tf_op jit(solution)/shard_map/all_to_all | solution.py:1053
  229.9 36.9 %feed.2 = (bf16[1024,1536]{1,0:T(8,128)(2,1)}, bf16[1024,1024]{1,0:T(8,128)(2,1)}, bf16[1024,2048]{1,0:T(8,128)(2,1)}, f32[512,1536]{1,0:T(8,128)}, bf16[512,153...) custom-call(s32[1]{0:T(128)} %bitcast.refs_0_, bf16[1024,1536]{1,0:T(8,128)(2,1)} %bitcast.102, ...), custom_call_target="tpu_custom_call" | custom-call | flops 295999995904 | tf_op jit(solution)/shard_map/feed/pallas_call | solution.py:61
  268.8 37.0 %feed.3 = (bf16[1024,1536]{1,0:T(8,128)(2,1)}, bf16[1024,1024]{1,0:T(8,128)(2,1)}, bf16[1024,2048]{1,0:T(8,128)(2,1)}, f32[512,1536]{1,0:T(8,128)}, bf16[512,153...) custom-call(s32[1]{0:T(128)} %bitcast.refs_0_, ...), custom_call_target="tpu_custom_call", output_to_operand_aliasing={{0}: (12, {}), {1}: (13, {}), {2}: (14, {})} | custom-call | flops 295999995904 | tf_op jit(solution)/shard_map/feed/pallas_call | solution.py:61
  305.9 8.3 %hidden_back.2 = (bf16[1024,1536]{1,0:T(8,128)(2,1)}, bf16[1024,384]{1,0:T(8,128)(2,1)}, f32[512,1536]{1,0:T(8,128)}, f32[2,1,1536]{2,1,0:T(1,128)}, bf16[8,1,12...) custom-call(bf16[512,1536]{1,0:T(8,128)(2,1)} %get-tuple-element.139, ...), custom_call_target="tpu_custom_call", output_to_operand_aliasing={{6}: (8, {})} | custom-call | flops 64000000000 | tf_op jit(solution)/shard_map/hidden_back/pallas_call | solution.py:61
  317.7 15.9 %turned_products.2 = (bf16[1536,3072]{1,0:T(8,128)(2,1)}, f32[8,128]{1,0:T(8,128)}) custom-call(bf16[1024,1536]{1,0:T(8,128)(2,1)} %get-tuple-element.152.refs_0_, bf16[1024,2048]{1,0:T(8,128)(2,1)} %get-tuple-element.153.refs_1_, bf16[1024,1536]{1,0:T(8,128)(2,1)} %bitcast.99, bf16[1024,1024]{1,0:T(8,128)(2,1)} %get-tuple-element.154.refs_3_, ...), custom_call_target="tpu_custom_call" | custom-call | flops 103999995904 | tf_op jit(solution)/shard_map/turned_products/pallas_call | solution.py:61
  337.0 20.1 %attend_back.3 = (bf16[8,2,256,256]{3,2,1,0:T(8,128)(2,1)}, f32[8,128]{1,0:T(8,128)}) custom-call(bf16[1,2048,128]{2,1,0:T(8,128)(2,1)} %get-tuple-element.147.refs_0_, bf16[1,2048,128]{2,1,0:T(8,128)(2,1)} %get-tuple-element.148.refs_1_, bf16[1,2048,128]{2,1,0:T(8,128)(2,1)} %get-tuple-element.149.refs_2_, ...), custom_call_target="tpu_custom_call" | custom-call | flops 176000008192 | tf_op jit(solution)/shard_map/attend_back/pallas_call | solution.py:61
  357.2 8.6 %hidden_back.3 = (bf16[1024,1536]{1,0:T(8,128)(2,1)}, bf16[1024,384]{1,0:T(8,128)(2,1)}, f32[512,1536]{1,0:T(8,128)}, f32[2,1,1536]{2,1,0:T(1,128)}, bf16[8,2,12...) custom-call(bf16[512,1536]{1,0:T(8,128)(2,1)} %get-tuple-element.138, ...), custom_call_target="tpu_custom_call", output_to_operand_aliasing={{0}: (9, {}), {1}: (10, {}), {5}: (11, {})} | custom-call | flops 64000000000 | tf_op jit(solution)/shard_map/hidden_back/pallas_call | solution.py:61
  371.9 8.4 %turned_products.3 = (bf16[1536,768]{1,0:T(8,128)(2,1)}, f32[8,128]{1,0:T(8,128)}) custom-call(bf16[1024,1536]{1,0:T(8,128)(2,1)} %get-tuple-element.170.refs_0_, bf16[1024,384]{1,0:T(8,128)(2,1)} %get-tuple-element.171.refs_1_, bf16[1024,1536]{1,0:T(8,128)(2,1)} %get-tuple-element.172.refs_2_.refs_0_, bf16[1024,384]{1,0:T(8,128)(2,1)} %get-tuple-element.173.refs_3_, ...), custom_call_target="tpu_custom_call" | custom-call | flops 64000000000 | tf_op jit(solution)/shard_map/turned_products/pallas_call | solution.py:61
  386.4 20.2 %attend_back.4 = (bf16[8,2,256,256]{3,2,1,0:T(8,128)(2,1)}, bf16[1536,768]{1,0:T(8,128)(2,1)}, f32[8,128]{1,0:T(8,128)}) custom-call(bf16[1,2048,128]{2,1,0:T(8,128)(2,1)} %get-tuple-element.165.refs_0_, bf16[1,2048,128]{2,1,0:T(8,128)(2,1)} %get-tuple-element.166.refs_1_, ...), custom_call_target="tpu_custom_call", output_to_operand_aliasing={{0}: (8, {}), {1}: (9, {})} | custom-call | flops 176000008192 | tf_op jit(solution)/shard_map/attend_back/pallas_call | solution.py:61
  411.1 20.2 %attend_back.5 = (bf16[8,1,256,256]{3,2,1,0:T(8,128)(2,1)}, bf16[1536,768]{1,0:T(8,128)(2,1)}, f32[8,128]{1,0:T(8,128)}) custom-call(bf16[1,2048,128]{2,1,0:T(8,128)(2,1)} %get-tuple-element.160.refs_0_, bf16[1,2048,128]{2,1,0:T(8,128)(2,1)} %get-tuple-element.161.refs_1_, ...), custom_call_target="tpu_custom_call", output_to_operand_aliasing={{1}: (8, {})} | custom-call | flops 176000008192 | tf_op jit(solution)/shard_map/attend_back/pallas_call | solution.py:61
  443.2 12.1 %project_back.2 = (bf16[1024,1280]{1,0:T(8,128)(2,1)}, bf16[512,1536]{1,0:T(8,128)(2,1)}, f32[2,1,1920]{2,1,0:T(1,128)}, bf16[1536,768]{1,0:T(8,128)(2,1)}, f32[8,128]{1,0:T(8,128)}) custom-call(s32[1]{0:T(128)S(6)} %convert_element_type.75.refs_0_, f32[1024,768]{1,0:T(8,128)} %get-tuple-element.181.refs_1_, ...), custom_call_target="tpu_custom_call", output_to_operand_aliasing={{3}: (8, {})} | custom-call | flops 96000000000 | tf_op jit(solution)/shard_map/project_back/pallas_call | solution.py:61
  459.5 12.2 %project_back.3 = (bf16[1024,1280]{1,0:T(8,128)(2,1)}, bf16[2,128,1536]{2,1,0:T(8,128)(2,1)}, bf16[2,128,1536]{2,1,0:T(8,128)(2,1)}, f32[2,1,1920]{2,1,0:T(1,128...) custom-call(s32[1]{0:T(128)S(6)} %convert_element_type.75.refs_0_, ...), custom_call_target="tpu_custom_call", output_to_operand_aliasing={{0}: (9, {}), {4}: (10, {})} | custom-call | flops 96000000000 | tf_op jit(solution)/shard_map/project_back/pallas_call | solution.py:61
  479.4 8.6 %owned_product.1 = (bf16[8,208,1280]{2,1,0:T(8,128)(2,1)}, bf16[1536,768]{1,0:T(8,128)(2,1)}, f32[8,128]{1,0:T(8,128)}) custom-call(bf16[1024,1536]{1,0:T(8,128)(2,1)} %get-tuple-element.172.refs_2_.refs_0_, bf16[1024,1280]{1,0:T(8,128)(2,1)} %get-tuple-element.190.refs_1_, bf16[8,16,1280]{2,1,0:T(8,128)(2,1)} %pad.43.refs_2_, ...), custom_call_target="tpu_custom_call", output_to_operand_aliasing={{1}: (3, {})} | custom-call | flops 71999995904 | tf_op jit(solution)/shard_map/owned_product/pallas_call | solution.py:61
  494.8 13.9 %collective-permute-done.8 = bf16[128,1536]{1,0:T(8,128)(2,1)S(1)} collective-permute-done((bf16[128,1536]{1,0:T(8,128)(2,1)S(1)}, bf16[128,1536]{1,0:T(8,128)(2,1)S(1)}, u32[]{:S(2)}, u32[]{:S(2)}) %collective-permute-start.8) | collective-permute-done | bytes 393248 | tf_op jit(solution)/shard_map/ppermute | solution.py:1039
  519.9 45.1 %collective-permute-done.10 = bf16[128,1536]{1,0:T(8,128)(2,1)S(1)} collective-permute-done((bf16[128,1536]{1,0:T(8,128)(2,1)S(1)}, bf16[128,1536]{1,0:T(8,128)(2,1)S(1)}, u32[]{:S(2)}, u32[]{:S(2)}) %collective-permute-start.10) | collective-permute-done | bytes 393248 | tf_op jit(solution)/shard_map/ppermute | solution.py:1039
  575.6 6.3 collective-permute-done.17.refs_5_
  596.4 12.0 %collective-permute-done.19.refs_7_ = bf16[128,1536]{1,0:T(8,128)(2,1)S(1)} collective-permute-done((bf16[128,1536]{1,0:T(8,128)(2,1)S(1)}, bf16[128,1536]{1,0:T(8,128)(2,1)S(1)}, u32[]{:S(2)}, u32[]{:S(2)}) %collective-permute-start.19) | collective-permute-done | bytes 393248 | tf_op jit(solution)/shard_map/ppermute | solution.py:1043
  (261 shorter events, 207.8 us)
Async XLA Ops:
  7.2 50.3 %all-gather.4.cloned.1.call-start = ((), (), s32[]{:S(2)}) async-start(), calls=%async_computation.14 | async-start | bytes 5750784 | tf_op jit(solution)/shard_map/all_gather | solution.py:1109
  14.2 215.7 %all-gather.8.cloned.1.call-start = ((), (), s32[]{:S(2)}) async-start(), calls=%async_computation.16 | async-start | bytes 10616832 | tf_op jit(solution)/shard_map/all_gather | solution.py:1111
  14.2 45.7 %collective-permute-start = (bf16[192,384]{1,0:T(8,128)(2,1)}, bf16[192,384]{1,0:T(8,128)(2,1)}, u32[]{:S(2)}, u32[]{:S(2)}) collective-permute-start(bf16[192,384]{1,0:T(8,128)(2,1)} %bitcast.79), channel_id=1, source_target_pairs={{0,1},{1,0},{2,3},{3,2},{4,5},{5,4},{6,7},{7,6},{8,9},{9,8},{10,11... | collective-permute-start | bytes 442376 | tf_op jit(solution)/shard_map/ppermute | solution.py:1049
  19.7 100.4 %collective-permute-start.2 = (bf16[192,1536]{1,0:T(8,128)(2,1)}, bf16[192,1536]{1,0:T(8,128)(2,1)}, u32[]{:S(2)}, u32[]{:S(2)}) collective-permute-start(bf16[192,1536]{1,0:T(8,128)(2,1)} %get-tuple-element.317), channel_id=1, source_target_pairs={{0,2},{1,3},{2,0},{3,1},{4,6},{5,7},{6,4},{7,5},{8,10},{9,11},{10,... | collective-permute-start | bytes 1769480 | tf_op jit(solution)/shard_map/ppermute | solution.py:1049
  22.3 97.9 %collective-permute-start.3 = (bf16[192,1536]{1,0:T(8,128)(2,1)}, bf16[192,1536]{1,0:T(8,128)(2,1)}, u32[]{:S(2)}, u32[]{:S(2)}) collective-permute-start(bf16[192,1536]{1,0:T(8,128)(2,1)} %get-tuple-element.316), channel_id=1, source_target_pairs={{0,2},{1,3},{2,0},{3,1},{4,6},{5,7},{6,4},{7,5},{8,10},{9,11},{10,... | collective-permute-start | bytes 1769480 | tf_op jit(solution)/shard_map/ppermute | solution.py:1049
  77.8 24.4 %all-to-all-start = ((bf16[8,1,256,256]{3,2,1,0:T(8,128)(2,1)}), bf16[8,1,256,256]{3,2,1,0:T(8,128)(2,1)S(1)}, u32[]{:S(2)}, u32[]{:S(2)}) async-start(bf16[8,1,256,256]{3,2,1,0:T(8,128)(2,1)} %get-tuple-element.115), calls=%async_computation | async-start | bytes 2097152 | tf_op jit(solution)/shard_map/all_to_all | solution.py:1053
  89.7 30.4 %collective-permute-start.1 = (bf16[192,768]{1,0:T(8,128)(2,1)S(1)}, bf16[192,768]{1,0:T(8,128)(2,1)S(1)}, u32[]{:S(2)}, u32[]{:S(2)}) collective-permute-start(bf16[192,768]{1,0:T(8,128)(2,1)S(1)} %pad_maximum_fusion.7), channel_id=1, source_target_pairs={{0,2},{1,3},{2,0},{3,1},{4,6},{5,7},{6,4},{7,5},{8,10},{9,11},{10,... | collective-permute-start | bytes 884744 | tf_op jit(solution)/shard_map/ppermute | solution.py:1049
  102.1 30.4 %all-to-all-start.1 = ((bf16[8,1,256,256]{3,2,1,0:T(8,128)(2,1)}), bf16[8,1,256,256]{3,2,1,0:T(8,128)(2,1)S(1)}, u32[]{:S(2)}, u32[]{:S(2)}) async-start(bf16[8,1,256,256]{3,2,1,0:T(8,128)(2,1)} %get-tuple-element.119), calls=%async_computation.1 | async-start | bytes 2097152 | tf_op jit(solution)/shard_map/all_to_all | solution.py:1053
  105.7 124.1 %all-gather.6.cloned.1.call-start = ((), (), s32[]{:S(2)}) async-start(), calls=%async_computation.15 | async-start | bytes 15925248 | tf_op jit(solution)/shard_map/all_gather | solution.py:1177
  185.0 40.3 %all-to-all-start.6 = ((bf16[4,512,384]{2,1,0:T(8,128)(2,1)}), bf16[4,512,384]{2,1,0:T(8,128)(2,1)S(1)}, u32[]{:S(2)}, u32[]{:S(2)}) async-start(bf16[4,512,384]{2,1,0:T(8,128)(2,1)} %get-tuple-element.131), calls=%async_computation.6 | async-start | bytes 3145728 | tf_op jit(solution)/shard_map/all_to_all | solution.py:1053
  225.3 43.5 %all-to-all-start.5 = ((bf16[4,512,384]{2,1,0:T(8,128)(2,1)}), bf16[4,512,384]{2,1,0:T(8,128)(2,1)}, u32[]{:S(2)}, u32[]{:S(2)}) async-start(bf16[4,512,384]{2,1,0:T(8,128)(2,1)} %get-tuple-element.130), calls=%async_computation.5 | async-start | bytes 3145728 | tf_op jit(solution)/shard_map/all_to_all | solution.py:1053
  266.7 39.2 %collective-permute-start.5 = (bf16[512,1536]{1,0:T(8,128)(2,1)}, bf16[512,1536]{1,0:T(8,128)(2,1)}, u32[]{:S(2)}, u32[]{:S(2)}) collective-permute-start(bf16[512,1536]{1,0:T(8,128)(2,1)} %get-tuple-element.139.refs_0_), channel_id=1, source_target_pairs={{0,1},{1,0},{2,3},{3,2},{4,5},{5,4},{6,7},{7,6},{8,9},{9,8},{10,11... | collective-permute-start | bytes 4718600 | tf_op jit(solution)/shard_map/ppermute | solution.py:1049
  305.8 51.3 %collective-permute-start.4 = (bf16[512,1536]{1,0:T(8,128)(2,1)}, bf16[512,1536]{1,0:T(8,128)(2,1)}, u32[]{:S(2)}, u32[]{:S(2)}) collective-permute-start(bf16[512,1536]{1,0:T(8,128)(2,1)} %get-tuple-element.138.refs_0_), channel_id=1, source_target_pairs={{0,1},{1,0},{2,3},{3,2},{4,5},{5,4},{6,7},{7,6},{8,9},{9,8},{10,11... | collective-permute-start | bytes 4718600 | tf_op jit(solution)/shard_map/ppermute | solution.py:1049
  314.3 22.0 %all-to-all-start.7 = ((bf16[8,1,128,128]{3,2,1,0:T(8,128)(2,1)}), bf16[8,1,128,128]{3,2,1,0:T(8,128)(2,1)S(1)}, u32[]{:S(2)}, u32[]{:S(2)}) async-start(bf16[8,1,128,128]{3,2,1,0:T(8,128)(2,1)} %get-tuple-element.151), calls=%async_computation.7 | async-start | bytes 524288 | tf_op jit(solution)/shard_map/all_to_all | solution.py:1053
  317.7 125.5 %reduce-scatter.3.cloned.1.call-start = ((), (), s32[]{:S(2)}) async-start(), calls=%async_computation.17 | async-start | bytes 10616832 | tf_op jit(solution)/shard_map/reduce_scatter | solution.py:1230
  333.6 97.7 %collective-permute-start.7 = (bf16[512,1536]{1,0:T(8,128)(2,1)}, bf16[512,1536]{1,0:T(8,128)(2,1)}, u32[]{:S(2)}, u32[]{:S(2)}) collective-permute-start(bf16[512,1536]{1,0:T(8,128)(2,1)} %get-tuple-element.159.refs_1_), channel_id=1, source_target_pairs={{0,1},{1,0},{2,3},{3,2},{4,5},{5,4},{6,7},{7,6},{8,9},{9,8},{10,11... | collective-permute-start | bytes 4718600 | tf_op jit(solution)/shard_map/ppermute | solution.py:1049
  371.3 138.8 %collective-permute-start.6 = (bf16[512,1536]{1,0:T(8,128)(2,1)}, bf16[512,1536]{1,0:T(8,128)(2,1)}, u32[]{:S(2)}, u32[]{:S(2)}) collective-permute-start(bf16[512,1536]{1,0:T(8,128)(2,1)} %get-tuple-element.158.refs_1_), channel_id=1, source_target_pairs={{0,1},{1,0},{2,3},{3,2},{4,5},{5,4},{6,7},{7,6},{8,9},{9,8},{10,11... | collective-permute-start | bytes 4718600 | tf_op jit(solution)/shard_map/ppermute | solution.py:1049
  406.5 33.0 %all-to-all-start.9 = ((bf16[8,2,256,256]{3,2,1,0:T(8,128)(2,1)}), bf16[8,2,256,256]{3,2,1,0:T(8,128)(2,1)}, u32[]{:S(2)}, u32[]{:S(2)}) async-start(bf16[8,2,256,256]{3,2,1,0:T(8,128)(2,1)} %get-tuple-element.182), calls=%async_computation.9 | async-start | bytes 4194304 | tf_op jit(solution)/shard_map/all_to_all | solution.py:1053
  443.1 144.4 %all-reduce.14.cloned.1.call-start = ((), (), s32[]{:S(2)}) async-start(), calls=%async_computation.18 | async-start | bytes 3145728 | tf_op jit(solution)/shard_map/psum | solution.py:1313
  477.2 31.4 %collective-permute-start.8 = (bf16[128,1536]{1,0:T(8,128)(2,1)S(1)}, bf16[128,1536]{1,0:T(8,128)(2,1)S(1)}, u32[]{:S(2)}, u32[]{:S(2)}) collective-permute-start(bf16[128,1536]{1,0:T(8,128)(2,1)S(1)} %get-tuple-element.306), channel_id=1, source_target_pairs={{0,1},{3,2},{4,5},{7,6},{8,9},{11,10},{12,13},{15,14},{16,17},{19,... | collective-permute-start | bytes 1179656 | tf_op jit(solution)/shard_map/ppermute | solution.py:1039
  488.0 131.0 %all-to-all-start.11 = ((bf16[8,208,1280]{2,1,0:T(8,128)(2,1)}), bf16[8,208,1280]{2,1,0:T(8,128)(2,1)}, u32[]{:S(2)}, u32[]{:S(2)}) async-start(bf16[8,208,1280]{2,1,0:T(8,128)(2,1)} %get-tuple-element.212), calls=%async_computation.12 | async-start | bytes 8519680 | tf_op jit(solution)/shard_map/all_to_all | solution.py:1053
  492.6 125.3 %reduce-scatter.5.cloned.1.call-start = ((), (), s32[]{:S(2)}) async-start(), calls=%async_computation.19 | async-start | bytes 2654208 | tf_op jit(solution)/shard_map/reduce_scatter | solution.py:1230
  516.1 48.9 %collective-permute-start.10 = (bf16[128,1536]{1,0:T(8,128)(2,1)S(1)}, bf16[128,1536]{1,0:T(8,128)(2,1)S(1)}, u32[]{:S(2)}, u32[]{:S(2)}) collective-permute-start(bf16[128,1536]{1,0:T(8,128)(2,1)S(1)} %get-tuple-element.302), channel_id=1, source_target_pairs={{2,3},{1,0},{6,7},{5,4},{10,11},{9,8},{14,15},{13,12},{18,19},{17,... | collective-permute-start | bytes 1179656 | tf_op jit(solution)/shard_map/ppermute | solution.py:1039
  517.4 53.3 %collective-permute-start.16 = (bf16[128,1536]{1,0:T(8,128)(2,1)S(1)}, bf16[128,1536]{1,0:T(8,128)(2,1)S(1)}, u32[]{:S(2)}, u32[]{:S(2)}) collective-permute-start(bf16[128,1536]{1,0:T(8,128)(2,1)S(1)} %get-tuple-element.301), channel_id=1, source_target_pairs={{2,3},{1,0},{6,7},{5,4},{10,11},{9,8},{14,15},{13,12},{18,19},{17,... | collective-permute-start | bytes 1179656 | tf_op jit(solution)/shard_map/ppermute | solution.py:1039
  (53 other events, 481.8 us)
Sparse Core Ops, SparseCore 0:
  14.3 43.2 all-gather.3
  59.5 74.8 all-gather.7
  136.9 87.3 all-gather.5
  333.8 85.7 reduce-scatter.2
  472.8 89.3 all-reduce.13
  565.3 41.8 reduce-scatter.4

commit v5 on v4

--- a/solution.py
+++ b/solution.py
@@ -850,15 +850,11 @@
     grads_ref[:, : 3 * cols] = all_ref[:, : 3 * cols]
     grads_ref[:, 3 * cols :] = all_ref[:, 4 * cols :]
     da = dot(all_ref[...], w_ref[...], NT)
-    if len(da_refs) == 1:
-        da_refs[0][...] = da.astype(BF16)
-    else:
-        da_ref[...] = da
-        half = rows // 2
-        upper = upper_ref[0]
-        for ref, part in zip(da_refs, (upper, 1 - upper)):
-            ref[0] = da_ref[pl.ds(pl.multiple_of(part * half, half), half), :].astype(BF16)
-
+    da_ref[...] = da
+    half = rows // 2
+    upper = upper_ref[0]
+    for ref, part in zip(da_refs, (upper, 1 - upper)):
+        ref[0] = da_ref[pl.ds(pl.multiple_of(part * half, half), half), :].astype(BF16)
     x = x_ref[...].astype(F32)
     sums_ref[0, :, :width] = jnp.sum(da * x * rms_factor(x), axis=0, keepdims=True)
     sums_ref[0, :, width : width + LANES] = sums[0]
@@ -867,7 +863,7 @@
 
 
 def project_back(
-    order, heads, upper, returned, raw, x, dgl, weights, gq_row, gk_row, rows, first, count, halves, before, after, carry
+    order, heads, upper, returned, raw, x, dgl, weights, gq_row, gk_row, rows, first, count, before, after, carry
 ):
     total, cols = dgl.shape
     width, wide = weights.shape
@@ -876,10 +872,7 @@
     here = lambda i, upper: (first + i, 0)
     row = pl.BlockSpec((1, LANES), whole)
     sums = width + 3 * LANES
-    if halves:
-        da = [((count, half, width), BF16, pl.BlockSpec((1, half, width), lambda i, upper: (i, 0, 0)))] * 2
-    else:
-        da = [((count * rows, width), BF16, pl.BlockSpec((rows, width), lambda i, upper: (i, 0)))]
+    da = [((count, half, width), BF16, pl.BlockSpec((1, half, width), lambda i, upper: (i, 0, 0)))] * 2
     return order.call(
         functools.partial(project_back_kernel, heads, first, len(returned)),
         "project_back",
@@ -908,29 +901,28 @@
 def input_back_kernel(rank_ref, x_ref, dh_ref, gain_ref, own_ref, *refs):
     *passed, out_ref = refs
     rank, count = rank_ref[0], len(passed) + 1
-    da = own_ref[...].astype(F32)
+    da = own_ref[0].astype(F32)
     for t, ref in enumerate(passed):
-        taken = jnp.where(pl.program_id(0) == 0, rank == t + 1, rank == count - 2 - t)
-        da = jnp.where(taken, ref[...].astype(F32), da)
+        taken = jnp.where(pl.program_id(1) == 0, rank == t + 1, rank == count - 2 - t)
+        da = jnp.where(taken, ref[0].astype(F32), da)
     x = x_ref[...].astype(F32)
     out_ref[...] = dh_ref[...] + norm_back(x, rms_factor(x), gain_ref[...], da)
 
 
-def input_back(order, rank, summed, place, x, dh, dh_place, gain_row, rows, micro, before, after):
+def input_back(order, rank, summed, x, dh, gain_row, rows, first, before, after):
     total, width = x.shape
-    half = rows // 2
-    here = pl.BlockSpec((half, width), lambda i, rank: (2 * micro + i, 0))
-    one = pl.BlockSpec((half, width), lambda i, rank: (2 * place + i, 0))
-    mine = pl.BlockSpec((half, width), lambda i, rank: (2 * dh_place + i, 0))
-    passing = pl.BlockSpec((half, width), lambda i, rank: (0, 0))
+    size, half, _ = summed[0].shape
+    here = pl.BlockSpec((half, width), lambda m, i, rank: (2 * (first + m) + i, 0))
+    one = pl.BlockSpec((half, width), lambda m, i, rank: (2 * m + i, 0))
+    passing = pl.BlockSpec((1, half, width), lambda m, i, rank: (m, 0, 0))
     return order.call(
         input_back_kernel,
         "input_back",
-        (2,),
-        [(x, here), (dh, mine), (gain_row, pl.BlockSpec((1, width), lambda i, rank: (0, 0)))]
-        + [(block, one if len(summed) == 1 else passing) for block in summed],
+        (size, 2),
+        [(x, here), (dh, one), (gain_row, pl.BlockSpec((1, width), lambda m, i, rank: (0, 0)))]
+        + [(block, passing) for block in summed],
         [((total, width), F32, here)],
-        4,
+        4 * size,
         before=before,
         scalars=(rank,),
         after=after,
@@ -1031,17 +1023,25 @@
     return [((t - 1, t), (count - t, count - 1 - t)) for t in range(1, count)]
 
 
-def line_sum(kept, sent, axis):
-    count = lax.axis_size(axis)
-    steps = line_steps(count)
-    moving = sent
-    for t, hops in enumerate(steps):
-        arrived = lax.ppermute(moving, axis, hops)
-        moving = arrived + (sent if t + 2 <= count // 2 else kept)
-    passed = [moving]
-    for hops in steps:
-        passed.append(lax.ppermute(passed[-1], axis, hops))
-    return passed
+def fold_kernel(*refs):
+    count = len(refs) // 3
+    for i in range(count):
+        total = refs[2 * i][...].astype(F32) + refs[2 * i + 1][...].astype(F32)
+        refs[2 * count + i][...] = total.astype(BF16)
+
+
+def fold(order, pairs, after):
+    size, rows, width = pairs[0][0].shape
+    block = pl.BlockSpec((1, rows, width), lambda i: (i, 0, 0))
+    return order.call(
+        fold_kernel,
+        "fold",
+        (size,),
+        [(array, block) for pair in pairs for array in pair],
+        [((size, rows, width), BF16, block) for _ in pairs],
+        0.2 * len(pairs),
+        after=after,
+    )
 
 
 def exchanged(array, axis, flip):
@@ -1280,11 +1280,11 @@
         if j >= most - 1:
             returned.append(to_all(grad, "seq"))
 
-    put_out(0)
-
-    grads, da_sums, gains_one = (), [], []
+    for out in range(groups):
+        put_out(out)
+
+    grads, streams, gains_one = (), [], []
     for g in range(groups):
-        last = g == groups - 1
         results = project_back(
             order,
             heads,
@@ -1299,37 +1299,50 @@
             rows,
             g * size,
             size,
-            last,
             grads,
             (unit_grads,) if g == 0 else (),
             mixed,
         )
-        count = 2 if last else 1
-        grads, da, gain, mixed = results[:1], results[1 : 1 + count], results[1 + count], results[2 + count :]
+        grads, da, gain, mixed = results[:1], results[1:3], results[3], results[4:]
         gains_one.append(gain)
-        if last:
-            da_sums += [(line_sum(da[0][i], da[1][i], "head"), 0) for i in range(size)]
-        else:
-            total_da = lax.psum(da[0], "head")
-            da_sums += [([total_da], i) for i in range(size)]
-
-    one_sums = jnp.sum(jnp.concatenate(gains_one, axis=0), axis=0)
-    two_sums = jnp.sum(jnp.concatenate(gains_two, axis=0), axis=0) * (1.0 / head_count)
-    own_rows = gain_one.shape[0]
-    shared = pad_to(one_sums[:, width:], 3 * LANES, 1)
-    owned_sums = jnp.concatenate(
-        [
-            one_sums[:, :width].reshape(seq_count, own_rows),
-            two_sums.reshape(seq_count, own_rows),
-            jnp.broadcast_to(shared, (seq_count, 3 * LANES)),
-        ],
-        axis=1,
-    ).astype(BF16)
-    owned_sums = jnp.pad(owned_sums[:, None], ((0, 0), (0, 15), (0, grads[0].shape[1] - owned_sums.shape[1])))
-    head_grads, *mixed = owned_product(order, a, grads[0], owned_sums, 9, mixed)
-    mixed_grads = scattered(mixed[0]) if mixed else mixed_grads
-    for out in range(1, groups):
-        put_out(out)
+        streams.append(da)
+
+    hops = line_steps(head_count)
+    moving = [sent for _, sent in streams]
+    passed = [[] for _ in streams]
+    for step in range(1, head_count + groups - 1):
+        active = [(g, step - g) for g in range(groups) if 1 <= step - g < head_count]
+        terms = []
+        for g, t in active:
+            kept, sent = streams[g]
+            terms.append((lax.ppermute(moving[g], "head", hops[t - 1]), sent if t < head_count // 2 else kept))
+        waited = tuple(blocks[-1] for blocks in passed if len(blocks) > 1)
+        for (g, t), total_now in zip(active, fold(order, terms, waited)):
+            moving[g] = total_now
+            if t == head_count - 1:
+                passed[g].append(total_now)
+        if step == 1:
+            one_sums = jnp.sum(jnp.concatenate(gains_one, axis=0), axis=0)
+            two_sums = jnp.sum(jnp.concatenate(gains_two, axis=0), axis=0) * (1.0 / head_count)
+            own_rows = gain_one.shape[0]
+            shared = pad_to(one_sums[:, width:], 3 * LANES, 1)
+            owned_sums = jnp.concatenate(
+                [
+                    one_sums[:, :width].reshape(seq_count, own_rows),
+                    two_sums.reshape(seq_count, own_rows),
+                    jnp.broadcast_to(shared, (seq_count, 3 * LANES)),
+                ],
+                axis=1,
+            ).astype(BF16)
+            owned_sums = jnp.pad(owned_sums[:, None], ((0, 0), (0, 15), (0, grads[0].shape[1] - owned_sums.shape[1])))
+            head_grads, *mixed = owned_product(order, a, grads[0], owned_sums, 9, mixed)
+            mixed_grads = scattered(mixed[0]) if mixed else mixed_grads
+        for g in range(groups):
+            if passed[g] and len(passed[g]) <= head_count - 1:
+                passed[g].append(lax.ppermute(passed[g][-1], "head", hops[len(passed[g]) - 1]))
+    for blocks in passed:
+        while len(blocks) < head_count:
+            blocks.append(lax.ppermute(blocks[-1], "head", hops[len(blocks) - 1]))
 
     head_grads = jnp.sum(to_all(head_grads, "seq").astype(F32), axis=0)
     sums = head_grads[own_rows : own_rows + 1]
@@ -1352,10 +1365,18 @@
     bias_total = sums[bias_at:]
 
     input_grad = ()
-    for m in range(micros):
-        summed, place = da_sums[m]
+    for g in range(groups):
         input_grad = input_back(
-            order, rank, summed, place, x, dhs[m // size], m % size, gain_one_row, rows, m, input_grad, ()
+            order,
+            rank,
+            passed[g],
+            x,
+            dhs[g],
+            gain_one_row,
+            rows,
+            g * size,
+            input_grad,
+            (sums[None],) if g == groups - 1 else (),
         )
 
     input_grad, layer_out = input_grad[0], layer_out[0]

time: 649 us -> 637 us (0.982)
  waiting for transfers between devices: 185 us -> 150 us
  starting transfers between devices: 78.2 us -> 92.8 us
  Pallas kernels: 300 us -> 310 us
    ppermute x12, waiting for transfers between devices: 88.9 us -> 55.7 us  [the longest x6 29.6 us: shards(): lax.ppermute(moving[g], 'head', hops[t - 1])]
    pallas_call x25 -> x27, Pallas kernels: 300 us -> 310 us  [call(): pl.pallas_call(linked(kernel, count, len(extra), len(outs), len(carry)),...]
    ppermute x12, starting transfers between devices: 15.4 us -> 22.9 us  [the longest x3 10.3 us: shards(): lax.ppermute(passed[g][-1], 'head', hops[len(passed[g]) - 1])]
  transfers between devices with their start and end apart: 40 -> 39, of which waited for: 19 -> 16; matrix products, arithmetic and copies ran while one was open for 7% -> 7% of each run, Pallas kernels for 47% -> 48%
where the time goes in v5:
time: 637 us; the launch traced here: 628 us
  Pallas kernels  310 us (49%)
  waiting for transfers between devices  150 us (24%)
  starting transfers between devices  92.8 us (15%)
  local copies, waits for them, and re-layouts  36.5 us (6%)
  other arithmetic  24.2 us (4%)
  between operations  15.2 us (2%)
    pallas_call x27, Pallas kernels, call(): pl.pallas_call(linked(kernel, count, len(extra), len(outs), len(carry)),...  310 us
    all_to_all x12, waiting for transfers between devices, to_all(): return lax.all_to_all(array, axis, 0, 0, tiled=True)  65.9 us
    all_to_all x12, starting transfers between devices, to_all(): return lax.all_to_all(array, axis, 0, 0, tiled=True)  48.6 us
    ppermute x6, waiting for transfers between devices, shards(): lax.ppermute(moving[g], 'head', hops[t - 1])  29.6 us
    ppermute x10, starting transfers between devices, exchanged(): return lax.ppermute(array, axis, [(i, i ^ flip) for i in range(count)])  21 us
    all_gather x1, waiting for transfers between devices, shards(): first = lax.all_gather(first_shard, 'seq', axis=0, tiled=True)  19.8 us
    ppermute x3, waiting for transfers between devices, shards(): lax.ppermute(passed[g][-1], 'head', hops[len(passed[g]) - 1])  19.8 us
    unnamed x80, local copies, waits for them, and re-layouts  15.5 us
  transfers between devices with their start and end apart: 39, of which 16 were waited for; matrix products, arithmetic and copies ran while one was open for 7% of the time, Pallas kernels for 48%

profile of v5, /device:TPU:0, one launch (start us, length us, event | category | flops | bytes accessed | tf_op | source)
XLA Modules:
  0.0 628.5 jit_solution(7572962223248003846)
XLA Ops:
  37.8 19.8 %all-gather.4.cloned.1.call-done.refs_1_.refs_4_ = bf16[1536,1664]{1,0:T(8,128)(2,1)} async-done(((bf16[192,1664]{1,0:T(8,128)(2,1)}), bf16[1536,1664]{1,0:T(8,128)(2,1)}) %all-gather.4.cloned.1.call-update) | async-done | bytes 5111824 | tf_op jit(solution)/shard_map/all_gather | solution.py:1109
  59.9 17.9 %project.1 = (bf16[1024,1536]{1,0:T(8,128)(2,1)}, f32[1024,768]{1,0:T(8,128)}, f32[1024,384]{1,0:T(8,128)}, bf16[8,1,256,256]{3,2,1,0:T(8,128)(2,1)}, bf16[8,1,2...) custom-call(bf16[1024,1536]{1,0:T(8,128)(2,1)} %bitcast.87, ...), custom_call_target="tpu_custom_call" | custom-call | flops 103999995904 | tf_op jit(solution)/shard_map/project/pallas_call | solution.py:61
  92.8 9.3 %all-to-all-done.refs_0_.refs_7_ = bf16[8,1,256,256]{3,2,1,0:T(8,128)(2,1)S(1)} async-done(((bf16[8,1,256,256]{3,2,1,0:T(8,128)(2,1)}), bf16[8,1,256,256]{3,2,1,0:T(8,128)(2,1)S(1)}, u32[]{:S(2)}, u32[]{:S(2)}) %all-to-all-start) | async-done | bytes 1048608 | tf_op jit(solution)/shard_map/all_to_all | solution.py:1053
  105.9 14.1 %attend.3 = (bf16[8,2,128,128]{3,2,1,0:T(8,128)(2,1)}, f32[1,2048,128]{2,1,0:T(8,128)}, bf16[1,2048,128]{2,1,0:T(8,128)(2,1)}, bf16[1,2048,128]{2,1,0:T(8,128)(2...) custom-call(bf16[8,1,256,256]{3,2,1,0:T(8,128)(2,1)} %copy-done.10, ...), custom_call_target="tpu_custom_call" | custom-call | flops 112000000000 | tf_op jit(solution)/shard_map/attend/pallas_call | solution.py:61
  123.6 8.9 %all-to-all-done.1.refs_0_.refs_7_ = bf16[8,1,256,256]{3,2,1,0:T(8,128)(2,1)S(1)} async-done(((bf16[8,1,256,256]{3,2,1,0:T(8,128)(2,1)}), bf16[8,1,256,256]{3,2,1,0:T(8,128)(2,1)S(1)}, u32[]{:S(2)}, u32[]{:S(2)}) %all-to-all-start.1) | async-done | bytes 1048608 | tf_op jit(solution)/shard_map/all_to_all | solution.py:1053
  136.3 14.1 %attend.4 = (bf16[8,2,128,128]{3,2,1,0:T(8,128)(2,1)}, f32[1,2048,128]{2,1,0:T(8,128)}, bf16[1,2048,128]{2,1,0:T(8,128)(2,1)}, bf16[1,2048,128]{2,1,0:T(8,128)(2...) custom-call(bf16[8,1,256,256]{3,2,1,0:T(8,128)(2,1)} %copy-done.9, ...), custom_call_target="tpu_custom_call", output_to_operand_aliasing={{0}: (3, {})} | custom-call | flops 112000000000 | tf_op jit(solution)/shard_map/attend/pallas_call | solution.py:61
  158.4 13.9 %attend.5 = (bf16[8,1,128,128]{3,2,1,0:T(8,128)(2,1)}, f32[1,2048,128]{2,1,0:T(8,128)}, bf16[1,2048,128]{2,1,0:T(8,128)(2,1)}, bf16[1,2048,128]{2,1,0:T(8,128)(2...) custom-call(bf16[8,1,256,256]{3,2,1,0:T(8,128)(2,1)} %copy-done.11, ...), custom_call_target="tpu_custom_call" | custom-call | flops 112000000000 | tf_op jit(solution)/shard_map/attend/pallas_call | solution.py:61
  193.2 32.1 %all-to-all-done.6.refs_11_ = bf16[4,512,384]{2,1,0:T(8,128)(2,1)S(1)} async-done(((bf16[4,512,384]{2,1,0:T(8,128)(2,1)}), bf16[4,512,384]{2,1,0:T(8,128)(2,1)S(1)}, u32[]{:S(2)}, u32[]{:S(2)}) %all-to-all-start.6) | async-done | bytes 1572896 | tf_op jit(solution)/shard_map/all_to_all | solution.py:1053
  229.8 36.9 %feed.2 = (bf16[1024,1536]{1,0:T(8,128)(2,1)}, bf16[1024,1024]{1,0:T(8,128)(2,1)}, bf16[1024,2048]{1,0:T(8,128)(2,1)}, f32[512,1536]{1,0:T(8,128)}, bf16[512,153...) custom-call(s32[1]{0:T(128)} %bitcast.refs_0_, bf16[1024,1536]{1,0:T(8,128)(2,1)} %bitcast.88, ...), custom_call_target="tpu_custom_call" | custom-call | flops 295999995904 | tf_op jit(solution)/shard_map/feed/pallas_call | solution.py:61
  268.8 37.0 %feed.3 = (bf16[1024,1536]{1,0:T(8,128)(2,1)}, bf16[1024,1024]{1,0:T(8,128)(2,1)}, bf16[1024,2048]{1,0:T(8,128)(2,1)}, f32[512,1536]{1,0:T(8,128)}, bf16[512,153...) custom-call(s32[1]{0:T(128)} %bitcast.refs_0_, ...), custom_call_target="tpu_custom_call", output_to_operand_aliasing={{0}: (12, {}), {1}: (13, {}), {2}: (14, {})} | custom-call | flops 295999995904 | tf_op jit(solution)/shard_map/feed/pallas_call | solution.py:61
  305.9 8.3 %hidden_back.2 = (bf16[1024,1536]{1,0:T(8,128)(2,1)}, bf16[1024,384]{1,0:T(8,128)(2,1)}, f32[512,1536]{1,0:T(8,128)}, f32[2,1,1536]{2,1,0:T(1,128)}, bf16[8,1,12...) custom-call(bf16[512,1536]{1,0:T(8,128)(2,1)} %get-tuple-element.146, ...), custom_call_target="tpu_custom_call", output_to_operand_aliasing={{6}: (8, {})} | custom-call | flops 64000000000 | tf_op jit(solution)/shard_map/hidden_back/pallas_call | solution.py:61
  317.7 15.8 %turned_products.2 = (bf16[1536,3072]{1,0:T(8,128)(2,1)}, f32[8,128]{1,0:T(8,128)}) custom-call(bf16[1024,1536]{1,0:T(8,128)(2,1)} %get-tuple-element.159.refs_0_, bf16[1024,2048]{1,0:T(8,128)(2,1)} %get-tuple-element.160.refs_1_, bf16[1024,1536]{1,0:T(8,128)(2,1)} %bitcast.85, bf16[1024,1024]{1,0:T(8,128)(2,1)} %get-tuple-element.161.refs_3_, ...), custom_call_target="tpu_custom_call" | custom-call | flops 103999995904 | tf_op jit(solution)/shard_map/turned_products/pallas_call | solution.py:61
  337.0 20.1 %attend_back.3 = (bf16[8,2,256,256]{3,2,1,0:T(8,128)(2,1)}, f32[8,128]{1,0:T(8,128)}) custom-call(bf16[1,2048,128]{2,1,0:T(8,128)(2,1)} %get-tuple-element.154.refs_0_, bf16[1,2048,128]{2,1,0:T(8,128)(2,1)} %get-tuple-element.155.refs_1_, bf16[1,2048,128]{2,1,0:T(8,128)(2,1)} %get-tuple-element.156.refs_2_, ...), custom_call_target="tpu_custom_call" | custom-call | flops 176000008192 | tf_op jit(solution)/shard_map/attend_back/pallas_call | solution.py:61
  357.1 8.6 %hidden_back.3 = (bf16[1024,1536]{1,0:T(8,128)(2,1)}, bf16[1024,384]{1,0:T(8,128)(2,1)}, f32[512,1536]{1,0:T(8,128)}, f32[2,1,1536]{2,1,0:T(1,128)}, bf16[8,2,12...) custom-call(bf16[512,1536]{1,0:T(8,128)(2,1)} %get-tuple-element.145, ...), custom_call_target="tpu_custom_call", output_to_operand_aliasing={{0}: (9, {}), {1}: (10, {}), {5}: (11, {})} | custom-call | flops 64000000000 | tf_op jit(solution)/shard_map/hidden_back/pallas_call | solution.py:61
  370.4 8.8 %turned_products.3 = (bf16[1536,768]{1,0:T(8,128)(2,1)}, f32[8,128]{1,0:T(8,128)}) custom-call(bf16[1024,1536]{1,0:T(8,128)(2,1)} %get-tuple-element.177.refs_0_, bf16[1024,384]{1,0:T(8,128)(2,1)} %get-tuple-element.178.refs_1_, bf16[1024,1536]{1,0:T(8,128)(2,1)} %get-tuple-element.179.refs_2_.refs_0_, bf16[1024,384]{1,0:T(8,128)(2,1)} %get-tuple-element.180.refs_3_, ...), custom_call_target="tpu_custom_call" | custom-call | flops 64000000000 | tf_op jit(solution)/shard_map/turned_products/pallas_call | solution.py:61
  386.3 20.2 %attend_back.4 = (bf16[8,2,256,256]{3,2,1,0:T(8,128)(2,1)}, bf16[1536,768]{1,0:T(8,128)(2,1)}, f32[8,128]{1,0:T(8,128)}) custom-call(bf16[1,2048,128]{2,1,0:T(8,128)(2,1)} %get-tuple-element.172.refs_0_, bf16[1,2048,128]{2,1,0:T(8,128)(2,1)} %get-tuple-element.173.refs_1_, ...), custom_call_target="tpu_custom_call", output_to_operand_aliasing={{0}: (8, {}), {1}: (9, {})} | custom-call | flops 176000008192 | tf_op jit(solution)/shard_map/attend_back/pallas_call | solution.py:61
  411.0 20.2 %attend_back.5 = (bf16[8,1,256,256]{3,2,1,0:T(8,128)(2,1)}, bf16[1536,768]{1,0:T(8,128)(2,1)}, f32[8,128]{1,0:T(8,128)}) custom-call(bf16[1,2048,128]{2,1,0:T(8,128)(2,1)} %get-tuple-element.167.refs_0_, bf16[1,2048,128]{2,1,0:T(8,128)(2,1)} %get-tuple-element.168.refs_1_, ...), custom_call_target="tpu_custom_call", output_to_operand_aliasing={{1}: (8, {})} | custom-call | flops 176000008192 | tf_op jit(solution)/shard_map/attend_back/pallas_call | solution.py:61
  444.8 12.0 %project_back.2 = (bf16[1024,1280]{1,0:T(8,128)(2,1)}, bf16[2,128,1536]{2,1,0:T(8,128)(2,1)}, bf16[2,128,1536]{2,1,0:T(8,128)(2,1)}, f32[2,1,1920]{2,1,0:T(1,128...) custom-call(s32[1]{0:T(128)S(6)} %convert_element_type.75.refs_0_, ...), custom_call_target="tpu_custom_call", output_to_operand_aliasing={{4}: (8, {})} | custom-call | flops 96000000000 | tf_op jit(solution)/shard_map/project_back/pallas_call | solution.py:61
  461.1 12.2 %project_back.3 = (bf16[1024,1280]{1,0:T(8,128)(2,1)}, bf16[2,128,1536]{2,1,0:T(8,128)(2,1)}, bf16[2,128,1536]{2,1,0:T(8,128)(2,1)}, f32[2,1,1920]{2,1,0:T(1,128...) custom-call(s32[1]{0:T(128)S(6)} %convert_element_type.75.refs_0_, ...), custom_call_target="tpu_custom_call", output_to_operand_aliasing={{0}: (9, {}), {4}: (10, {})} | custom-call | flops 96000000000 | tf_op jit(solution)/shard_map/project_back/pallas_call | solution.py:61
  481.7 8.6 %owned_product.1 = (bf16[8,208,1280]{2,1,0:T(8,128)(2,1)}, bf16[1536,768]{1,0:T(8,128)(2,1)}, f32[8,128]{1,0:T(8,128)}) custom-call(bf16[1024,1536]{1,0:T(8,128)(2,1)} %get-tuple-element.179.refs_2_.refs_0_, bf16[1024,1280]{1,0:T(8,128)(2,1)} %get-tuple-element.205.refs_1_, bf16[8,16,1280]{2,1,0:T(8,128)(2,1)} %pad.43.refs_2_, ...), custom_call_target="tpu_custom_call", output_to_operand_aliasing={{1}: (3, {})} | custom-call | flops 71999995904 | tf_op jit(solution)/shard_map/owned_product/pallas_call | solution.py:61
  501.5 24.6 %collective-permute-done.11.refs_0_ = bf16[2,128,1536]{2,1,0:T(8,128)(2,1)S(1)} collective-permute-done((bf16[2,128,1536]{2,1,0:T(8,128)(2,1)}, bf16[2,128,1536]{2,1,0:T(8,128)(2,1)S(1)}, u32[]{:S(2)}, u32[]{:S(2)}) %collective-permute-start.11) | collective-permute-done | bytes 786464 | tf_op jit(solution)/shard_map/ppermute | solution.py:1318
  538.0 12.6 %collective-permute-done.14.refs_2_.refs_5_ = bf16[2,128,1536]{2,1,0:T(8,128)(2,1)} collective-permute-done((bf16[2,128,1536]{2,1,0:T(8,128)(2,1)}, bf16[2,128,1536]{2,1,0:T(8,128)(2,1)}, u32[]{:S(2)}, u32[]{:S(2)}) %collective-permute-start.14) | collective-permute-done | bytes 786464 | tf_op jit(solution)/shard_map/ppermute | solution.py:1342
  566.3 7.2 %collective-permute-done.15.refs_5_ = bf16[2,128,1536]{2,1,0:T(8,128)(2,1)} collective-permute-done((bf16[2,128,1536]{2,1,0:T(8,128)(2,1)}, bf16[2,128,1536]{2,1,0:T(8,128)(2,1)}, u32[]{:S(2)}, u32[]{:S(2)}) %collective-permute-start.15) | collective-permute-done | bytes 786464 | tf_op jit(solution)/shard_map/ppermute | solution.py:1342
  578.3 7.5 %collective-permute-start.20 = (f32[1,664]{1,0:T(1,128)S(1)}, f32[1,664]{1,0:T(1,128)S(1)}, u32[]{:S(2)}, u32[]{:S(2)}) collective-permute-start(f32[1,664]{1,0:T(1,128)S(1)} %pad_maximum_fusion.9), channel_id=1, source_target_pairs={{0,1},{1,0},{2,3},{3,2},{4,5},{5,4},{6,7},{7,6},{8,9},{9,8},{10,11... | collective-permute-start | bytes 7976 | tf_op jit(solution)/shard_map/ppermute | solution.py:1049
  (256 shorter events, 222.6 us)
Async XLA Ops:
  7.2 50.3 %all-gather.4.cloned.1.call-start = ((), (), s32[]{:S(2)}) async-start(), calls=%async_computation.14 | async-start | bytes 5750784 | tf_op jit(solution)/shard_map/all_gather | solution.py:1109
  14.2 215.6 %all-gather.8.cloned.1.call-start = ((), (), s32[]{:S(2)}) async-start(), calls=%async_computation.16 | async-start | bytes 10616832 | tf_op jit(solution)/shard_map/all_gather | solution.py:1111
  14.2 45.7 %collective-permute-start = (bf16[192,384]{1,0:T(8,128)(2,1)}, bf16[192,384]{1,0:T(8,128)(2,1)}, u32[]{:S(2)}, u32[]{:S(2)}) collective-permute-start(bf16[192,384]{1,0:T(8,128)(2,1)} %bitcast.65), channel_id=1, source_target_pairs={{0,1},{1,0},{2,3},{3,2},{4,5},{5,4},{6,7},{7,6},{8,9},{9,8},{10,11... | collective-permute-start | bytes 442376 | tf_op jit(solution)/shard_map/ppermute | solution.py:1049
  19.7 100.4 %collective-permute-start.2 = (bf16[192,1536]{1,0:T(8,128)(2,1)}, bf16[192,1536]{1,0:T(8,128)(2,1)}, u32[]{:S(2)}, u32[]{:S(2)}) collective-permute-start(bf16[192,1536]{1,0:T(8,128)(2,1)} %get-tuple-element.323), channel_id=1, source_target_pairs={{0,2},{1,3},{2,0},{3,1},{4,6},{5,7},{6,4},{7,5},{8,10},{9,11},{10,... | collective-permute-start | bytes 1769480 | tf_op jit(solution)/shard_map/ppermute | solution.py:1049
  22.3 97.8 %collective-permute-start.3 = (bf16[192,1536]{1,0:T(8,128)(2,1)}, bf16[192,1536]{1,0:T(8,128)(2,1)}, u32[]{:S(2)}, u32[]{:S(2)}) collective-permute-start(bf16[192,1536]{1,0:T(8,128)(2,1)} %get-tuple-element.322), channel_id=1, source_target_pairs={{0,2},{1,3},{2,0},{3,1},{4,6},{5,7},{6,4},{7,5},{8,10},{9,11},{10,... | collective-permute-start | bytes 1769480 | tf_op jit(solution)/shard_map/ppermute | solution.py:1049
  77.8 24.3 %all-to-all-start = ((bf16[8,1,256,256]{3,2,1,0:T(8,128)(2,1)}), bf16[8,1,256,256]{3,2,1,0:T(8,128)(2,1)S(1)}, u32[]{:S(2)}, u32[]{:S(2)}) async-start(bf16[8,1,256,256]{3,2,1,0:T(8,128)(2,1)} %get-tuple-element.122), calls=%async_computation | async-start | bytes 2097152 | tf_op jit(solution)/shard_map/all_to_all | solution.py:1053
  89.7 30.4 %collective-permute-start.1 = (bf16[192,768]{1,0:T(8,128)(2,1)S(1)}, bf16[192,768]{1,0:T(8,128)(2,1)S(1)}, u32[]{:S(2)}, u32[]{:S(2)}) collective-permute-start(bf16[192,768]{1,0:T(8,128)(2,1)S(1)} %pad_maximum_fusion.7), channel_id=1, source_target_pairs={{0,2},{1,3},{2,0},{3,1},{4,6},{5,7},{6,4},{7,5},{8,10},{9,11},{10,... | collective-permute-start | bytes 884744 | tf_op jit(solution)/shard_map/ppermute | solution.py:1049
  102.1 30.4 %all-to-all-start.1 = ((bf16[8,1,256,256]{3,2,1,0:T(8,128)(2,1)}), bf16[8,1,256,256]{3,2,1,0:T(8,128)(2,1)S(1)}, u32[]{:S(2)}, u32[]{:S(2)}) async-start(bf16[8,1,256,256]{3,2,1,0:T(8,128)(2,1)} %get-tuple-element.126), calls=%async_computation.1 | async-start | bytes 2097152 | tf_op jit(solution)/shard_map/all_to_all | solution.py:1053
  105.7 124.1 %all-gather.6.cloned.1.call-start = ((), (), s32[]{:S(2)}) async-start(), calls=%async_computation.15 | async-start | bytes 15925248 | tf_op jit(solution)/shard_map/all_gather | solution.py:1177
  184.9 40.3 %all-to-all-start.6 = ((bf16[4,512,384]{2,1,0:T(8,128)(2,1)}), bf16[4,512,384]{2,1,0:T(8,128)(2,1)S(1)}, u32[]{:S(2)}, u32[]{:S(2)}) async-start(bf16[4,512,384]{2,1,0:T(8,128)(2,1)} %get-tuple-element.138), calls=%async_computation.6 | async-start | bytes 3145728 | tf_op jit(solution)/shard_map/all_to_all | solution.py:1053
  225.2 43.5 %all-to-all-start.5 = ((bf16[4,512,384]{2,1,0:T(8,128)(2,1)}), bf16[4,512,384]{2,1,0:T(8,128)(2,1)}, u32[]{:S(2)}, u32[]{:S(2)}) async-start(bf16[4,512,384]{2,1,0:T(8,128)(2,1)} %get-tuple-element.137), calls=%async_computation.5 | async-start | bytes 3145728 | tf_op jit(solution)/shard_map/all_to_all | solution.py:1053
  266.7 39.2 %collective-permute-start.5 = (bf16[512,1536]{1,0:T(8,128)(2,1)}, bf16[512,1536]{1,0:T(8,128)(2,1)}, u32[]{:S(2)}, u32[]{:S(2)}) collective-permute-start(bf16[512,1536]{1,0:T(8,128)(2,1)} %get-tuple-element.146.refs_0_), channel_id=1, source_target_pairs={{0,1},{1,0},{2,3},{3,2},{4,5},{5,4},{6,7},{7,6},{8,9},{9,8},{10,11... | collective-permute-start | bytes 4718600 | tf_op jit(solution)/shard_map/ppermute | solution.py:1049
  305.8 51.3 %collective-permute-start.4 = (bf16[512,1536]{1,0:T(8,128)(2,1)}, bf16[512,1536]{1,0:T(8,128)(2,1)}, u32[]{:S(2)}, u32[]{:S(2)}) collective-permute-start(bf16[512,1536]{1,0:T(8,128)(2,1)} %get-tuple-element.145.refs_0_), channel_id=1, source_target_pairs={{0,1},{1,0},{2,3},{3,2},{4,5},{5,4},{6,7},{7,6},{8,9},{9,8},{10,11... | collective-permute-start | bytes 4718600 | tf_op jit(solution)/shard_map/ppermute | solution.py:1049
  314.2 22.0 %all-to-all-start.7 = ((bf16[8,1,128,128]{3,2,1,0:T(8,128)(2,1)}), bf16[8,1,128,128]{3,2,1,0:T(8,128)(2,1)S(1)}, u32[]{:S(2)}, u32[]{:S(2)}) async-start(bf16[8,1,128,128]{3,2,1,0:T(8,128)(2,1)} %get-tuple-element.158), calls=%async_computation.7 | async-start | bytes 524288 | tf_op jit(solution)/shard_map/all_to_all | solution.py:1053
  317.7 127.1 %reduce-scatter.3.cloned.1.call-start = ((), (), s32[]{:S(2)}) async-start(), calls=%async_computation.17 | async-start | bytes 10616832 | tf_op jit(solution)/shard_map/reduce_scatter | solution.py:1230
  333.6 97.6 %collective-permute-start.7 = (bf16[512,1536]{1,0:T(8,128)(2,1)}, bf16[512,1536]{1,0:T(8,128)(2,1)}, u32[]{:S(2)}, u32[]{:S(2)}) collective-permute-start(bf16[512,1536]{1,0:T(8,128)(2,1)} %get-tuple-element.166.refs_1_), channel_id=1, source_target_pairs={{0,1},{1,0},{2,3},{3,2},{4,5},{5,4},{6,7},{7,6},{8,9},{9,8},{10,11... | collective-permute-start | bytes 4718600 | tf_op jit(solution)/shard_map/ppermute | solution.py:1049
  369.8 66.0 %collective-permute-start.6 = (bf16[512,1536]{1,0:T(8,128)(2,1)}, bf16[512,1536]{1,0:T(8,128)(2,1)}, u32[]{:S(2)}, u32[]{:S(2)}) collective-permute-start(bf16[512,1536]{1,0:T(8,128)(2,1)} %get-tuple-element.165.refs_1_), channel_id=1, source_target_pairs={{0,1},{1,0},{2,3},{3,2},{4,5},{5,4},{6,7},{7,6},{8,9},{9,8},{10,11... | collective-permute-start | bytes 4718600 | tf_op jit(solution)/shard_map/ppermute | solution.py:1049
  406.4 33.9 %all-to-all-start.9 = ((bf16[8,2,256,256]{3,2,1,0:T(8,128)(2,1)}), bf16[8,2,256,256]{3,2,1,0:T(8,128)(2,1)}, u32[]{:S(2)}, u32[]{:S(2)}) async-start(bf16[8,2,256,256]{3,2,1,0:T(8,128)(2,1)} %get-tuple-element.192), calls=%async_computation.9 | async-start | bytes 4194304 | tf_op jit(solution)/shard_map/all_to_all | solution.py:1053
  490.3 84.9 %all-to-all-start.11 = ((bf16[8,208,1280]{2,1,0:T(8,128)(2,1)}), bf16[8,208,1280]{2,1,0:T(8,128)(2,1)}, u32[]{:S(2)}, u32[]{:S(2)}) async-start(bf16[8,208,1280]{2,1,0:T(8,128)(2,1)} %get-tuple-element.224), calls=%async_computation.12 | async-start | bytes 8519680 | tf_op jit(solution)/shard_map/all_to_all | solution.py:1053
  494.8 79.3 %reduce-scatter.5.cloned.1.call-start = ((), (), s32[]{:S(2)}) async-start(), calls=%async_computation.18 | async-start | bytes 2654208 | tf_op jit(solution)/shard_map/reduce_scatter | solution.py:1230
  499.5 26.6 %collective-permute-start.11 = (bf16[2,128,1536]{2,1,0:T(8,128)(2,1)}, bf16[2,128,1536]{2,1,0:T(8,128)(2,1)S(1)}, u32[]{:S(2)}, u32[]{:S(2)}) collective-permute-start(bf16[2,128,1536]{2,1,0:T(8,128)(2,1)} %get-tuple-element.213), channel_id=1, source_target_pairs={{2,3},{1,0},{6,7},{5,4},{10,11},{9,8},{14,15},{13,12},{18,19},{17,... | collective-permute-start | bytes 2359304 | tf_op jit(solution)/shard_map/ppermute | solution.py:1318
  500.8 25.3 %collective-permute-start.12 = (bf16[2,128,1536]{2,1,0:T(8,128)(2,1)}, bf16[2,128,1536]{2,1,0:T(8,128)(2,1)S(1)}, u32[]{:S(2)}, u32[]{:S(2)}) collective-permute-start(bf16[2,128,1536]{2,1,0:T(8,128)(2,1)} %get-tuple-element.214), channel_id=1, source_target_pairs={{1,2},{2,1},{5,6},{6,5},{9,10},{10,9},{13,14},{14,13},{17,18},{18,... | collective-permute-start | bytes 2359304 | tf_op jit(solution)/shard_map/ppermute | solution.py:1318
  565.0 34.7 %collective-permute-start.19 = (bf16[2,128,1536]{2,1,0:T(8,128)(2,1)}, bf16[2,128,1536]{2,1,0:T(8,128)(2,1)S(1)}, u32[]{:S(2)}, u32[]{:S(2)}) collective-permute-start(bf16[2,128,1536]{2,1,0:T(8,128)(2,1)} %collective-permute-done.18.refs_6_), channel_id=1, source_target_pairs={{2,3},{1,0},{6,7},{5,4},{10,11},{9,8},{14,15},{13,12},{18,19},{17,... | collective-permute-start | bytes 2359304 | tf_op jit(solution)/shard_map/ppermute | solution.py:1345
  573.4 25.0 %collective-permute-start.16 = (bf16[2,128,1536]{2,1,0:T(8,128)(2,1)}, bf16[2,128,1536]{2,1,0:T(8,128)(2,1)S(1)}, u32[]{:S(2)}, u32[]{:S(2)}) collective-permute-start(bf16[2,128,1536]{2,1,0:T(8,128)(2,1)} %collective-permute-done.15.refs_5_), channel_id=1, source_target_pairs={{1,2},{2,1},{5,6},{6,5},{9,10},{10,9},{13,14},{14,13},{17,18},{18,... | collective-permute-start | bytes 2359304 | tf_op jit(solution)/shard_map/ppermute | solution.py:1345
  (52 other events, 466.4 us)
Sparse Core Ops, SparseCore 0:
  14.3 43.2 all-gather.3
  59.5 74.8 all-gather.7
  136.9 87.3 all-gather.5
  333.7 85.8 reduce-scatter.2
  498.7 61.2 reduce-scatter.4

commit v6 on v5

--- a/solution.py
+++ b/solution.py
@@ -199,8 +199,7 @@
                 both = merge_swapped(low, query, key)
                 rest = jnp.where(low, swap_halves(value), zl)
             pair = pl.program_id(0) * heads + head
-            put_pair(pay_refs, pair, both.astype(BF16))
-            put_pair(pay_refs, pair, rest.astype(BF16), LANES)
+            put_pair(pay_refs, pair, jnp.concatenate([both, rest], axis=1).astype(BF16))
 
     @pl.when(pl.program_id(0) == 0)
     def _():
@@ -394,14 +393,14 @@
         return prob.astype(BF16), score_grad.astype(BF16)
 
     tail_length = tk_ref.shape[1]
-    tail_count = tail_length // size
 
     for qi in range(count):
         at = block_at(qi)
         total = jnp.zeros((LANES, size), F32)
-        for t in range(tail_count):
-            key = tk_ref[0, pl.ds(t * size, size), :]
-            _, score_grad = pieces(key, tv_ref[0, pl.ds(t * size, size), :], at)
+        for t in range(0, tail_length, 2 * size):
+            here = pl.ds(t, min(2 * size, tail_length - t))
+            key = tk_ref[0, here, :]
+            _, score_grad = pieces(key, tv_ref[0, here, :], at)
             total = total + dot(key.T, score_grad)
         dqt_ref[:, at] = total
 
@@ -972,7 +971,7 @@
 
 def turned_products(order, pairs, us):
     height = pairs[0][0].shape[1]
-    tile = 256
+    tile = 512 if height % 512 == 0 else 256
     ins, wide = [], 0
     for left, right in pairs:
         ins.append((left, pl.BlockSpec((left.shape[0], tile), lambda i: (0, i))))

time: 637 us -> 634 us (level)
  transfers between devices with their start and end apart: 39 -> 39, of which waited for: 16 -> 17; matrix products, arithmetic and copies ran while one was open for 7% -> 7% of each run, Pallas kernels for 48% -> 48%
where the time goes in v6:
time: 634 us; the launch traced here: 625 us
  Pallas kernels  308 us (49%)
  waiting for transfers between devices  147 us (23%)
  starting transfers between devices  94.7 us (15%)
  local copies, waits for them, and re-layouts  36.4 us (6%)
  other arithmetic  24.2 us (4%)
  between operations  15.2 us (2%)
    pallas_call x27, Pallas kernels, call(): pl.pallas_call(linked(kernel, count, len(extra), len(outs), len(carry)),...  308 us
    all_to_all x12, waiting for transfers between devices, to_all(): return lax.all_to_all(array, axis, 0, 0, tiled=True)  65.9 us
    all_to_all x12, starting transfers between devices, to_all(): return lax.all_to_all(array, axis, 0, 0, tiled=True)  48.4 us
    ppermute x6, waiting for transfers between devices, shards(): lax.ppermute(moving[g], 'head', hops[t - 1])  29 us
    ppermute x10, starting transfers between devices, exchanged(): return lax.ppermute(array, axis, [(i, i ^ flip) for i in range(count)])  22.2 us
    all_gather x1, waiting for transfers between devices, shards(): first = lax.all_gather(first_shard, 'seq', axis=0, tiled=True)  19.8 us
    ppermute x3, waiting for transfers between devices, shards(): lax.ppermute(passed[g][-1], 'head', hops[len(passed[g]) - 1])  19.3 us
    unnamed x80, local copies, waits for them, and re-layouts  15.4 us
  transfers between devices with their start and end apart: 39, of which 17 were waited for; matrix products, arithmetic and copies ran while one was open for 7% of the time, Pallas kernels for 48%

profile of v6, /device:TPU:0, one launch (start us, length us, event | category | flops | bytes accessed | tf_op | source)
XLA Modules:
  0.0 625.0 jit_solution(16626495899886326828)
XLA Ops:
  37.8 19.8 %all-gather.4.cloned.1.call-done.refs_1_.refs_4_ = bf16[1536,1664]{1,0:T(8,128)(2,1)} async-done(((bf16[192,1664]{1,0:T(8,128)(2,1)}), bf16[1536,1664]{1,0:T(8,128)(2,1)}) %all-gather.4.cloned.1.call-update) | async-done | bytes 5111824 | tf_op jit(solution)/shard_map/all_gather | solution.py:1108
  59.9 17.4 %project.1 = (bf16[1024,1536]{1,0:T(8,128)(2,1)}, f32[1024,768]{1,0:T(8,128)}, f32[1024,384]{1,0:T(8,128)}, bf16[8,1,256,256]{3,2,1,0:T(8,128)(2,1)}, bf16[8,1,2...) custom-call(bf16[1024,1536]{1,0:T(8,128)(2,1)} %bitcast.87, ...), custom_call_target="tpu_custom_call" | custom-call | flops 103999995904 | tf_op jit(solution)/shard_map/project/pallas_call | solution.py:61
  92.2 9.0 %all-to-all-done.refs_0_.refs_7_ = bf16[8,1,256,256]{3,2,1,0:T(8,128)(2,1)S(1)} async-done(((bf16[8,1,256,256]{3,2,1,0:T(8,128)(2,1)}), bf16[8,1,256,256]{3,2,1,0:T(8,128)(2,1)S(1)}, u32[]{:S(2)}, u32[]{:S(2)}) %all-to-all-start) | async-done | bytes 1048608 | tf_op jit(solution)/shard_map/all_to_all | solution.py:1052
  105.0 14.2 %attend.3 = (bf16[8,2,128,128]{3,2,1,0:T(8,128)(2,1)}, f32[1,2048,128]{2,1,0:T(8,128)}, bf16[1,2048,128]{2,1,0:T(8,128)(2,1)}, bf16[1,2048,128]{2,1,0:T(8,128)(2...) custom-call(bf16[8,1,256,256]{3,2,1,0:T(8,128)(2,1)} %copy-done.10, ...), custom_call_target="tpu_custom_call" | custom-call | flops 112000000000 | tf_op jit(solution)/shard_map/attend/pallas_call | solution.py:61
  122.7 8.9 %all-to-all-done.1.refs_0_.refs_7_ = bf16[8,1,256,256]{3,2,1,0:T(8,128)(2,1)S(1)} async-done(((bf16[8,1,256,256]{3,2,1,0:T(8,128)(2,1)}), bf16[8,1,256,256]{3,2,1,0:T(8,128)(2,1)S(1)}, u32[]{:S(2)}, u32[]{:S(2)}) %all-to-all-start.1) | async-done | bytes 1048608 | tf_op jit(solution)/shard_map/all_to_all | solution.py:1052
  135.4 14.1 %attend.4 = (bf16[8,2,128,128]{3,2,1,0:T(8,128)(2,1)}, f32[1,2048,128]{2,1,0:T(8,128)}, bf16[1,2048,128]{2,1,0:T(8,128)(2,1)}, bf16[1,2048,128]{2,1,0:T(8,128)(2...) custom-call(bf16[8,1,256,256]{3,2,1,0:T(8,128)(2,1)} %copy-done.9, ...), custom_call_target="tpu_custom_call", output_to_operand_aliasing={{0}: (3, {})} | custom-call | flops 112000000000 | tf_op jit(solution)/shard_map/attend/pallas_call | solution.py:61
  157.0 13.9 %attend.5 = (bf16[8,1,128,128]{3,2,1,0:T(8,128)(2,1)}, f32[1,2048,128]{2,1,0:T(8,128)}, bf16[1,2048,128]{2,1,0:T(8,128)(2,1)}, bf16[1,2048,128]{2,1,0:T(8,128)(2...) custom-call(bf16[8,1,256,256]{3,2,1,0:T(8,128)(2,1)} %copy-done.11, ...), custom_call_target="tpu_custom_call" | custom-call | flops 112000000000 | tf_op jit(solution)/shard_map/attend/pallas_call | solution.py:61
  191.2 32.6 %all-to-all-done.6.refs_11_ = bf16[4,512,384]{2,1,0:T(8,128)(2,1)S(1)} async-done(((bf16[4,512,384]{2,1,0:T(8,128)(2,1)}), bf16[4,512,384]{2,1,0:T(8,128)(2,1)S(1)}, u32[]{:S(2)}, u32[]{:S(2)}) %all-to-all-start.6) | async-done | bytes 1572896 | tf_op jit(solution)/shard_map/all_to_all | solution.py:1052
  228.4 36.9 %feed.2 = (bf16[1024,1536]{1,0:T(8,128)(2,1)}, bf16[1024,1024]{1,0:T(8,128)(2,1)}, bf16[1024,2048]{1,0:T(8,128)(2,1)}, f32[512,1536]{1,0:T(8,128)}, bf16[512,153...) custom-call(s32[1]{0:T(128)} %bitcast.refs_0_, bf16[1024,1536]{1,0:T(8,128)(2,1)} %bitcast.88, ...), custom_call_target="tpu_custom_call" | custom-call | flops 295999995904 | tf_op jit(solution)/shard_map/feed/pallas_call | solution.py:61
  267.4 37.0 %feed.3 = (bf16[1024,1536]{1,0:T(8,128)(2,1)}, bf16[1024,1024]{1,0:T(8,128)(2,1)}, bf16[1024,2048]{1,0:T(8,128)(2,1)}, f32[512,1536]{1,0:T(8,128)}, bf16[512,153...) custom-call(s32[1]{0:T(128)} %bitcast.refs_0_, ...), custom_call_target="tpu_custom_call", output_to_operand_aliasing={{0}: (12, {}), {1}: (13, {}), {2}: (14, {})} | custom-call | flops 295999995904 | tf_op jit(solution)/shard_map/feed/pallas_call | solution.py:61
  304.5 8.3 %hidden_back.2 = (bf16[1024,1536]{1,0:T(8,128)(2,1)}, bf16[1024,384]{1,0:T(8,128)(2,1)}, f32[512,1536]{1,0:T(8,128)}, f32[2,1,1536]{2,1,0:T(1,128)}, bf16[8,1,12...) custom-call(bf16[512,1536]{1,0:T(8,128)(2,1)} %get-tuple-element.146, ...), custom_call_target="tpu_custom_call", output_to_operand_aliasing={{6}: (8, {})} | custom-call | flops 64000000000 | tf_op jit(solution)/shard_map/hidden_back/pallas_call | solution.py:61
  316.3 16.0 %turned_products.2 = (bf16[1536,3072]{1,0:T(8,128)(2,1)}, f32[8,128]{1,0:T(8,128)}) custom-call(bf16[1024,1536]{1,0:T(8,128)(2,1)} %get-tuple-element.159.refs_0_, bf16[1024,2048]{1,0:T(8,128)(2,1)} %get-tuple-element.160.refs_1_, bf16[1024,1536]{1,0:T(8,128)(2,1)} %bitcast.85, bf16[1024,1024]{1,0:T(8,128)(2,1)} %get-tuple-element.161.refs_3_, ...), custom_call_target="tpu_custom_call" | custom-call | flops 103999995904 | tf_op jit(solution)/shard_map/turned_products/pallas_call | solution.py:61
  335.7 19.8 %attend_back.3 = (bf16[8,2,256,256]{3,2,1,0:T(8,128)(2,1)}, f32[8,128]{1,0:T(8,128)}) custom-call(bf16[1,2048,128]{2,1,0:T(8,128)(2,1)} %get-tuple-element.154.refs_0_, bf16[1,2048,128]{2,1,0:T(8,128)(2,1)} %get-tuple-element.155.refs_1_, bf16[1,2048,128]{2,1,0:T(8,128)(2,1)} %get-tuple-element.156.refs_2_, ...), custom_call_target="tpu_custom_call" | custom-call | flops 176000008192 | tf_op jit(solution)/shard_map/attend_back/pallas_call | solution.py:61
  355.5 8.6 %hidden_back.3 = (bf16[1024,1536]{1,0:T(8,128)(2,1)}, bf16[1024,384]{1,0:T(8,128)(2,1)}, f32[512,1536]{1,0:T(8,128)}, f32[2,1,1536]{2,1,0:T(1,128)}, bf16[8,2,12...) custom-call(bf16[512,1536]{1,0:T(8,128)(2,1)} %get-tuple-element.145, ...), custom_call_target="tpu_custom_call", output_to_operand_aliasing={{0}: (9, {}), {1}: (10, {}), {5}: (11, {})} | custom-call | flops 64000000000 | tf_op jit(solution)/shard_map/hidden_back/pallas_call | solution.py:61
  368.8 7.7 %turned_products.3 = (bf16[1536,768]{1,0:T(8,128)(2,1)}, f32[8,128]{1,0:T(8,128)}) custom-call(bf16[1024,1536]{1,0:T(8,128)(2,1)} %get-tuple-element.177.refs_0_, bf16[1024,384]{1,0:T(8,128)(2,1)} %get-tuple-element.178.refs_1_, bf16[1024,1536]{1,0:T(8,128)(2,1)} %get-tuple-element.179.refs_2_.refs_0_, bf16[1024,384]{1,0:T(8,128)(2,1)} %get-tuple-element.180.refs_3_, ...), custom_call_target="tpu_custom_call" | custom-call | flops 64000000000 | tf_op jit(solution)/shard_map/turned_products/pallas_call | solution.py:61
  384.7 19.9 %attend_back.4 = (bf16[8,2,256,256]{3,2,1,0:T(8,128)(2,1)}, bf16[1536,768]{1,0:T(8,128)(2,1)}, f32[8,128]{1,0:T(8,128)}) custom-call(bf16[1,2048,128]{2,1,0:T(8,128)(2,1)} %get-tuple-element.172.refs_0_, bf16[1,2048,128]{2,1,0:T(8,128)(2,1)} %get-tuple-element.173.refs_1_, ...), custom_call_target="tpu_custom_call", output_to_operand_aliasing={{0}: (8, {}), {1}: (9, {})} | custom-call | flops 176000008192 | tf_op jit(solution)/shard_map/attend_back/pallas_call | solution.py:61
  409.1 19.9 %attend_back.5 = (bf16[8,1,256,256]{3,2,1,0:T(8,128)(2,1)}, bf16[1536,768]{1,0:T(8,128)(2,1)}, f32[8,128]{1,0:T(8,128)}) custom-call(bf16[1,2048,128]{2,1,0:T(8,128)(2,1)} %get-tuple-element.167.refs_0_, bf16[1,2048,128]{2,1,0:T(8,128)(2,1)} %get-tuple-element.168.refs_1_, ...), custom_call_target="tpu_custom_call", output_to_operand_aliasing={{1}: (8, {})} | custom-call | flops 176000008192 | tf_op jit(solution)/shard_map/attend_back/pallas_call | solution.py:61
  442.5 12.0 %project_back.2 = (bf16[1024,1280]{1,0:T(8,128)(2,1)}, bf16[2,128,1536]{2,1,0:T(8,128)(2,1)}, bf16[2,128,1536]{2,1,0:T(8,128)(2,1)}, f32[2,1,1920]{2,1,0:T(1,128...) custom-call(s32[1]{0:T(128)S(6)} %convert_element_type.75.refs_0_, ...), custom_call_target="tpu_custom_call", output_to_operand_aliasing={{4}: (8, {})} | custom-call | flops 96000000000 | tf_op jit(solution)/shard_map/project_back/pallas_call | solution.py:61
  458.8 12.2 %project_back.3 = (bf16[1024,1280]{1,0:T(8,128)(2,1)}, bf16[2,128,1536]{2,1,0:T(8,128)(2,1)}, bf16[2,128,1536]{2,1,0:T(8,128)(2,1)}, f32[2,1,1920]{2,1,0:T(1,128...) custom-call(s32[1]{0:T(128)S(6)} %convert_element_type.75.refs_0_, ...), custom_call_target="tpu_custom_call", output_to_operand_aliasing={{0}: (9, {}), {4}: (10, {})} | custom-call | flops 96000000000 | tf_op jit(solution)/shard_map/project_back/pallas_call | solution.py:61
  479.7 8.6 %owned_product.1 = (bf16[8,208,1280]{2,1,0:T(8,128)(2,1)}, bf16[1536,768]{1,0:T(8,128)(2,1)}, f32[8,128]{1,0:T(8,128)}) custom-call(bf16[1024,1536]{1,0:T(8,128)(2,1)} %get-tuple-element.179.refs_2_.refs_0_, bf16[1024,1280]{1,0:T(8,128)(2,1)} %get-tuple-element.205.refs_1_, bf16[8,16,1280]{2,1,0:T(8,128)(2,1)} %pad.43.refs_2_, ...), custom_call_target="tpu_custom_call", output_to_operand_aliasing={{1}: (3, {})} | custom-call | flops 71999995904 | tf_op jit(solution)/shard_map/owned_product/pallas_call | solution.py:61
  499.5 24.0 %collective-permute-done.11.refs_0_ = bf16[2,128,1536]{2,1,0:T(8,128)(2,1)S(1)} collective-permute-done((bf16[2,128,1536]{2,1,0:T(8,128)(2,1)}, bf16[2,128,1536]{2,1,0:T(8,128)(2,1)S(1)}, u32[]{:S(2)}, u32[]{:S(2)}) %collective-permute-start.11) | collective-permute-done | bytes 786464 | tf_op jit(solution)/shard_map/ppermute | solution.py:1317
  535.5 12.5 %collective-permute-done.14.refs_2_.refs_5_ = bf16[2,128,1536]{2,1,0:T(8,128)(2,1)} collective-permute-done((bf16[2,128,1536]{2,1,0:T(8,128)(2,1)}, bf16[2,128,1536]{2,1,0:T(8,128)(2,1)}, u32[]{:S(2)}, u32[]{:S(2)}) %collective-permute-start.14) | collective-permute-done | bytes 786464 | tf_op jit(solution)/shard_map/ppermute | solution.py:1341
  575.4 8.1 %collective-permute-start.20 = (f32[1,664]{1,0:T(1,128)S(1)}, f32[1,664]{1,0:T(1,128)S(1)}, u32[]{:S(2)}, u32[]{:S(2)}) collective-permute-start(f32[1,664]{1,0:T(1,128)S(1)} %pad_maximum_fusion.9), channel_id=1, source_target_pairs={{0,1},{1,0},{2,3},{3,2},{4,5},{5,4},{6,7},{7,6},{8,9},{9,8},{10,11... | collective-permute-start | bytes 7976 | tf_op jit(solution)/shard_map/ppermute | solution.py:1048
  611.1 6.9 %input_back.3 = (f32[1024,1536]{1,0:T(8,128)}, f32[8,128]{1,0:T(8,128)}) custom-call(s32[1]{0:T(128)} %bitcast.refs_0_, bf16[1024,1536]{1,0:T(8,128)(2,1)} %bitcast.93, f32[512,1536]{1,0:T(8,128)} %get-tuple-element.190.refs_2_, f32[1,1536]{1,0:T(1,128)} %reshape.521.refs_3_, ...), custom_call_target="tpu_custom_call", output_to_operand_aliasing={{0}: (8, {})} | custom-call | flops 64000000000 | tf_op jit(solution)/shard_map/input_back/pallas_call | solution.py:61
  (256 shorter events, 221.7 us)
Async XLA Ops:
  7.2 50.3 %all-gather.4.cloned.1.call-start = ((), (), s32[]{:S(2)}) async-start(), calls=%async_computation.14 | async-start | bytes 5750784 | tf_op jit(solution)/shard_map/all_gather | solution.py:1108
  14.2 214.2 %all-gather.8.cloned.1.call-start = ((), (), s32[]{:S(2)}) async-start(), calls=%async_computation.16 | async-start | bytes 10616832 | tf_op jit(solution)/shard_map/all_gather | solution.py:1110
  14.2 45.7 %collective-permute-start = (bf16[192,384]{1,0:T(8,128)(2,1)}, bf16[192,384]{1,0:T(8,128)(2,1)}, u32[]{:S(2)}, u32[]{:S(2)}) collective-permute-start(bf16[192,384]{1,0:T(8,128)(2,1)} %bitcast.65), channel_id=1, source_target_pairs={{0,1},{1,0},{2,3},{3,2},{4,5},{5,4},{6,7},{7,6},{8,9},{9,8},{10,11... | collective-permute-start | bytes 442376 | tf_op jit(solution)/shard_map/ppermute | solution.py:1048
  19.7 99.5 %collective-permute-start.2 = (bf16[192,1536]{1,0:T(8,128)(2,1)}, bf16[192,1536]{1,0:T(8,128)(2,1)}, u32[]{:S(2)}, u32[]{:S(2)}) collective-permute-start(bf16[192,1536]{1,0:T(8,128)(2,1)} %get-tuple-element.323), channel_id=1, source_target_pairs={{0,2},{1,3},{2,0},{3,1},{4,6},{5,7},{6,4},{7,5},{8,10},{9,11},{10,... | collective-permute-start | bytes 1769480 | tf_op jit(solution)/shard_map/ppermute | solution.py:1048
  22.3 96.9 %collective-permute-start.3 = (bf16[192,1536]{1,0:T(8,128)(2,1)}, bf16[192,1536]{1,0:T(8,128)(2,1)}, u32[]{:S(2)}, u32[]{:S(2)}) collective-permute-start(bf16[192,1536]{1,0:T(8,128)(2,1)} %get-tuple-element.322), channel_id=1, source_target_pairs={{0,2},{1,3},{2,0},{3,1},{4,6},{5,7},{6,4},{7,5},{8,10},{9,11},{10,... | collective-permute-start | bytes 1769480 | tf_op jit(solution)/shard_map/ppermute | solution.py:1048
  77.3 23.9 %all-to-all-start = ((bf16[8,1,256,256]{3,2,1,0:T(8,128)(2,1)}), bf16[8,1,256,256]{3,2,1,0:T(8,128)(2,1)S(1)}, u32[]{:S(2)}, u32[]{:S(2)}) async-start(bf16[8,1,256,256]{3,2,1,0:T(8,128)(2,1)} %get-tuple-element.122), calls=%async_computation | async-start | bytes 2097152 | tf_op jit(solution)/shard_map/all_to_all | solution.py:1052
  89.2 30.0 %collective-permute-start.1 = (bf16[192,768]{1,0:T(8,128)(2,1)S(1)}, bf16[192,768]{1,0:T(8,128)(2,1)S(1)}, u32[]{:S(2)}, u32[]{:S(2)}) collective-permute-start(bf16[192,768]{1,0:T(8,128)(2,1)S(1)} %pad_maximum_fusion.7), channel_id=1, source_target_pairs={{0,2},{1,3},{2,0},{3,1},{4,6},{5,7},{6,4},{7,5},{8,10},{9,11},{10,... | collective-permute-start | bytes 884744 | tf_op jit(solution)/shard_map/ppermute | solution.py:1048
  101.2 30.4 %all-to-all-start.1 = ((bf16[8,1,256,256]{3,2,1,0:T(8,128)(2,1)}), bf16[8,1,256,256]{3,2,1,0:T(8,128)(2,1)S(1)}, u32[]{:S(2)}, u32[]{:S(2)}) async-start(bf16[8,1,256,256]{3,2,1,0:T(8,128)(2,1)} %get-tuple-element.126), calls=%async_computation.1 | async-start | bytes 2097152 | tf_op jit(solution)/shard_map/all_to_all | solution.py:1052
  104.7 123.7 %all-gather.6.cloned.1.call-start = ((), (), s32[]{:S(2)}) async-start(), calls=%async_computation.15 | async-start | bytes 15925248 | tf_op jit(solution)/shard_map/all_gather | solution.py:1176
  182.9 40.9 %all-to-all-start.6 = ((bf16[4,512,384]{2,1,0:T(8,128)(2,1)}), bf16[4,512,384]{2,1,0:T(8,128)(2,1)S(1)}, u32[]{:S(2)}, u32[]{:S(2)}) async-start(bf16[4,512,384]{2,1,0:T(8,128)(2,1)} %get-tuple-element.138), calls=%async_computation.6 | async-start | bytes 3145728 | tf_op jit(solution)/shard_map/all_to_all | solution.py:1052
  223.8 43.5 %all-to-all-start.5 = ((bf16[4,512,384]{2,1,0:T(8,128)(2,1)}), bf16[4,512,384]{2,1,0:T(8,128)(2,1)}, u32[]{:S(2)}, u32[]{:S(2)}) async-start(bf16[4,512,384]{2,1,0:T(8,128)(2,1)} %get-tuple-element.137), calls=%async_computation.5 | async-start | bytes 3145728 | tf_op jit(solution)/shard_map/all_to_all | solution.py:1052
  265.3 39.2 %collective-permute-start.5 = (bf16[512,1536]{1,0:T(8,128)(2,1)}, bf16[512,1536]{1,0:T(8,128)(2,1)}, u32[]{:S(2)}, u32[]{:S(2)}) collective-permute-start(bf16[512,1536]{1,0:T(8,128)(2,1)} %get-tuple-element.146.refs_0_), channel_id=1, source_target_pairs={{0,1},{1,0},{2,3},{3,2},{4,5},{5,4},{6,7},{7,6},{8,9},{9,8},{10,11... | collective-permute-start | bytes 4718600 | tf_op jit(solution)/shard_map/ppermute | solution.py:1048
  304.4 51.1 %collective-permute-start.4 = (bf16[512,1536]{1,0:T(8,128)(2,1)}, bf16[512,1536]{1,0:T(8,128)(2,1)}, u32[]{:S(2)}, u32[]{:S(2)}) collective-permute-start(bf16[512,1536]{1,0:T(8,128)(2,1)} %get-tuple-element.145.refs_0_), channel_id=1, source_target_pairs={{0,1},{1,0},{2,3},{3,2},{4,5},{5,4},{6,7},{7,6},{8,9},{9,8},{10,11... | collective-permute-start | bytes 4718600 | tf_op jit(solution)/shard_map/ppermute | solution.py:1048
  312.8 22.2 %all-to-all-start.7 = ((bf16[8,1,128,128]{3,2,1,0:T(8,128)(2,1)}), bf16[8,1,128,128]{3,2,1,0:T(8,128)(2,1)S(1)}, u32[]{:S(2)}, u32[]{:S(2)}) async-start(bf16[8,1,128,128]{3,2,1,0:T(8,128)(2,1)} %get-tuple-element.158), calls=%async_computation.7 | async-start | bytes 524288 | tf_op jit(solution)/shard_map/all_to_all | solution.py:1052
  316.3 126.2 %reduce-scatter.3.cloned.1.call-start = ((), (), s32[]{:S(2)}) async-start(), calls=%async_computation.17 | async-start | bytes 10616832 | tf_op jit(solution)/shard_map/reduce_scatter | solution.py:1229
  332.3 96.7 %collective-permute-start.7 = (bf16[512,1536]{1,0:T(8,128)(2,1)}, bf16[512,1536]{1,0:T(8,128)(2,1)}, u32[]{:S(2)}, u32[]{:S(2)}) collective-permute-start(bf16[512,1536]{1,0:T(8,128)(2,1)} %get-tuple-element.166.refs_1_), channel_id=1, source_target_pairs={{0,1},{1,0},{2,3},{3,2},{4,5},{5,4},{6,7},{7,6},{8,9},{9,8},{10,11... | collective-permute-start | bytes 4718600 | tf_op jit(solution)/shard_map/ppermute | solution.py:1048
  368.2 65.4 %collective-permute-start.6 = (bf16[512,1536]{1,0:T(8,128)(2,1)}, bf16[512,1536]{1,0:T(8,128)(2,1)}, u32[]{:S(2)}, u32[]{:S(2)}) collective-permute-start(bf16[512,1536]{1,0:T(8,128)(2,1)} %get-tuple-element.165.refs_1_), channel_id=1, source_target_pairs={{0,1},{1,0},{2,3},{3,2},{4,5},{5,4},{6,7},{7,6},{8,9},{9,8},{10,11... | collective-permute-start | bytes 4718600 | tf_op jit(solution)/shard_map/ppermute | solution.py:1048
  404.6 33.7 %all-to-all-start.9 = ((bf16[8,2,256,256]{3,2,1,0:T(8,128)(2,1)}), bf16[8,2,256,256]{3,2,1,0:T(8,128)(2,1)}, u32[]{:S(2)}, u32[]{:S(2)}) async-start(bf16[8,2,256,256]{3,2,1,0:T(8,128)(2,1)} %get-tuple-element.192), calls=%async_computation.9 | async-start | bytes 4194304 | tf_op jit(solution)/shard_map/all_to_all | solution.py:1052
  488.3 84.0 %all-to-all-start.11 = ((bf16[8,208,1280]{2,1,0:T(8,128)(2,1)}), bf16[8,208,1280]{2,1,0:T(8,128)(2,1)}, u32[]{:S(2)}, u32[]{:S(2)}) async-start(bf16[8,208,1280]{2,1,0:T(8,128)(2,1)} %get-tuple-element.224), calls=%async_computation.12 | async-start | bytes 8519680 | tf_op jit(solution)/shard_map/all_to_all | solution.py:1052
  492.9 78.4 %reduce-scatter.5.cloned.1.call-start = ((), (), s32[]{:S(2)}) async-start(), calls=%async_computation.18 | async-start | bytes 2654208 | tf_op jit(solution)/shard_map/reduce_scatter | solution.py:1229
  497.5 26.0 %collective-permute-start.11 = (bf16[2,128,1536]{2,1,0:T(8,128)(2,1)}, bf16[2,128,1536]{2,1,0:T(8,128)(2,1)S(1)}, u32[]{:S(2)}, u32[]{:S(2)}) collective-permute-start(bf16[2,128,1536]{2,1,0:T(8,128)(2,1)} %get-tuple-element.213), channel_id=1, source_target_pairs={{2,3},{1,0},{6,7},{5,4},{10,11},{9,8},{14,15},{13,12},{18,19},{17,... | collective-permute-start | bytes 2359304 | tf_op jit(solution)/shard_map/ppermute | solution.py:1317
  498.8 24.7 %collective-permute-start.12 = (bf16[2,128,1536]{2,1,0:T(8,128)(2,1)}, bf16[2,128,1536]{2,1,0:T(8,128)(2,1)S(1)}, u32[]{:S(2)}, u32[]{:S(2)}) collective-permute-start(bf16[2,128,1536]{2,1,0:T(8,128)(2,1)} %get-tuple-element.214), channel_id=1, source_target_pairs={{1,2},{2,1},{5,6},{6,5},{9,10},{10,9},{13,14},{14,13},{17,18},{18,... | collective-permute-start | bytes 2359304 | tf_op jit(solution)/shard_map/ppermute | solution.py:1317
  562.4 34.2 %collective-permute-start.19 = (bf16[2,128,1536]{2,1,0:T(8,128)(2,1)}, bf16[2,128,1536]{2,1,0:T(8,128)(2,1)S(1)}, u32[]{:S(2)}, u32[]{:S(2)}) collective-permute-start(bf16[2,128,1536]{2,1,0:T(8,128)(2,1)} %collective-permute-done.18.refs_6_), channel_id=1, source_target_pairs={{2,3},{1,0},{6,7},{5,4},{10,11},{9,8},{14,15},{13,12},{18,19},{17,... | collective-permute-start | bytes 2359304 | tf_op jit(solution)/shard_map/ppermute | solution.py:1344
  570.5 24.8 %collective-permute-start.16 = (bf16[2,128,1536]{2,1,0:T(8,128)(2,1)}, bf16[2,128,1536]{2,1,0:T(8,128)(2,1)S(1)}, u32[]{:S(2)}, u32[]{:S(2)}) collective-permute-start(bf16[2,128,1536]{2,1,0:T(8,128)(2,1)} %collective-permute-done.15.refs_5_), channel_id=1, source_target_pairs={{1,2},{2,1},{5,6},{6,5},{9,10},{10,9},{13,14},{14,13},{17,18},{18,... | collective-permute-start | bytes 2359304 | tf_op jit(solution)/shard_map/ppermute | solution.py:1344
  (52 other events, 463.5 us)
Sparse Core Ops, SparseCore 0:
  14.3 43.2 all-gather.3
  59.5 74.4 all-gather.7
  136.5 86.4 all-gather.5
  332.5 86.4 reduce-scatter.2
  496.8 60.9 reduce-scatter.4
